TPU v7x, 32 devices: a whole 2x2x4 slice. The times are simulated.
32 devices in a mesh: section: 2 (over core), shard: 4 (over z), replica: 4 (over y, x).
Axes of the slice: x: 2, y: 2, z: 4, core: 2. Of those that a mesh axis runs over, the one named last changes fastest.
Arguments:
- patches: bfloat16 [32, 197, 384], P(('shard', 'replica')), may hold values from -6 to 6
- live_slots: int32 [32], P(('shard', 'replica')), may hold values from 0 to 1, as said below
- cotangent: bfloat16 [32, 197, 384], P(('shard', 'replica')), may hold values from -6 to 6
- w_qkv: bfloat16 [2, 384, 1152], P('section', 'shard'), may hold values from -0.3125 to 0.3125
- w_out: bfloat16 [2, 384, 384], P('section', 'shard'), may hold values from -0.625 to 0.625
- w_up: bfloat16 [2, 384, 1536], P('section', 'shard'), may hold values from -0.3125 to 0.3125
- w_down: bfloat16 [2, 1536, 384], P('section', 'shard'), may hold values from -0.15625 to 0.15625
- bias_q: float32 [2, 384], P('section', 'shard'), may hold values from -1.5 to 1.5
- bias_v: float32 [2, 384], P('section', 'shard'), may hold values from -1.5 to 1.5
- bias_out: float32 [2, 384], P('section', 'shard'), may hold values from -1.5 to 1.5
- bias_up: float32 [2, 1536], P('section', 'shard'), may hold values from -1.5 to 1.5
- bias_down: float32 [2, 384], P('section', 'shard'), may hold values from -1.5 to 1.5
- gain_one: float32 [2, 384], P('section', 'shard'), may hold values from 0.5 to 1.5
- offset_one: float32 [2, 384], P('section', 'shard'), may hold values from -1.5 to 1.5
- gain_two: float32 [2, 384], P('section', 'shard'), may hold values from 0.5 to 1.5
- offset_two: float32 [2, 384], P('section', 'shard'), may hold values from -1.5 to 1.5
Outputs:
- layer_outputs: bfloat16 [2, 32, 197, 384], P('section', ('shard', 'replica'))
- input_grads: float32 [2, 32, 197, 384], P('section', ('shard', 'replica'))
- grad_w_qkv: float32 [2, 384, 1152], P('section', 'shard')
- grad_w_out: float32 [2, 384, 384], P('section', 'shard')
- grad_w_up: float32 [2, 384, 1536], P('section', 'shard')
- grad_w_down: float32 [2, 1536, 384], P('section', 'shard')
- grad_bias_q: float32 [2, 384], P('section', 'shard')
- grad_bias_v: float32 [2, 384], P('section', 'shard')
- grad_bias_out: float32 [2, 384], P('section', 'shard')
- grad_bias_up: float32 [2, 1536], P('section', 'shard')
- grad_bias_down: float32 [2, 384], P('section', 'shard')
- grad_gain_one: float32 [2, 384], P('section', 'shard')
- grad_offset_one: float32 [2, 384], P('section', 'shard')
- grad_gain_two: float32 [2, 384], P('section', 'shard')
- grad_offset_two: float32 [2, 384], P('section', 'shard')
Inputs may be any that keep to these rules, and one draw needn't show every extreme that they name: `live_slots`: exactly 25 of the 32 slots hold an image.
All inputs are finite; a program needn't handle non-finite values.
Results may differ from a plain program's by a relative error of at most 0.04.
Values may be sent and summed in bfloat16 or wider, within the bound.
No kernel may reach another device: no remote copies, remote signals or barrier semaphores. Data moves between devices by JAX's collectives and lax.ppermute only.
A program may use at most 128 MiB of HBM per device.

v0:
```python
import jax
import jax.numpy as jnp
from jax import lax
from jax.sharding import PartitionSpec as P

HEAD_DIM = 64
MICRO = 2


epsilon = 1e-06
root_half = 0.7071067811865476
inverse_root_two_pi = 0.3989422804014327


def shifted(value, axis, steps):
    count = lax.axis_size(axis)
    initial, last = (max(0, -steps), min(count, count - steps))
    return lax.ppermute(value, axis, [(source, source + steps) for source in range(initial, last)])


def normalize(values):
    row_mean = jnp.mean(values, -1, keepdims=True)
    centred = values - row_mean
    inverse = lax.rsqrt(jnp.mean(centred * centred, -1, keepdims=True) + epsilon)
    return (centred * inverse, inverse)


def norm_backward(grad_normed, unit_rows, inverse):
    centre_term = jnp.mean(grad_normed, -1, keepdims=True)
    slope_term = jnp.mean(grad_normed * unit_rows, -1, keepdims=True)
    return inverse * (grad_normed - centre_term - unit_rows * slope_term)


def project(rows, matrix):
    return jnp.einsum("bsi,ij->bsj", rows, matrix, preferred_element_type=jnp.float32)


def project_back(grads, matrix):
    return jnp.einsum("bsj,ij->bsi", grads, matrix, preferred_element_type=jnp.float32)


def weight_grad(rows, grads):
    return jnp.einsum("bsi,bsj->ij", rows, grads, preferred_element_type=jnp.float32)


def row_total(values):
    return jnp.sum(values, axis=(0, 1))


def split_heads(rows):
    return rows.reshape(rows.shape[:-1] + (rows.shape[-1] // HEAD_DIM, HEAD_DIM))


def score_rows(queries, key_rows):
    scores = jnp.einsum("bqhe,bkhe->bhqk", queries, key_rows, preferred_element_type=jnp.float32)
    return scores * HEAD_DIM ** (-0.5)


def forward_layer(inputs, gathered):
    (
        w_qkv,
        w_out,
        w_up,
        w_down,
        bias_q,
        bias_v,
        bias_out,
        bias_up,
        bias_down,
        gain_one,
        offset_one,
        gain_two,
        offset_two,
    ) = gathered
    model_width = inputs.shape[-1]
    unit_one, inverse_one = normalize(inputs)
    normed = (unit_one * gain_one + offset_one).astype(jnp.bfloat16)
    qkv_out = project(normed, w_qkv)
    queries = split_heads((qkv_out[..., :model_width] + bias_q).astype(jnp.bfloat16))
    key_rows = split_heads(qkv_out[..., model_width : 2 * model_width].astype(jnp.bfloat16))
    value_rows = split_heads((qkv_out[..., 2 * model_width :] + bias_v).astype(jnp.bfloat16))
    scores = score_rows(queries, key_rows)
    row_max = jnp.max(scores, -1, keepdims=True)
    logsum = row_max + jnp.log(jnp.sum(jnp.exp(scores - row_max), -1, keepdims=True))
    attention = jnp.exp(scores - logsum).astype(jnp.bfloat16)
    attended = jnp.einsum(
        "bhqk,bkhe->bqhe", attention, value_rows, preferred_element_type=jnp.float32
    )
    attended = attended.reshape(inputs.shape).astype(jnp.bfloat16)
    hidden = inputs + project(attended, w_out) + bias_out
    unit_two, inverse_two = normalize(hidden)
    normed_two = (unit_two * gain_two + offset_two).astype(jnp.bfloat16)
    up_branch = project(normed_two, w_up) + bias_up
    activated = jax.nn.gelu(up_branch, approximate=False).astype(jnp.bfloat16)
    output = hidden + project(activated, w_down) + bias_down
    stored = (
        unit_one,
        inverse_one,
        normed,
        queries,
        key_rows,
        value_rows,
        logsum,
        attended,
        unit_two,
        inverse_two,
        normed_two,
        up_branch,
        activated,
    )
    return (output, stored)


def backward_layer(grad_output, stored, gathered):
    (
        w_qkv,
        w_out,
        w_up,
        w_down,
        bias_q,
        bias_v,
        bias_out,
        bias_up,
        bias_down,
        gain_one,
        offset_one,
        gain_two,
        offset_two,
    ) = gathered
    (
        unit_one,
        inverse_one,
        normed,
        queries,
        key_rows,
        value_rows,
        logsum,
        attended,
        unit_two,
        inverse_two,
        normed_two,
        up_branch,
        activated,
    ) = stored
    flat_shape = grad_output.shape
    down_grad = grad_output.astype(jnp.bfloat16)
    grad_w_down = weight_grad(activated, down_grad)
    grad_activated = project_back(down_grad, w_down)
    normal_cdf = 0.5 * (1.0 + lax.erf(up_branch * root_half))
    density = jnp.exp(-0.5 * up_branch * up_branch) * inverse_root_two_pi
    up_grad = (grad_activated * (normal_cdf + up_branch * density)).astype(jnp.bfloat16)
    grad_w_up = weight_grad(normed_two, up_grad)
    grad_normed_two = project_back(up_grad, w_up)
    grad_hidden = grad_output + norm_backward(grad_normed_two * gain_two, unit_two, inverse_two)
    out_grad = grad_hidden.astype(jnp.bfloat16)
    grad_w_out = weight_grad(attended, out_grad)
    attended_grad = split_heads(project_back(out_grad, w_out).astype(jnp.bfloat16))
    probability = jnp.exp(score_rows(queries, key_rows) - logsum)
    grad_probability = jnp.einsum(
        "bqhe,bkhe->bhqk", attended_grad, value_rows, preferred_element_type=jnp.float32
    )
    value_grad = jnp.einsum(
        "bhqk,bqhe->bkhe",
        probability.astype(jnp.bfloat16),
        attended_grad,
        preferred_element_type=jnp.float32,
    ).astype(jnp.bfloat16)
    centred_grad = grad_probability - jnp.sum(grad_probability * probability, -1, keepdims=True)
    score_grad = (probability * centred_grad).astype(jnp.bfloat16)
    query_grad = jnp.einsum(
        "bhqk,bkhe->bqhe", score_grad, key_rows, preferred_element_type=jnp.float32
    )
    query_grad = (query_grad * HEAD_DIM ** (-0.5)).astype(jnp.bfloat16).reshape(flat_shape)
    key_grad = jnp.einsum(
        "bhqk,bqhe->bkhe", score_grad, queries, preferred_element_type=jnp.float32
    )
    key_grad = (key_grad * HEAD_DIM ** (-0.5)).astype(jnp.bfloat16).reshape(flat_shape)
    value_grad = value_grad.reshape(flat_shape)
    qkv_grad = jnp.concatenate([query_grad, key_grad, value_grad], -1)
    grad_w_qkv = weight_grad(normed, qkv_grad)
    grad_normed = project_back(qkv_grad, w_qkv)
    grad_inputs = grad_hidden + norm_backward(grad_normed * gain_one, unit_one, inverse_one)
    partials = (
        grad_w_qkv,
        grad_w_out,
        grad_w_up,
        grad_w_down,
        row_total(query_grad.astype(jnp.float32)),
        row_total(value_grad.astype(jnp.float32)),
        row_total(grad_hidden),
        row_total(up_grad.astype(jnp.float32)),
        row_total(grad_output),
        row_total(grad_normed * unit_one),
        row_total(grad_normed),
        row_total(grad_normed_two * unit_two),
        row_total(grad_normed_two),
    )
    return (grad_inputs, partials)


def local(
    patches,
    live_slots,
    cotangent,
    w_qkv,
    w_out,
    w_up,
    w_down,
    bias_q,
    bias_v,
    bias_out,
    bias_up,
    bias_down,
    gain_one,
    offset_one,
    gain_two,
    offset_two,
):
    first_section = lax.axis_index("section") == 0
    per_batch = patches.shape[0] // MICRO
    batch_shape = (per_batch,) + patches.shape[1:]

    def fetch_weights():
        whole = (
            lax.all_gather(w_qkv, "shard", axis=1, tiled=True),
            lax.all_gather(w_out, "shard", axis=1, tiled=True),
            lax.all_gather(w_up, "shard", axis=1, tiled=True),
            lax.all_gather(w_down, "shard", axis=1, tiled=True),
            lax.all_gather(bias_q.astype(jnp.bfloat16), "shard", axis=1, tiled=True).astype(
                bias_q.dtype
            ),
            lax.all_gather(bias_v.astype(jnp.bfloat16), "shard", axis=1, tiled=True).astype(
                bias_v.dtype
            ),
            lax.all_gather(bias_out.astype(jnp.bfloat16), "shard", axis=1, tiled=True).astype(
                bias_out.dtype
            ),
            lax.all_gather(bias_up.astype(jnp.bfloat16), "shard", axis=1, tiled=True).astype(
                bias_up.dtype
            ),
            lax.all_gather(bias_down.astype(jnp.bfloat16), "shard", axis=1, tiled=True).astype(
                bias_down.dtype
            ),
            lax.all_gather(gain_one.astype(jnp.bfloat16), "shard", axis=1, tiled=True).astype(
                gain_one.dtype
            ),
            lax.all_gather(offset_one.astype(jnp.bfloat16), "shard", axis=1, tiled=True).astype(
                offset_one.dtype
            ),
            lax.all_gather(gain_two.astype(jnp.bfloat16), "shard", axis=1, tiled=True).astype(
                gain_two.dtype
            ),
            lax.all_gather(offset_two.astype(jnp.bfloat16), "shard", axis=1, tiled=True).astype(
                offset_two.dtype
            ),
        )
        return tuple((member[0] for member in whole))

    received = jnp.zeros(batch_shape, jnp.bfloat16)
    caches = []
    outputs = []
    for period in range(MICRO + 1):
        gathered = fetch_weights()
        if period < MICRO:
            own_batch = patches[period * per_batch : (period + 1) * per_batch]
        else:
            own_batch = jnp.zeros(batch_shape, jnp.bfloat16)
        layer_input = jnp.where(first_section, own_batch, received).astype(jnp.float32)
        result, stored = forward_layer(layer_input, gathered)
        rounded = result.astype(jnp.bfloat16)
        outputs.append(rounded)
        caches.append(stored)
        if period < MICRO:
            received = shifted(rounded, "section", 1)
    seed_rows = cotangent.astype(jnp.float32) * live_slots.astype(jnp.float32)[:, None, None]
    returned = jnp.zeros(batch_shape, jnp.float32)
    grad_parts = []
    owned_sum = None
    for period in range(MICRO + 1):
        gathered = fetch_weights()
        earlier_cache = caches[max(period - 1, 0)]
        later_cache = caches[min(period + 1, MICRO)]
        stored = lax.cond(first_section, lambda: earlier_cache, lambda: later_cache)
        if period < MICRO:
            later_seed = seed_rows[period * per_batch : (period + 1) * per_batch]
        else:
            later_seed = jnp.zeros(batch_shape, jnp.float32)
        grad_output = jnp.where(first_section, returned, later_seed)
        grad_inputs, partials = backward_layer(grad_output, stored, gathered)
        to_send = grad_inputs.astype(jnp.bfloat16)
        grad_parts.append(jnp.where(first_section, grad_inputs, to_send.astype(jnp.float32)))
        if period < MICRO:
            returned = shifted(to_send, "section", -1).astype(jnp.float32)
        expanded = tuple((member[None] for member in partials))
        reduced = (
            lax.psum_scatter(
                expanded[0].astype(jnp.bfloat16), "shard", scatter_dimension=1, tiled=True
            ).astype(jnp.float32),
            lax.psum_scatter(
                expanded[1].astype(jnp.bfloat16), "shard", scatter_dimension=1, tiled=True
            ).astype(jnp.float32),
            lax.psum_scatter(
                expanded[2].astype(jnp.bfloat16), "shard", scatter_dimension=1, tiled=True
            ).astype(jnp.float32),
            lax.psum_scatter(
                expanded[3].astype(jnp.bfloat16), "shard", scatter_dimension=1, tiled=True
            ).astype(jnp.float32),
            lax.psum_scatter(
                expanded[4].astype(jnp.bfloat16), "shard", scatter_dimension=1, tiled=True
            ).astype(jnp.float32),
            lax.psum_scatter(
                expanded[5].astype(jnp.bfloat16), "shard", scatter_dimension=1, tiled=True
            ).astype(jnp.float32),
            lax.psum_scatter(
                expanded[6].astype(jnp.bfloat16), "shard", scatter_dimension=1, tiled=True
            ).astype(jnp.float32),
            lax.psum_scatter(
                expanded[7].astype(jnp.bfloat16), "shard", scatter_dimension=1, tiled=True
            ).astype(jnp.float32),
            lax.psum_scatter(
                expanded[8].astype(jnp.bfloat16), "shard", scatter_dimension=1, tiled=True
            ).astype(jnp.float32),
            lax.psum_scatter(
                expanded[9].astype(jnp.bfloat16), "shard", scatter_dimension=1, tiled=True
            ).astype(jnp.float32),
            lax.psum_scatter(
                expanded[10].astype(jnp.bfloat16), "shard", scatter_dimension=1, tiled=True
            ).astype(jnp.float32),
            lax.psum_scatter(
                expanded[11].astype(jnp.bfloat16), "shard", scatter_dimension=1, tiled=True
            ).astype(jnp.float32),
            lax.psum_scatter(
                expanded[12].astype(jnp.bfloat16), "shard", scatter_dimension=1, tiled=True
            ).astype(jnp.float32),
        )
        owned_sum = reduced if owned_sum is None else jax.tree.map(jnp.add, owned_sum, reduced)
    totals = (
        lax.psum(owned_sum[0].astype(jnp.bfloat16), "replica").astype(jnp.float32),
        lax.psum(owned_sum[1].astype(jnp.bfloat16), "replica").astype(jnp.float32),
        lax.psum(owned_sum[2].astype(jnp.bfloat16), "replica").astype(jnp.float32),
        lax.psum(owned_sum[3].astype(jnp.bfloat16), "replica").astype(jnp.float32),
        lax.psum(owned_sum[4].astype(jnp.bfloat16), "replica").astype(jnp.float32),
        lax.psum(owned_sum[5].astype(jnp.bfloat16), "replica").astype(jnp.float32),
        lax.psum(owned_sum[6].astype(jnp.bfloat16), "replica").astype(jnp.float32),
        lax.psum(owned_sum[7].astype(jnp.bfloat16), "replica").astype(jnp.float32),
        lax.psum(owned_sum[8].astype(jnp.bfloat16), "replica").astype(jnp.float32),
        lax.psum(owned_sum[9].astype(jnp.bfloat16), "replica").astype(jnp.float32),
        lax.psum(owned_sum[10].astype(jnp.bfloat16), "replica").astype(jnp.float32),
        lax.psum(owned_sum[11].astype(jnp.bfloat16), "replica").astype(jnp.float32),
        lax.psum(owned_sum[12].astype(jnp.bfloat16), "replica").astype(jnp.float32),
    )
    layer_outputs = jnp.concatenate(
        [
            jnp.where(first_section, outputs[batch_index], outputs[batch_index + 1])
            for batch_index in range(MICRO)
        ],
        0,
    )[None]
    input_grads = jnp.concatenate(
        [
            jnp.where(first_section, grad_parts[batch_index + 1], grad_parts[batch_index])
            for batch_index in range(MICRO)
        ],
        0,
    )[None]
    return (layer_outputs, input_grads) + tuple(totals)


def solution(mesh):
    placed = (
        P(("shard", "replica"), None, None),
        P(("shard", "replica")),
        P(("shard", "replica"), None, None),
        P("section", "shard", None),
        P("section", "shard", None),
        P("section", "shard", None),
        P("section", "shard", None),
        P("section", "shard"),
        P("section", "shard"),
        P("section", "shard"),
        P("section", "shard"),
        P("section", "shard"),
        P("section", "shard"),
        P("section", "shard"),
        P("section", "shard"),
        P("section", "shard"),
    )
    return jax.shard_map(
        local,
        mesh=mesh,
        in_specs=placed,
        out_specs=(
            P("section", ("shard", "replica"), None, None),
            P("section", ("shard", "replica"), None, None),
            P("section", "shard", None),
            P("section", "shard", None),
            P("section", "shard", None),
            P("section", "shard", None),
            P("section", "shard"),
            P("section", "shard"),
            P("section", "shard"),
            P("section", "shard"),
            P("section", "shard"),
            P("section", "shard"),
            P("section", "shard"),
            P("section", "shard"),
            P("section", "shard"),
        ),
        check_vma=False,
    )
```

profile of v0, /device:TPU:0, one launch (start us, length us, event | category | flops | bytes accessed | tf_op | source)
XLA Modules:
  0.0 1066.1 jit_solution(12353294064508752497)
XLA Ops:
  51.9 25.3 %all_gather.28 = bf16[1,384,1152]{2,1,0:T(8,128)(2,1)S(1)} all-gather(bf16[1,96,1152]{2,1,0:T(8,128)(2,1)S(1)} %copy-done.123), channel_id=1, replica_groups=mesh['section'=2,'shard'=4,'replica'=4] {'shard'}, dimensions={1}, use_global_device_ids=true | all-gather | bytes 1105920 | tf_op jit(solution)/shard_map/all_gather | solution.py:225
  262.9 18.8 %reduce-scatter.148.cloned.1.call-done = bf16[96,1]{1,0:T(8,128)(2,1)} async-done(((bf16[384,1]{1,0:T(8,128)(2,1)}), bf16[96,1]{1,0:T(8,128)(2,1)}) %reduce-scatter.148.cloned.1.call-update) | async-done | bytes 208
  282.5 20.8 %reduce-scatter.136.cloned.1.call-done = bf16[384,1]{1,0:T(8,128)(2,1)} async-done(((bf16[1536,1]{1,0:T(8,128)(2,1)}), bf16[384,1]{1,0:T(8,128)(2,1)}) %reduce-scatter.136.cloned.1.call-update) | async-done | bytes 784
  323.7 18.7 %reduce-scatter.168.cloned.1.call-done = bf16[96,1]{1,0:T(8,128)(2,1)} async-done(((bf16[384,1]{1,0:T(8,128)(2,1)}), bf16[96,1]{1,0:T(8,128)(2,1)}) %reduce-scatter.168.cloned.1.call-update) | async-done | bytes 208
  343.2 18.8 %reduce-scatter.162.cloned.1.call-done = bf16[96,1]{1,0:T(8,128)(2,1)} async-done(((bf16[384,1]{1,0:T(8,128)(2,1)}), bf16[96,1]{1,0:T(8,128)(2,1)}) %reduce-scatter.162.cloned.1.call-update) | async-done | bytes 208
  362.8 18.7 %reduce-scatter.144.cloned.1.call-done = bf16[96,1]{1,0:T(8,128)(2,1)} async-done(((bf16[384,1]{1,0:T(8,128)(2,1)}), bf16[96,1]{1,0:T(8,128)(2,1)}) %reduce-scatter.144.cloned.1.call-update) | async-done | bytes 208
  382.3 18.6 %reduce-scatter.132.cloned.1.call-done = bf16[96,1]{1,0:T(8,128)(2,1)} async-done(((bf16[384,1]{1,0:T(8,128)(2,1)}), bf16[96,1]{1,0:T(8,128)(2,1)}) %reduce-scatter.132.cloned.1.call-update) | async-done | bytes 208
  421.1 18.7 %reduce-scatter.120.cloned.1.call-done = bf16[96,1]{1,0:T(8,128)(2,1)} async-done(((bf16[384,1]{1,0:T(8,128)(2,1)}), bf16[96,1]{1,0:T(8,128)(2,1)}) %reduce-scatter.120.cloned.1.call-update) | async-done | bytes 208
  440.6 18.7 %reduce-scatter.156.cloned.1.call-done = bf16[96,1]{1,0:T(8,128)(2,1)} async-done(((bf16[384,1]{1,0:T(8,128)(2,1)}), bf16[96,1]{1,0:T(8,128)(2,1)}) %reduce-scatter.156.cloned.1.call-update) | async-done | bytes 208
  460.1 18.8 %reduce-scatter.150.cloned.1.call-done = bf16[96,1]{1,0:T(8,128)(2,1)} async-done(((bf16[384,1]{1,0:T(8,128)(2,1)}), bf16[96,1]{1,0:T(8,128)(2,1)}) %reduce-scatter.150.cloned.1.call-update) | async-done | bytes 208
  479.7 20.8 %reduce-scatter.138.cloned.1.call-done = bf16[384,1]{1,0:T(8,128)(2,1)} async-done(((bf16[1536,1]{1,0:T(8,128)(2,1)}), bf16[384,1]{1,0:T(8,128)(2,1)}) %reduce-scatter.138.cloned.1.call-update) | async-done | bytes 784
  520.9 18.8 %reduce-scatter.170.cloned.1.call-done = bf16[96,1]{1,0:T(8,128)(2,1)} async-done(((bf16[384,1]{1,0:T(8,128)(2,1)}), bf16[96,1]{1,0:T(8,128)(2,1)}) %reduce-scatter.170.cloned.1.call-update) | async-done | bytes 208
  540.5 18.8 %reduce-scatter.164.cloned.1.call-done = bf16[96,1]{1,0:T(8,128)(2,1)} async-done(((bf16[384,1]{1,0:T(8,128)(2,1)}), bf16[96,1]{1,0:T(8,128)(2,1)}) %reduce-scatter.164.cloned.1.call-update) | async-done | bytes 208
  560.1 18.7 %reduce-scatter.146.cloned.1.call-done = bf16[96,1]{1,0:T(8,128)(2,1)} async-done(((bf16[384,1]{1,0:T(8,128)(2,1)}), bf16[96,1]{1,0:T(8,128)(2,1)}) %reduce-scatter.146.cloned.1.call-update) | async-done | bytes 208
  579.6 19.4 %reduce-scatter.128.cloned.1.call-done = bf16[96,1]{1,0:T(8,128)(2,1)} async-done(((bf16[384,1]{1,0:T(8,128)(2,1)}), bf16[96,1]{1,0:T(8,128)(2,1)}) %reduce-scatter.128.cloned.1.call-update) | async-done | bytes 208
  599.7 18.7 %reduce-scatter.122.cloned.1.call-done = bf16[96,1]{1,0:T(8,128)(2,1)} async-done(((bf16[384,1]{1,0:T(8,128)(2,1)}), bf16[96,1]{1,0:T(8,128)(2,1)}) %reduce-scatter.122.cloned.1.call-update) | async-done | bytes 208
  619.2 18.6 %reduce-scatter.158.cloned.1.call-done = bf16[96,1]{1,0:T(8,128)(2,1)} async-done(((bf16[384,1]{1,0:T(8,128)(2,1)}), bf16[96,1]{1,0:T(8,128)(2,1)}) %reduce-scatter.158.cloned.1.call-update) | async-done | bytes 208
  638.6 18.8 %reduce-scatter.152.cloned.1.call-done = bf16[96,1]{1,0:T(8,128)(2,1)} async-done(((bf16[384,1]{1,0:T(8,128)(2,1)}), bf16[96,1]{1,0:T(8,128)(2,1)}) %reduce-scatter.152.cloned.1.call-update) | async-done | bytes 208
  658.3 19.6 %reduce-scatter.100.cloned.1.call-done = bf16[1,96,384]{2,1,0:T(8,128)(2,1)} async-done(((bf16[1,384,384]{2,1,0:T(8,128)(2,1)}), bf16[1,96,384]{2,1,0:T(8,128)(2,1)}) %reduce-scatter.100.cloned.1.call-update) | async-done | bytes 73744 | tf_op jit(solution)/shard_map/reduce_scatter | solution.py:299
  677.8 20.3 %reduce-scatter.102.cloned.1.call-done = bf16[1,96,384]{2,1,0:T(8,128)(2,1)} async-done(((bf16[1,384,384]{2,1,0:T(8,128)(2,1)}), bf16[1,96,384]{2,1,0:T(8,128)(2,1)}) %reduce-scatter.102.cloned.1.call-update) | async-done | bytes 73744 | tf_op jit(solution)/shard_map/reduce_scatter | solution.py:299
  698.1 21.0 %reduce-scatter.104.cloned.1.call-done = bf16[1,96,384]{2,1,0:T(8,128)(2,1)} async-done(((bf16[1,384,384]{2,1,0:T(8,128)(2,1)}), bf16[1,96,384]{2,1,0:T(8,128)(2,1)}) %reduce-scatter.104.cloned.1.call-update) | async-done | bytes 73744 | tf_op jit(solution)/shard_map/reduce_scatter | solution.py:299
  720.7 23.6 %reduce-scatter.94.cloned.1.call-done = bf16[1,96,1152]{2,1,0:T(8,128)(2,1)} async-done(((bf16[1,384,1152]{2,1,0:T(8,128)(2,1)}), bf16[1,96,1152]{2,1,0:T(8,128)(2,1)}) %reduce-scatter.94.cloned.1.call-update) | async-done | bytes 221200 | tf_op jit(solution)/shard_map/reduce_scatter | solution.py:296
  744.2 25.8 %reduce-scatter.96.cloned.1.call-done = bf16[1,96,1152]{2,1,0:T(8,128)(2,1)} async-done(((bf16[1,384,1152]{2,1,0:T(8,128)(2,1)}), bf16[1,96,1152]{2,1,0:T(8,128)(2,1)}) %reduce-scatter.96.cloned.1.call-update) | async-done | bytes 221200 | tf_op jit(solution)/shard_map/reduce_scatter | solution.py:296
  770.1 26.0 %reduce-scatter.98.cloned.1.call-done = bf16[1,96,1152]{2,1,0:T(8,128)(2,1)} async-done(((bf16[1,384,1152]{2,1,0:T(8,128)(2,1)}), bf16[1,96,1152]{2,1,0:T(8,128)(2,1)}) %reduce-scatter.98.cloned.1.call-update) | async-done | bytes 221200 | tf_op jit(solution)/shard_map/reduce_scatter | solution.py:296
  798.0 28.6 %reduce-scatter.106.cloned.1.call-done = bf16[1,96,1536]{2,1,0:T(8,128)(2,1)} async-done(((bf16[1,384,1536]{2,1,0:T(8,128)(2,1)}), bf16[1,96,1536]{2,1,0:T(8,128)(2,1)}) %reduce-scatter.106.cloned.1.call-update) | async-done | bytes 294928 | tf_op jit(solution)/shard_map/reduce_scatter | solution.py:302
  826.6 30.1 %reduce-scatter.108.cloned.1.call-done = bf16[1,96,1536]{2,1,0:T(8,128)(2,1)} async-done(((bf16[1,384,1536]{2,1,0:T(8,128)(2,1)}), bf16[1,96,1536]{2,1,0:T(8,128)(2,1)}) %reduce-scatter.108.cloned.1.call-update) | async-done | bytes 294928 | tf_op jit(solution)/shard_map/reduce_scatter | solution.py:302
  856.7 30.1 %reduce-scatter.110.cloned.1.call-done = bf16[1,96,1536]{2,1,0:T(8,128)(2,1)} async-done(((bf16[1,384,1536]{2,1,0:T(8,128)(2,1)}), bf16[1,96,1536]{2,1,0:T(8,128)(2,1)}) %reduce-scatter.110.cloned.1.call-update) | async-done | bytes 294928 | tf_op jit(solution)/shard_map/reduce_scatter | solution.py:302
  888.7 28.3 %reduce-scatter.112.cloned.1.call-done = bf16[1,384,384]{2,1,0:T(8,128)(2,1)} async-done(((bf16[1,1536,384]{2,1,0:T(8,128)(2,1)}), bf16[1,384,384]{2,1,0:T(8,128)(2,1)}) %reduce-scatter.112.cloned.1.call-update) | async-done | bytes 294928 | tf_op jit(solution)/shard_map/reduce_scatter | solution.py:305
  917.0 30.1 %reduce-scatter.114.cloned.1.call-done = bf16[1,384,384]{2,1,0:T(8,128)(2,1)} async-done(((bf16[1,1536,384]{2,1,0:T(8,128)(2,1)}), bf16[1,384,384]{2,1,0:T(8,128)(2,1)}) %reduce-scatter.114.cloned.1.call-update) | async-done | bytes 294928 | tf_op jit(solution)/shard_map/reduce_scatter | solution.py:305
  947.1 30.2 %reduce-scatter.116.cloned.1.call-done = bf16[1,384,384]{2,1,0:T(8,128)(2,1)} async-done(((bf16[1,1536,384]{2,1,0:T(8,128)(2,1)}), bf16[1,384,384]{2,1,0:T(8,128)(2,1)}) %reduce-scatter.116.cloned.1.call-update) | async-done | bytes 294928 | tf_op jit(solution)/shard_map/reduce_scatter | solution.py:305
  979.4 20.2 %reduce-scatter.140.cloned.1.call-done = bf16[384,1]{1,0:T(8,128)(2,1)} async-done(((bf16[1536,1]{1,0:T(8,128)(2,1)}), bf16[384,1]{1,0:T(8,128)(2,1)}) %reduce-scatter.140.cloned.1.call-update) | async-done | bytes 784
  1015.3 37.8 %all-reduce.13.cloned.1.call-done = (bf16[1,96,1152]{2,1,0:T(8,128)(2,1)}, bf16[1,96,384]{2,1,0:T(8,128)(2,1)}, bf16[1,96,1536]{2,1,0:T(8,128)(2,1)}, bf16[1,384,384]{2,1,0:T(8,128)(2,1)}) async-done(((bf16[1,96,1152]{2,1,0:T(8,128)(2,1)}, bf16[1,96,384]{2,1,0:T(8,128)(2,1)}, bf16[1,96,1536]{2,1,0:T(8,128)(2,1)}, bf16[1,384,384]{2,1,0:T(8,128)(2,1)}), (bf16[1,96,1152]{2,1,0:T(8,128)(2,1)}, ...) | async-done | bytes 884752 | tf_op jit(solution)/shard_map/psum | solution.py:338
  (652 shorter events, 340.7 us)
Async XLA Ops:
  8.7 244.2 %reduce-scatter.130.cloned.1.call-start = ((), (), s32[]{:S(2)}) async-start(), calls=%async_computation.59 | async-start | bytes 122880
  154.6 168.3 %reduce-scatter.142.cloned.1.call-start = ((), (), s32[]{:S(2)}) async-start(), calls=%async_computation.65 | async-start | bytes 122880
  198.7 163.3 %reduce-scatter.162.cloned.1.call-start = ((), (), s32[]{:S(2)}) async-start(), calls=%async_computation.75 | async-start | bytes 122880
  199.5 181.9 %reduce-scatter.144.cloned.1.call-start = ((), (), s32[]{:S(2)}) async-start(), calls=%async_computation.66 | async-start | bytes 122880
  200.4 200.5 %reduce-scatter.132.cloned.1.call-start = ((), (), s32[]{:S(2)}) async-start(), calls=%async_computation.60 | async-start | bytes 122880
  201.2 219.1 %reduce-scatter.126.cloned.1.call-start = ((), (), s32[]{:S(2)}) async-start(), calls=%async_computation.57 | async-start | bytes 122880
  203.2 236.6 %reduce-scatter.120.cloned.1.call-start = ((), (), s32[]{:S(2)}) async-start(), calls=%async_computation.54 | async-start | bytes 122880
  204.1 255.1 %reduce-scatter.156.cloned.1.call-start = ((), (), s32[]{:S(2)}) async-start(), calls=%async_computation.72 | async-start | bytes 122880
  205.0 273.9 %reduce-scatter.150.cloned.1.call-start = ((), (), s32[]{:S(2)}) async-start(), calls=%async_computation.69 | async-start | bytes 122880
  210.3 290.2 %reduce-scatter.138.cloned.1.call-start = ((), (), s32[]{:S(2)}) async-start(), calls=%async_computation.63 | async-start | bytes 491520
  211.4 308.7 %reduce-scatter.134.cloned.1.call-start = ((), (), s32[]{:S(2)}) async-start(), calls=%async_computation.61 | async-start | bytes 122880
  224.8 314.9 %reduce-scatter.170.cloned.1.call-start = ((), (), s32[]{:S(2)}) async-start(), calls=%async_computation.79 | async-start | bytes 122880
  225.6 333.7 %reduce-scatter.164.cloned.1.call-start = ((), (), s32[]{:S(2)}) async-start(), calls=%async_computation.76 | async-start | bytes 122880
  226.4 352.3 %reduce-scatter.146.cloned.1.call-start = ((), (), s32[]{:S(2)}) async-start(), calls=%async_computation.67 | async-start | bytes 122880
  227.3 371.7 %reduce-scatter.128.cloned.1.call-start = ((), (), s32[]{:S(2)}) async-start(), calls=%async_computation.58 | async-start | bytes 122880
  229.1 389.3 %reduce-scatter.122.cloned.1.call-start = ((), (), s32[]{:S(2)}) async-start(), calls=%async_computation.55 | async-start | bytes 122880
  232.5 405.4 %reduce-scatter.158.cloned.1.call-start = ((), (), s32[]{:S(2)}) async-start(), calls=%async_computation.73 | async-start | bytes 122880
  233.3 424.1 %reduce-scatter.152.cloned.1.call-start = ((), (), s32[]{:S(2)}) async-start(), calls=%async_computation.70 | async-start | bytes 122880
  234.1 443.7 %reduce-scatter.100.cloned.1.call-start = ((), (), s32[]{:S(2)}) async-start(), calls=%async_computation.44 | async-start | bytes 368640 | tf_op jit(solution)/shard_map/reduce_scatter | solution.py:299
  235.3 462.8 %reduce-scatter.102.cloned.1.call-start = ((), (), s32[]{:S(2)}) async-start(), calls=%async_computation.45 | async-start | bytes 368640 | tf_op jit(solution)/shard_map/reduce_scatter | solution.py:299
  236.4 482.7 %reduce-scatter.104.cloned.1.call-start = ((), (), s32[]{:S(2)}) async-start(), calls=%async_computation.46 | async-start | bytes 368640 | tf_op jit(solution)/shard_map/reduce_scatter | solution.py:299
  237.5 506.8 %reduce-scatter.94.cloned.1.call-start = ((), (), s32[]{:S(2)}) async-start(), calls=%async_computation.41 | async-start | bytes 1105920 | tf_op jit(solution)/shard_map/reduce_scatter | solution.py:296
  239.0 531.0 %reduce-scatter.96.cloned.1.call-start = ((), (), s32[]{:S(2)}) async-start(), calls=%async_computation.42 | async-start | bytes 1105920 | tf_op jit(solution)/shard_map/reduce_scatter | solution.py:296
  240.6 555.4 %reduce-scatter.98.cloned.1.call-start = ((), (), s32[]{:S(2)}) async-start(), calls=%async_computation.43 | async-start | bytes 1105920 | tf_op jit(solution)/shard_map/reduce_scatter | solution.py:296
  242.1 584.4 %reduce-scatter.106.cloned.1.call-start = ((), (), s32[]{:S(2)}) async-start(), calls=%async_computation.47 | async-start | bytes 1474560 | tf_op jit(solution)/shard_map/reduce_scatter | solution.py:302
  243.8 612.9 %reduce-scatter.108.cloned.1.call-start = ((), (), s32[]{:S(2)}) async-start(), calls=%async_computation.48 | async-start | bytes 1474560 | tf_op jit(solution)/shard_map/reduce_scatter | solution.py:302
  245.4 641.3 %reduce-scatter.110.cloned.1.call-start = ((), (), s32[]{:S(2)}) async-start(), calls=%async_computation.49 | async-start | bytes 1474560 | tf_op jit(solution)/shard_map/reduce_scatter | solution.py:302
  247.1 669.9 %reduce-scatter.112.cloned.1.call-start = ((), (), s32[]{:S(2)}) async-start(), calls=%async_computation.50 | async-start | bytes 1474560 | tf_op jit(solution)/shard_map/reduce_scatter | solution.py:305
  248.9 698.3 %reduce-scatter.114.cloned.1.call-start = ((), (), s32[]{:S(2)}) async-start(), calls=%async_computation.51 | async-start | bytes 1474560 | tf_op jit(solution)/shard_map/reduce_scatter | solution.py:305
  250.6 726.8 %reduce-scatter.116.cloned.1.call-start = ((), (), s32[]{:S(2)}) async-start(), calls=%async_computation.52 | async-start | bytes 1474560 | tf_op jit(solution)/shard_map/reduce_scatter | solution.py:305
  252.5 747.1 %reduce-scatter.140.cloned.1.call-start = ((), (), s32[]{:S(2)}) async-start(), calls=%async_computation.64 | async-start | bytes 491520
  503.9 549.2 %all-reduce.13.cloned.1.call-start = ((), (), s32[]{:S(2)}) async-start(), calls=%async_computation.80 | async-start | bytes 1769472 | tf_op jit(solution)/shard_map/psum | solution.py:338
  (148 other events, 2891.2 us)
Sparse Core Ops, SparseCore 0:
  9.6 38.2 all-gather.2
  49.4 36.3 all-gather.4
  145.2 19.2 reduce-scatter.129
  186.0 17.3 reduce-scatter.159
  225.0 17.3 reduce-scatter.117
  244.7 17.3 reduce-scatter.153
  264.3 17.3 reduce-scatter.147
  284.5 18.7 reduce-scatter.135
  305.5 17.3 reduce-scatter.141
  344.6 17.3 reduce-scatter.161
  383.6 17.3 reduce-scatter.131
  422.4 17.3 reduce-scatter.119
  461.5 17.3 reduce-scatter.149
  481.7 18.7 reduce-scatter.137
  502.7 17.3 reduce-scatter.133
  542.0 17.3 reduce-scatter.163
  581.6 17.3 reduce-scatter.127
  620.5 17.3 reduce-scatter.157
  659.7 18.0 reduce-scatter.99
  679.9 18.0 reduce-scatter.101
  700.9 18.0 reduce-scatter.103
  721.4 22.8 reduce-scatter.93
  746.4 23.6 reduce-scatter.95
  772.4 23.6 reduce-scatter.97
  798.4 28.1 reduce-scatter.105
  828.8 27.8 reduce-scatter.107
  858.9 27.8 reduce-scatter.109
  889.1 27.8 reduce-scatter.111
  919.2 27.8 reduce-scatter.113
  949.4 27.8 reduce-scatter.115
  980.2 19.2 reduce-scatter.139
  1003.9 49.1 all-reduce.12
  (10 shorter events, 171.7 us)
where the time goes:
time: 1080 us; the launch traced here: 1070 us
  waiting for transfers between devices  767 us (71%)
  local copies, waits for them, and re-layouts  81.1 us (8%)
  blocking collectives  78.2 us (7%)
  matrix products  70.7 us (7%)
  other arithmetic  43.4 us (4%)
  between operations  17.5 us (2%)
    unnamed x69, waiting for transfers between devices  402 us
    reduce_scatter x3, waiting for transfers between devices, local(): lax.psum_scatter(expanded[2].astype(jnp.bfloat16), 'shard', scatter_dimen...  88.8 us
    reduce_scatter x3, waiting for transfers between devices, local(): lax.psum_scatter(expanded[3].astype(jnp.bfloat16), 'shard', scatter_dimen...  88.6 us
    reduce_scatter x3, waiting for transfers between devices, local(): lax.psum_scatter(expanded[0].astype(jnp.bfloat16), 'shard', scatter_dimen...  75.4 us
    reduce_scatter x3, waiting for transfers between devices, local(): lax.psum_scatter(expanded[1].astype(jnp.bfloat16), 'shard', scatter_dimen...  60.8 us
    unnamed x330, local copies, waits for them, and re-layouts  53.4 us
    psum x1, waiting for transfers between devices, local(): lax.psum(owned_sum[0].astype(jnp.bfloat16), 'replica').astype(jnp.float32)  37.8 us
    all_gather x1, blocking collectives, fetch_weights(): lax.all_gather(w_qkv, 'shard', axis=1, tiled=True)  25.3 us
  transfers between devices with their start and end apart: 46, of which 38 were waited for; matrix products, arithmetic and copies ran while one was open for 13% of the time, Pallas kernels for 0%

commit v1 on v0

v1 whole, which is shorter than its diff:
```python
import functools

import jax
import jax.numpy as jnp
from jax import lax
from jax.experimental import pallas as pl
from jax.experimental.pallas import tpu as pltpu
from jax.sharding import PartitionSpec as P

HEAD_DIM = 64
EPSILON = 1e-06
ROOT_HALF = 0.7071067811865476
INVERSE_ROOT_TWO_PI = 0.3989422804014327
F32 = jnp.float32
BF16 = jnp.bfloat16
LANES = 128
VMEM_LIMIT = 48 * 1024 * 1024

BIAS_Q, BIAS_V, BIAS_OUT, BIAS_DOWN, GAIN_ONE, OFFSET_ONE, GAIN_TWO, OFFSET_TWO = range(8)


def dot(a, b):
    return lax.dot_general(a, b, (((1,), (0,)), ((), ())), preferred_element_type=F32)


def dot_back(a, b):
    return lax.dot_general(a, b, (((1,), (1,)), ((), ())), preferred_element_type=F32)


def dot_rows(a, b):
    return lax.dot_general(a, b, (((0,), (0,)), ((), ())), preferred_element_type=F32)


def normalize(values):
    row_mean = jnp.mean(values, -1, keepdims=True)
    centred = values - row_mean
    inverse = lax.rsqrt(jnp.mean(centred * centred, -1, keepdims=True) + EPSILON)
    return centred * inverse, inverse


def norm_backward(grad, unit, inverse):
    centre = jnp.mean(grad, -1, keepdims=True)
    slope = jnp.mean(grad * unit, -1, keepdims=True)
    return inverse * (grad - centre - unit * slope)


def total(values):
    return jnp.sum(values, axis=0, keepdims=True)


def head_masks(rows):
    lane = lax.broadcasted_iota(jnp.int32, (rows, LANES), 1)
    return (lane < HEAD_DIM, lane >= HEAD_DIM)


def pick(mask, value):
    return jnp.where(mask, value.astype(F32), 0.0).astype(BF16)


def layer_forward(x, seq, weights, vec, bias_up, acts):
    rows, width = x.shape
    w_qkv, w_out, w_up, w_down = weights
    qkv_ref, p_ref, attended_ref, hidden_ref, act_ref, slope_ref = acts
    unit, _ = normalize(x)
    normed = (unit * vec(GAIN_ONE) + vec(OFFSET_ONE)).astype(BF16)
    qkv = dot(normed, w_qkv())
    queries = (qkv[:, :width] + vec(BIAS_Q)).astype(BF16).astype(F32) * HEAD_DIM ** (-0.5)
    qkv_ref[:, :width] = queries.astype(BF16)
    qkv_ref[:, width : 2 * width] = qkv[:, width : 2 * width].astype(BF16)
    qkv_ref[:, 2 * width :] = (qkv[:, 2 * width :] + vec(BIAS_V)).astype(BF16)
    masks = head_masks(rows)
    key_live = lax.broadcasted_iota(jnp.int32, (rows, rows), 1) < seq
    for pair in range(width // LANES):
        lo = pair * LANES
        q = qkv_ref[:, lo : lo + LANES]
        k = qkv_ref[:, width + lo : width + lo + LANES]
        v = qkv_ref[:, 2 * width + lo : 2 * width + lo + LANES]
        gathered = None
        for half in range(2):
            scores = dot_back(pick(masks[half], q), k)
            scores = jnp.where(key_live, scores, -1e30)
            scores = jnp.exp(scores - jnp.max(scores, -1, keepdims=True))
            prob = (scores * (1.0 / jnp.sum(scores, -1, keepdims=True))).astype(BF16)
            p_ref[2 * pair + half] = prob
            part = dot(prob, pick(masks[half], v))
            gathered = part if gathered is None else gathered + part
        attended_ref[:, lo : lo + LANES] = gathered.astype(BF16)
    hidden = x + dot(attended_ref[...], w_out()) + vec(BIAS_OUT)
    hidden_ref[...] = hidden
    unit_two, _ = normalize(hidden)
    normed_two = (unit_two * vec(GAIN_TWO) + vec(OFFSET_TWO)).astype(BF16)
    output = hidden + vec(BIAS_DOWN)
    wide = act_ref.shape[1]
    step = 512
    for lo in range(0, wide, step):
        up = dot(normed_two, w_up(lo, step)) + bias_up(lo, step)
        cdf = 0.5 * (1.0 + lax.erf(up * ROOT_HALF))
        density = jnp.exp(-0.5 * up * up) * INVERSE_ROOT_TWO_PI
        act = (up * cdf).astype(BF16)
        act_ref[:, lo : lo + step] = act
        slope_ref[:, lo : lo + step] = (cdf + up * density).astype(BF16)
        output = output + dot(act, w_down(lo, step))
    return output


def layer_backward(grad, x, weights, vec, acts, up_grad_ref, qkv_grad_ref, put):
    rows, width = grad.shape
    w_qkv, w_out, w_up, w_down = weights
    qkv_ref, p_ref, attended_ref, hidden_ref, act_ref, slope_ref = acts
    wide = act_ref.shape[1]
    step = 512
    down_grad = grad.astype(BF16)
    unit_two, inverse_two = normalize(hidden_ref[...])
    normed_two = (unit_two * vec(GAIN_TWO) + vec(OFFSET_TWO)).astype(BF16)
    grad_normed_two = None
    sums_up = []
    for lo in range(0, wide, step):
        put.w_down(lo, dot_rows(act_ref[:, lo : lo + step], down_grad))
        up_grad = dot_back(down_grad, w_down(lo, step)) * slope_ref[:, lo : lo + step].astype(F32)
        up_grad = up_grad.astype(BF16)
        sums_up.append(total(up_grad.astype(F32)))
        put.w_up(lo, dot_rows(normed_two, up_grad))
        part = dot_back(up_grad, w_up(lo, step))
        grad_normed_two = part if grad_normed_two is None else grad_normed_two + part
    grad_hidden = grad + norm_backward(grad_normed_two * vec(GAIN_TWO), unit_two, inverse_two)
    out_grad = grad_hidden.astype(BF16)
    put.w_out(dot_rows(attended_ref[...], out_grad))
    attended_grad = dot_back(out_grad, w_out()).astype(BF16)
    masks = head_masks(rows)
    for pair in range(width // LANES):
        lo = pair * LANES
        q = qkv_ref[:, lo : lo + LANES]
        k = qkv_ref[:, width + lo : width + lo + LANES]
        v = qkv_ref[:, 2 * width + lo : 2 * width + lo + LANES]
        ag = attended_grad[:, lo : lo + LANES]
        q_grad = k_grad = v_grad = None
        for half in range(2):
            mine = pick(masks[half], ag)
            prob = p_ref[2 * pair + half]
            prob32 = prob.astype(F32)
            grad_prob = dot_back(mine, v)
            dv = dot_rows(prob, mine)
            row_term = jnp.sum(grad_prob * prob32, -1, keepdims=True)
            score_grad = (prob32 * (grad_prob - row_term)).astype(BF16)
            dq = dot(score_grad, pick(masks[half], k))
            dk = dot_rows(score_grad, pick(masks[half], q))
            q_grad = dq if q_grad is None else q_grad + dq
            k_grad = dk if k_grad is None else k_grad + dk
            v_grad = dv if v_grad is None else v_grad + dv
        qkv_grad_ref[:, lo : lo + LANES] = (q_grad * HEAD_DIM ** (-0.5)).astype(BF16)
        qkv_grad_ref[:, width + lo : width + lo + LANES] = k_grad.astype(BF16)
        qkv_grad_ref[:, 2 * width + lo : 2 * width + lo + LANES] = v_grad.astype(BF16)
    unit, inverse = normalize(x)
    normed = (unit * vec(GAIN_ONE) + vec(OFFSET_ONE)).astype(BF16)
    put.w_qkv(dot_rows(normed, qkv_grad_ref[...]))
    grad_normed = dot_back(qkv_grad_ref[...], w_qkv())
    grad_x = grad_hidden + norm_backward(grad_normed * vec(GAIN_ONE), unit, inverse)
    sums = jnp.concatenate(
        [
            total(qkv_grad_ref[:, :width].astype(F32)),
            total(qkv_grad_ref[:, 2 * width :].astype(F32)),
            total(grad_hidden),
            total(grad),
            total(grad_normed * unit),
            total(grad_normed),
            total(grad_normed_two * unit_two),
            total(grad_normed_two),
        ],
        0,
    )
    put.vectors(sums, jnp.concatenate(sums_up, 1))
    return grad_x


ROWS = 96
HALF = 48
UP0, QKV0, OUT0, DOWN0, VEC0, PACKED = 0, 1536, 2688, 3072, 4608, 4736
QUARTER = 896
TAIL0, TAIL = 3584, 1152
PIECE = 1280
SEQ_ROWS = 208


def positions():
    return lax.axis_index("section"), lax.axis_index("shard"), lax.axis_index("replica")


class PackedPut:
    def __init__(self, grads, shard, replica):
        self.grads, self.shard, self.replica = grads, shard, replica

    def store(self, owner, column, value, row=0):
        place = lax.rem(owner - self.shard + 4, 4)
        rows, columns = value.shape
        value = value.astype(BF16)
        while columns:
            piece, inside = column // PIECE, column % PIECE
            count = min(columns, PIECE - inside)
            where = lax.bitwise_xor(self.replica, piece)
            for half in range(2):
                lo, hi = max(row, half * HALF), min(row + rows, half * HALF + HALF)
                if lo < hi:
                    self.grads[half, where, place, lo - half * HALF : hi - half * HALF, inside : inside + count] = (
                        value[lo - row : hi - row, :count]
                    )
            value, column, columns = value[:, count:], column + count, columns - count

    def by_rows(self, column, value):
        for owner in range(4):
            self.store(owner, column, value[owner * ROWS : (owner + 1) * ROWS])

    def w_up(self, lo, value):
        self.by_rows(UP0 + lo, value)

    def w_qkv(self, value):
        self.by_rows(QKV0, value)

    def w_out(self, value):
        self.by_rows(OUT0, value)

    def w_down(self, lo, value):
        rows, at = value.shape[0], 0
        while at < rows:
            owner, inside = divmod(lo + at, 4 * ROWS)
            fold, row = divmod(inside, ROWS)
            count = min(rows - at, ROWS - row)
            self.store(owner, DOWN0 + fold * value.shape[1], value[at : at + count], row)
            at += count

    def vectors(self, sums, bias_up):
        place3 = lax.bitwise_xor(self.replica, 3)
        first = VEC0 - 3 * PIECE
        self.grads[:, place3, :, :, first:] = jnp.zeros((2, 4, HALF, PIECE - first), BF16)
        blank = jnp.zeros((8, LANES - ROWS), F32)
        rest = jnp.zeros((5, LANES), F32)
        for owner in range(4):
            up = [
                bias_up[:, owner * 384 + k * LANES : owner * 384 + (k + 1) * LANES] for k in range(3)
            ]
            top = jnp.concatenate([sums[:, owner * ROWS : (owner + 1) * ROWS], blank], 1)
            tile = jnp.concatenate([top] + up + [rest], 0)
            self.store(owner, VEC0, tile)


def packed_weights(packed, down, layer):
    def w_qkv():
        return packed[layer, :, :, QKV0:OUT0].reshape(4 * ROWS, OUT0 - QKV0)

    def w_out():
        return packed[layer, :, :, OUT0:DOWN0].reshape(4 * ROWS, DOWN0 - OUT0)

    def w_up(lo, step):
        return packed[layer, :, :, UP0 + lo : UP0 + lo + step].reshape(4 * ROWS, step)

    def w_down(lo, step):
        return down[layer, lo : lo + step]

    return w_qkv, w_out, w_up, w_down


def unfold(packed, down, vectors, biases, layer):
    width = down.shape[2]
    for owner in range(4):
        for fold in range(4):
            at = (owner * 4 + fold) * ROWS
            down[layer, at : at + ROWS] = packed[
                layer, owner, :, DOWN0 + fold * width : DOWN0 + (fold + 1) * width
            ]
    tiles = [
        packed[layer, owner, 0:16, VEC0:PACKED].astype(F32)
        + packed[layer, owner, 16:32, VEC0:PACKED].astype(F32)
        for owner in range(4)
    ]
    vectors[layer] = jnp.concatenate([tile[0:8, 0:ROWS] for tile in tiles], 1)
    biases[layer] = jnp.concatenate([tile[8 + k : 9 + k] for tile in tiles for k in range(3)], 1)


def start_copies(pieces, packed, layer, sems, shard, replica):
    own, tail1, tail2, tail3, same, across_x, across_y, across_d = pieces
    copies = [(own, packed.at[layer, shard])]
    for step, tail in ((1, tail1), (2, tail2), (3, tail3)):
        copies.append((tail, packed.at[layer, lax.rem(shard + 4 - step, 4), :, pl.ds(TAIL0, TAIL)]))
    for flip, group in ((0, same), (1, across_x), (2, across_y), (3, across_d)):
        column = pl.multiple_of(lax.bitwise_xor(replica, flip) * QUARTER, LANES)
        for step in (1, 2, 3):
            copies.append(
                (
                    group.at[step - 1],
                    packed.at[layer, lax.rem(shard + 4 - step, 4), :, pl.ds(column, QUARTER)],
                )
            )
    return [
        pltpu.make_async_copy(source, target, sems.at[layer, index])
        for index, (source, target) in enumerate(copies)
    ]


def main_kernel(seq, *refs):
    mine, other = refs[0:8], refs[8:16]
    patches, cotangent, live = refs[16:19]
    (
        out_one,
        out_two,
        grad_one,
        keep,
        send,
        kept_weights,
        kept_vectors,
        qkv0,
        p0,
        attended0,
        hidden0,
        act0,
        slope0,
    ) = refs[19:32]
    (
        packed,
        down,
        vectors,
        biases,
        rows_in,
        rows_mid,
        qkv1,
        p1,
        attended1,
        hidden1,
        act1,
        slope1,
        up_grad,
        qkv_grad,
        grads,
        sems,
        out_sems,
    ) = refs[32:]
    section, shard, replica = positions()
    for copy in start_copies(mine, packed, section, sems, shard, replica):
        copy.start()
    for copy in start_copies(other, packed, 1 - section, sems, shard, replica):
        copy.start()
    width = rows_in.shape[1]
    rows_in[seq - seq % 8 :] = jnp.zeros((SEQ_ROWS - seq + seq % 8, width), F32)
    rows_in[:seq] = patches[section].astype(F32)

    def ready(layer):
        for copy in start_copies(mine, packed, layer, sems, shard, replica):
            copy.wait()
        unfold(packed, down, vectors, biases, layer)
        vec = lambda index: vectors[layer, index : index + 1]
        bias_up = lambda lo, step: biases[layer, :, lo : lo + step]
        return packed_weights(packed, down, layer), vec, bias_up

    weights0, vec0, bias_up0 = ready(0)
    save = [
        pltpu.make_async_copy(packed.at[0], kept_weights.at[0], out_sems.at[0]),
    ]
    for copy in save:
        copy.start()
    kept_vectors[...] = vectors[0]
    x0 = rows_in[...]
    acts0 = (qkv0, p0, attended0, hidden0, act0, slope0)
    result = layer_forward(x0, seq, weights0, vec0, bias_up0, acts0)
    out_one[...] = result[:seq].astype(BF16)
    live_rows = lax.broadcasted_iota(jnp.int32, (SEQ_ROWS, width), 0) < seq
    rows_mid[...] = jnp.where(live_rows, result.astype(BF16).astype(F32), 0.0)

    weights1, vec1, bias_up1 = ready(1)
    acts1 = (qkv1, p1, attended1, hidden1, act1, slope1)
    result = layer_forward(rows_mid[...], seq, weights1, vec1, bias_up1, acts1)
    out_two[...] = result[:seq].astype(BF16)

    rows_in[:seq] = cotangent[section].astype(F32) * live[section].astype(F32)
    put = PackedPut(grads, shard, replica)
    grad_x = layer_backward(
        rows_in[...], rows_mid[...], weights1, vec1, acts1, up_grad, qkv_grad, put
    )
    grad_one[...] = grad_x[:seq].astype(BF16)
    copies = [
        pltpu.make_async_copy(grads.at[section], keep, out_sems.at[1]),
        pltpu.make_async_copy(grads.at[1 - section], send, out_sems.at[2]),
    ]
    for copy in copies:
        copy.start()
    for copy in save + copies:
        copy.wait()


def last_kernel(seq, *refs):
    weights, vectors_in, grad_one, patches = refs[0:4]
    acts = refs[4:10]
    grad_out, keep, send = refs[10:13]
    packed, down, rows_in, rows_grad, up_grad, qkv_grad, grads, sems, out_sems = refs[13:]
    section, shard, replica = positions()
    load = pltpu.make_async_copy(weights, packed, sems.at[0])
    load.start()
    width = rows_in.shape[1]
    for buffer, source in ((rows_in, patches[section]), (rows_grad, grad_one[...])):
        buffer[seq - seq % 8 :] = jnp.zeros((SEQ_ROWS - seq + seq % 8, width), F32)
        buffer[:seq] = source.astype(F32)
    load.wait()
    for owner in range(4):
        for fold in range(4):
            at = (owner * 4 + fold) * ROWS
            down[0, at : at + ROWS] = packed[
                0, owner, :, DOWN0 + fold * width : DOWN0 + (fold + 1) * width
            ]
    vec = lambda index: vectors_in[index : index + 1]
    put = PackedPut(grads, shard, replica)
    grad_x = layer_backward(
        rows_grad[...],
        rows_in[...],
        packed_weights(packed, down, 0),
        vec,
        acts,
        up_grad,
        qkv_grad,
        put,
    )
    grad_out[...] = grad_x[:seq]
    copies = [
        pltpu.make_async_copy(grads.at[section], keep, out_sems.at[0]),
        pltpu.make_async_copy(grads.at[1 - section], send, out_sems.at[1]),
    ]
    for copy in copies:
        copy.start()
    for copy in copies:
        copy.wait()


def vmem(count):
    return [pl.BlockSpec(memory_space=pltpu.VMEM)] * count


def anywhere(count):
    return [pl.BlockSpec(memory_space=pl.ANY)] * count


def shape(dims, dtype):
    return jax.ShapeDtypeStruct(dims, dtype)


def act_shapes(width, wide):
    heads = width // HEAD_DIM
    return [
        ((SEQ_ROWS, 3 * width), BF16),
        ((heads, SEQ_ROWS, SEQ_ROWS), BF16),
        ((SEQ_ROWS, width), BF16),
        ((SEQ_ROWS, width), F32),
        ((SEQ_ROWS, wide), BF16),
        ((SEQ_ROWS, wide), BF16),
    ]


PARAMS = pltpu.CompilerParams(vmem_limit_bytes=VMEM_LIMIT)


def run_main(mine, other, patches, cotangent, live, wide):
    seq, width = patches.shape[1:]
    acts = act_shapes(width, wide)
    return pl.pallas_call(
        functools.partial(main_kernel, seq),
        out_shape=[
            shape((seq, width), BF16),
            shape((seq, width), BF16),
            shape((seq, width), BF16),
            shape((4, 4, HALF, PIECE), BF16),
            shape((4, 4, HALF, PIECE), BF16),
            shape((1, 4, ROWS, PACKED), BF16),
            shape((8, width), F32),
        ]
        + [shape(*a) for a in acts],
        in_specs=anywhere(16) + vmem(2) + [pl.BlockSpec(memory_space=pltpu.SMEM)],
        out_specs=vmem(3) + anywhere(3) + vmem(7),
        scratch_shapes=[
            pltpu.VMEM((2, 4, ROWS, PACKED), BF16),
            pltpu.VMEM((2, wide, width), BF16),
            pltpu.VMEM((2, 8, width), F32),
            pltpu.VMEM((2, 1, wide), F32),
            pltpu.VMEM((SEQ_ROWS, width), F32),
            pltpu.VMEM((SEQ_ROWS, width), F32),
        ]
        + [pltpu.VMEM(*a) for a in acts]
        + [
            pltpu.VMEM((SEQ_ROWS, wide), BF16),
            pltpu.VMEM((SEQ_ROWS, 3 * width), BF16),
            pltpu.VMEM((2, 4, 4, HALF, PIECE), BF16),
            pltpu.SemaphoreType.DMA((2, 16)),
            pltpu.SemaphoreType.DMA((3,)),
        ],
        compiler_params=PARAMS,
        name="forward_and_layer_one",
    )(*mine, *other, patches, cotangent, live)


def run_last(weights, vectors, grad_one, patches, acts, wide):
    seq, width = patches.shape[1:]
    return pl.pallas_call(
        functools.partial(last_kernel, seq),
        out_shape=[
            shape((seq, width), F32),
            shape((4, 4, HALF, PIECE), BF16),
            shape((4, 4, HALF, PIECE), BF16),
        ],
        in_specs=anywhere(1) + vmem(9),
        out_specs=vmem(1) + anywhere(2),
        scratch_shapes=[
            pltpu.VMEM((1, 4, ROWS, PACKED), BF16),
            pltpu.VMEM((1, wide, width), BF16),
            pltpu.VMEM((SEQ_ROWS, width), F32),
            pltpu.VMEM((SEQ_ROWS, width), F32),
            pltpu.VMEM((SEQ_ROWS, wide), BF16),
            pltpu.VMEM((SEQ_ROWS, 3 * width), BF16),
            pltpu.VMEM((2, 4, 4, HALF, PIECE), BF16),
            pltpu.SemaphoreType.DMA((1,)),
            pltpu.SemaphoreType.DMA((2,)),
        ],
        compiler_params=PARAMS,
        name="layer_zero_backward",
    )(weights, vectors, grad_one, patches, *acts)


def pair_sum_kernel(keep, recv, *outs):
    for place in range(4):
        outs[place][...] = (keep[place].astype(F32) + recv[place].astype(F32)).astype(BF16)


def pair_sum(keep, recv):
    return pl.pallas_call(
        pair_sum_kernel,
        out_shape=[shape(keep.shape[1:], BF16)] * 4,
        in_specs=vmem(2),
        out_specs=vmem(4),
        compiler_params=PARAMS,
        name="sum_of_cores",
    )(keep, recv)


def plane_sum_kernel(a, b, c, d, *outs):
    for place in range(4):
        outs[place][...] = (
            a[place].astype(F32) + b[place].astype(F32) + (c[place].astype(F32) + d[place].astype(F32))
        ).astype(BF16)


def plane_sum(parts):
    return pl.pallas_call(
        plane_sum_kernel,
        out_shape=[shape(parts[0].shape[1:], BF16)] * 4,
        in_specs=vmem(4),
        out_specs=vmem(4),
        compiler_params=PARAMS,
        name="sum_of_plane",
    )(*parts)


def column_sum_kernel(*refs):
    ins, (mine, other) = refs[:8], refs[8:]
    section = lax.axis_index("section")
    sums = []
    for group in (ins[:4], ins[4:]):
        a, b, c, d = (member[...].astype(F32) for member in group)
        sums.append((a + b + (c + d)).astype(BF16))

    @pl.when(section == 0)
    def _():
        mine[...] = sums[0]
        other[...] = sums[1]

    @pl.when(section == 1)
    def _():
        mine[...] = sums[1]
        other[...] = sums[0]


def column_sum(zero, one):
    return pl.pallas_call(
        column_sum_kernel,
        out_shape=[shape(zero[0].shape, BF16)] * 2,
        in_specs=vmem(8),
        out_specs=vmem(2),
        compiler_params=PARAMS,
        name="sum_of_column",
    )(*zero, *one)


def unpack_kernel(*refs):
    pieces, (qkv, out, up, down), rest = refs[:8], refs[8:12], refs[12:21]
    table, sems = refs[21:]
    section, _, replica = positions()
    copies = []
    for flip in range(4):
        place = lax.bitwise_xor(replica, flip)
        for half in range(2):
            where = section if half == 0 else 1 - section
            copies.append(
                pltpu.make_async_copy(
                    pieces[2 * flip + half], table.at[place, where], sems.at[2 * flip + half]
                )
            )
    for copy in copies:
        copy.start()
    for copy in copies:
        copy.wait()

    def put(target, row, column, start, count, at):
        while count:
            piece, inside = start // PIECE, start % PIECE
            some = min(count, PIECE - inside)
            for half in range(2):
                target[0, row + half * HALF : row + half * HALF + HALF, at : at + some] = table[
                    piece, half, :, inside : inside + some
                ].astype(F32)
            start, at, count = start + some, at + some, count - some

    put(up, 0, 0, UP0, QKV0 - UP0, 0)
    put(qkv, 0, 0, QKV0, OUT0 - QKV0, 0)
    put(out, 0, 0, OUT0, DOWN0 - OUT0, 0)
    width = out.shape[2]
    for fold in range(4):
        put(down, fold * ROWS, 0, DOWN0 + fold * width, width, 0)
    inside = VEC0 - 3 * PIECE
    tile = table[3, 0, 0:16, inside : inside + LANES].astype(F32)
    for index in range(8):
        rest[index][...] = tile[index : index + 1, :ROWS]
    rest[8][...] = jnp.concatenate([tile[8 + k : 9 + k] for k in range(3)], 1)


def unpack(pieces, width, wide):
    return pl.pallas_call(
        unpack_kernel,
        out_shape=[
            shape((1, ROWS, 3 * width), F32),
            shape((1, ROWS, width), F32),
            shape((1, ROWS, wide), F32),
            shape((1, 4 * ROWS, width), F32),
        ]
        + [shape((1, ROWS), F32)] * 8
        + [shape((1, 4 * ROWS), F32)],
        in_specs=anywhere(8),
        out_specs=vmem(13),
        scratch_shapes=[
            pltpu.VMEM((4, 2, HALF, PIECE), BF16),
            pltpu.SemaphoreType.DMA((8,)),
        ],
        compiler_params=PARAMS,
        name="unpack",
    )(*pieces)


def swap(value):
    return lax.ppermute(value, "section", [(0, 1), (1, 0)])


def flip(value, bits):
    return lax.ppermute(value, "replica", [(place, place ^ bits) for place in range(4)])


def shift(value, steps):
    return lax.ppermute(value, "shard", [(place, (place + steps) % 4) for place in range(4)])


def packed_local(patches, live_slots, cotangent, w_qkv, w_out, w_up, w_down, *small):
    bias_q, bias_v, bias_out, bias_up, bias_down, gain_one, offset_one, gain_two, offset_two = small
    section, _, replica = positions()
    width, wide = w_out.shape[2], w_up.shape[2]
    folded = [w_down[0, fold * ROWS : (fold + 1) * ROWS] for fold in range(4)]
    eight = jnp.concatenate(
        [bias_q, bias_v, bias_out, bias_down, gain_one, offset_one, gain_two, offset_two], 0
    )
    eight = jnp.pad(eight, ((0, 0), (0, LANES - ROWS)))
    tile = jnp.concatenate([eight, bias_up.reshape(3, LANES), jnp.zeros((5, LANES), F32)], 0)
    high = tile.astype(BF16)
    low = (tile - high.astype(F32)).astype(BF16)
    tile = jnp.concatenate([high, low, jnp.zeros((ROWS - 32, LANES), BF16)], 0)
    own = jnp.concatenate([w_up[0], w_qkv[0], w_out[0]] + folded + [tile], 1)
    tail = own[:, TAIL0:]
    quarter = lax.dynamic_slice(own, (0, replica * QUARTER), (ROWS, QUARTER))

    same = jnp.stack([shift(quarter, step) for step in (1, 2, 3)])
    across = [flip(same, bits) for bits in (1, 2, 3)]
    tails = [shift(tail, step) for step in (1, 2, 3)]
    mine = [own] + tails + [same] + across
    other = [swap(member) for member in mine]

    (out_one, out_two, grad_one, keep1, send1, kept, vectors, *acts) = run_main(
        mine, other, patches, cotangent, live_slots, wide
    )

    def reduce_plane(keep, send):
        same, x, y, d = pair_sum(keep, swap(send))
        parts = [same, flip(x, 1), flip(y, 2), flip(d, 3)]
        chunks = plane_sum(parts)
        return [chunks[0]] + [shift(chunks[step], step) for step in (1, 2, 3)]

    one = reduce_plane(keep1, send1)
    grad_zero, keep0, send0 = run_last(kept, vectors, grad_one, patches, acts, wide)
    zero = reduce_plane(keep0, send0)
    half_mine, half_other = column_sum(zero, one)
    halves = [half_mine, swap(half_other)]
    pieces = list(halves)
    for bits in (1, 2, 3):
        pieces += [flip(member, bits) for member in halves]
    grad_qkv, grad_out, grad_up, grad_down, *rest = unpack(pieces, width, wide)

    first = section == 0
    out_send = jnp.where(first, out_two, out_one)
    out_recv = swap(out_send)
    layer_outputs = jnp.stack(
        [jnp.where(first, out_one, out_recv), jnp.where(first, out_recv, out_two)]
    )[None]
    grad_one32 = grad_one.astype(F32)
    grad_recv = swap(jnp.where(first, grad_one32, grad_zero))
    input_grads = jnp.stack(
        [jnp.where(first, grad_zero, grad_recv), jnp.where(first, grad_recv, grad_one32)]
    )[None]
    (g_q, g_v, g_o, g_d, g_g1, g_o1, g_g2, g_o2, g_up) = rest
    return (
        layer_outputs,
        input_grads,
        grad_qkv,
        grad_out,
        grad_up,
        grad_down,
        g_q,
        g_v,
        g_o,
        g_up,
        g_d,
        g_g1,
        g_o1,
        g_g2,
        g_o2,
    )


class PlainPut:
    def __init__(self, outs, layer):
        self.outs, self.layer = outs, layer

    def w_qkv(self, value):
        self.outs[0][self.layer] = value

    def w_out(self, value):
        self.outs[1][self.layer] = value

    def w_up(self, lo, value):
        self.outs[2][self.layer, :, lo : lo + value.shape[1]] = value

    def w_down(self, lo, value):
        self.outs[3][self.layer, lo : lo + value.shape[0]] = value

    def vectors(self, sums, bias_up):
        self.outs[4][self.layer] = sums
        self.outs[5][self.layer] = bias_up


def plain_kernel(seq, *refs):
    patches, cotangent, live, w_qkv, w_out, w_up, w_down, vectors, biases = refs[:9]
    out_rows, grad_rows = refs[9:11]
    grads = refs[11:17]
    rows_in, rows_mid, up_grad, qkv_grad = refs[17:21]
    acts = (refs[21:27], refs[27:33])
    section = lax.axis_index("section")
    width = rows_in.shape[1]

    def weights_of(layer):
        return (
            lambda: w_qkv[layer],
            lambda: w_out[layer],
            lambda lo, step: w_up[layer, :, lo : lo + step],
            lambda lo, step: w_down[layer, lo : lo + step],
        )

    vec_of = lambda layer: lambda index: vectors[layer, index : index + 1]
    bias_of = lambda layer: lambda lo, step: biases[layer, :, lo : lo + step]
    live_rows = lax.broadcasted_iota(jnp.int32, (SEQ_ROWS, width), 0) < seq
    rows_in[seq - seq % 8 :] = jnp.zeros((SEQ_ROWS - seq + seq % 8, width), F32)
    rows_in[:seq] = patches[section].astype(F32)
    result = layer_forward(rows_in[...], seq, weights_of(0), vec_of(0), bias_of(0), acts[0])
    out_rows[0] = result[:seq].astype(BF16)
    rows_mid[...] = jnp.where(live_rows, result.astype(BF16).astype(F32), 0.0)
    result = layer_forward(rows_mid[...], seq, weights_of(1), vec_of(1), bias_of(1), acts[1])
    out_rows[1] = result[:seq].astype(BF16)
    seed = cotangent[section].astype(F32) * live[section].astype(F32)
    blank = jnp.zeros((SEQ_ROWS - seq, width), F32)
    grad_x = layer_backward(
        jnp.concatenate([seed, blank], 0),
        rows_mid[...],
        weights_of(1),
        vec_of(1),
        acts[1],
        up_grad,
        qkv_grad,
        PlainPut(grads, 1),
    )
    grad_x = grad_x.astype(BF16).astype(F32)
    grad_rows[1] = grad_x[:seq]
    grad_x = layer_backward(
        grad_x,
        rows_in[...],
        weights_of(0),
        vec_of(0),
        acts[0],
        up_grad,
        qkv_grad,
        PlainPut(grads, 0),
    )
    grad_rows[0] = grad_x[:seq]


def plain_local(patches, live_slots, cotangent, w_qkv, w_out, w_up, w_down, *small):
    bias_q, bias_v, bias_out, bias_up, bias_down, gain_one, offset_one, gain_two, offset_two = small
    seq, width = patches.shape[1:]
    wide = w_up.shape[2]

    def whole(value):
        along = lax.all_gather(value, "shard", axis=1, tiled=True)
        return lax.all_gather(along, "section", axis=0, tiled=True)

    small = (bias_q, bias_v, bias_out, bias_down, gain_one, offset_one, gain_two, offset_two)
    vectors = whole(jnp.stack(small, 2)).transpose(0, 2, 1)
    biases = whole(bias_up)[:, None]
    acts = act_shapes(width, wide)
    out_rows, grad_rows, *grads = pl.pallas_call(
        functools.partial(plain_kernel, seq),
        out_shape=[
            shape((2, seq, width), BF16),
            shape((2, seq, width), F32),
            shape((2, width, 3 * width), F32),
            shape((2, width, width), F32),
            shape((2, width, wide), F32),
            shape((2, wide, width), F32),
            shape((2, 8, width), F32),
            shape((2, 1, wide), F32),
        ],
        in_specs=vmem(2) + [pl.BlockSpec(memory_space=pltpu.SMEM)] + vmem(6),
        out_specs=vmem(8),
        scratch_shapes=[
            pltpu.VMEM((SEQ_ROWS, width), F32),
            pltpu.VMEM((SEQ_ROWS, width), F32),
            pltpu.VMEM((SEQ_ROWS, wide), BF16),
            pltpu.VMEM((SEQ_ROWS, 3 * width), BF16),
        ]
        + [pltpu.VMEM(*a) for a in acts + acts],
        compiler_params=PARAMS,
        name="both_layers",
    )(patches, cotangent, live_slots, *(whole(w) for w in (w_qkv, w_out, w_up, w_down)), vectors, biases)

    def owned(value):
        mine = lax.psum_scatter(value, "section", scatter_dimension=0, tiled=True)
        mine = lax.psum_scatter(mine.astype(BF16), "shard", scatter_dimension=1, tiled=True)
        return lax.psum(mine, "replica").astype(F32)

    grads = [owned(value) for value in grads[:4]] + [
        owned(grads[4].transpose(0, 2, 1)),
        owned(grads[5][:, 0]),
    ]
    q, v, out, down, g1, o1, g2, o2 = (grads[4][..., index] for index in range(8))

    def by_section(value):
        section = lax.axis_index("section")
        recv = swap(jnp.where(section == 0, value[1], value[0]))
        first = jnp.where(section == 0, value[0], recv)
        return jnp.stack([first, jnp.where(section == 0, recv, value[1])])[None]

    return (
        by_section(out_rows),
        by_section(grad_rows),
        *grads[:4],
        q,
        v,
        out,
        grads[5],
        down,
        g1,
        o1,
        g2,
        o2,
    )


def solution(mesh):
    slots = P(("shard", "replica"), None, None)
    matrix, vector = P("section", "shard", None), P("section", "shard")
    outs = P("section", ("shard", "replica"), None, None)
    packed = mesh.shape["shard"] == 4 and mesh.shape["replica"] == 4
    return jax.shard_map(
        packed_local if packed else plain_local,
        mesh=mesh,
        in_specs=(slots, P(("shard", "replica")), slots) + (matrix,) * 4 + (vector,) * 9,
        out_specs=(outs, outs) + (matrix,) * 4 + (vector,) * 9,
        check_vma=False,
    )
```

time: 1080 us -> 181 us (0.17); the launches traced: 1070 us -> 180 us
  waiting for transfers between devices: 767 us -> 90.1 us
  blocking collectives: 78.2 us -> 0 us
  matrix products: 70.7 us -> 0 us
  local copies, waits for them, and re-layouts: 81.1 us -> 12 us
  other arithmetic: 43.4 us -> 1.25 us
  starting transfers between devices: 7.96 us -> 43.3 us
  Pallas kernels: 0 us -> 32.3 us
  between operations: 17.5 us -> 1.14 us
    unnamed x69 -> x0, waiting for transfers between devices: 402 us -> none
    reduce_scatter x12 -> x0, waiting for transfers between devices: 314 us -> none  [the longest x3 88.8 us: local(): lax.psum_scatter(expanded[2].astype(jnp.bfloat16), 'shard', scatter_dimen...]
    ppermute x4 -> x40, waiting for transfers between devices: 14.2 us -> 90.1 us  [the longest x15 53.2 us: flip(): lax.ppermute(value, 'replica', [(place, place ^ bits) for place in range(...]
    dot_general x57 -> x0, matrix products: 70.7 us -> none  [the longest x12 20 us: project(): jnp.einsum('bsi,ij->bsj', rows, matrix, preferred_element_type=jnp.float32)]
    all_gather x3 -> x0, blocking collectives: 54 us -> none  [the longest x1 25.3 us: fetch_weights(): lax.all_gather(w_qkv, 'shard', axis=1, tiled=True)]
    unnamed x330 -> x43, local copies, waits for them, and re-layouts: 53.4 us -> 10.1 us
    ppermute x4 -> x40, starting transfers between devices: 5.46 us -> 43.3 us  [the longest x12 23.4 us: shift(): lax.ppermute(value, 'shard', [(place, (place + steps) % 4) for place in r...]
    psum x1 -> x0, waiting for transfers between devices: 37.8 us -> none  [local(): lax.psum(owned_sum[0].astype(jnp.bfloat16), 'replica').astype(jnp.float32)]
  transfers between devices with their start and end apart: 46 -> 40, of which waited for: 38 -> 21; matrix products, arithmetic and copies ran while one was open for 13% -> 3% of each run, Pallas kernels for 0% -> 3%
where the time goes in v1:
time: 181 us; the launch traced here: 180 us
  waiting for transfers between devices  90.1 us (50%)
  starting transfers between devices  43.3 us (24%)
  Pallas kernels  32.3 us (18%)
  local copies, waits for them, and re-layouts  12 us (7%)
    ppermute x15, waiting for transfers between devices, flip(): lax.ppermute(value, 'replica', [(place, place ^ bits) for place in range(...  53.2 us
    ppermute x12, waiting for transfers between devices, shift(): lax.ppermute(value, 'shard', [(place, (place + steps) % 4) for place in r...  28.7 us
    ppermute x12, starting transfers between devices, shift(): lax.ppermute(value, 'shard', [(place, (place + steps) % 4) for place in r...  23.4 us
    ppermute x15, starting transfers between devices, flip(): lax.ppermute(value, 'replica', [(place, place ^ bits) for place in range(...  17.2 us
    pallas_call x1, Pallas kernels, run_main(): pl.pallas_call(functools.partial(main_kernel, seq), out_shape=[shape((seq...  16.3 us
    unnamed x43, local copies, waits for them, and re-layouts  10.1 us
    pallas_call x1, Pallas kernels, run_last(): pl.pallas_call(functools.partial(last_kernel, seq), out_shape=[shape((seq...  8.66 us
    ppermute x13, waiting for transfers between devices, swap(): return lax.ppermute(value, 'section', [(0, 1), (1, 0)])  8.16 us
  transfers between devices with their start and end apart: 40, of which 21 were waited for; matrix products, arithmetic and copies ran while one was open for 3% of the time, Pallas kernels for 3%

profile of v1, /device:TPU:0, one launch (start us, length us, event | category | flops | bytes accessed | tf_op | source)
XLA Modules:
  0.0 180.2 jit_solution(12227066660639119701)
XLA Ops:
  3.5 4.1 %collective-permute-start.1 = (bf16[96,1152]{1,0:T(8,128)(2,1)S(1)}, bf16[96,1152]{1,0:T(8,128)(2,1)S(1)}, u32[]{:S(2)}, u32[]{:S(2)}) collective-permute-start(bf16[96,1152]{1,0:T(8,128)(2,1)S(1)} %fusion.1), channel_id=1, source_target_pairs={{0,8},{4,12},{8,0},{12,4},{1,9},{5,13},{9,1},{13,5},{2,10},{6,14},... | collective-permute-start | bytes 663560 | tf_op jit(solution)/shard_map/ppermute | solution.py:658
  11.1 1.7 collective-permute-start.4
  12.8 1.8 collective-permute-start
  14.6 4.1 %collective-permute-done.5 = bf16[96,896]{1,0:T(8,128)(2,1)S(1)} collective-permute-done((bf16[96,896]{1,0:T(8,128)(2,1)S(1)}, bf16[96,896]{1,0:T(8,128)(2,1)S(1)}, u32[]{:S(2)}, u32[]{:S(2)}) %collective-permute-start.5) | collective-permute-done | bytes 172064 | tf_op jit(solution)/shard_map/ppermute | solution.py:658
  18.7 2.8 %collective-permute-start.2 = (bf16[96,1152]{1,0:T(8,128)(2,1)S(1)}, bf16[96,1152]{1,0:T(8,128)(2,1)S(1)}, u32[]{:S(2)}, u32[]{:S(2)}) collective-permute-start(bf16[96,1152]{1,0:T(8,128)(2,1)S(1)} %fusion.1), channel_id=1, source_target_pairs={{0,12},{4,0},{8,4},{12,8},{1,13},{5,1},{9,5},{13,9},{2,14},{6,2},{... | collective-permute-start | bytes 663560 | tf_op jit(solution)/shard_map/ppermute | solution.py:658
  21.5 9.2 %collective-permute-done.1.refs_2_ = bf16[96,1152]{1,0:T(8,128)(2,1)S(1)} collective-permute-done((bf16[96,1152]{1,0:T(8,128)(2,1)S(1)}, bf16[96,1152]{1,0:T(8,128)(2,1)S(1)}, u32[]{:S(2)}, u32[]{:S(2)}) %collective-permute-start.1) | collective-permute-done | bytes 221216 | tf_op jit(solution)/shard_map/ppermute | solution.py:658
  30.7 7.4 %collective-permute-done.4 = bf16[96,896]{1,0:T(8,128)(2,1)S(1)} collective-permute-done((bf16[96,896]{1,0:T(8,128)(2,1)S(1)}, bf16[96,896]{1,0:T(8,128)(2,1)S(1)}, u32[]{:S(2)}, u32[]{:S(2)}) %collective-permute-start.4) | collective-permute-done | bytes 172064 | tf_op jit(solution)/shard_map/ppermute | solution.py:658
  38.2 2.9 %collective-permute-start.8 = (bf16[3,96,896]{2,1,0:T(8,128)(2,1)S(1)}, bf16[3,96,896]{2,1,0:T(8,128)(2,1)S(1)}, u32[]{:S(2)}, u32[]{:S(2)}) collective-permute-start(bf16[3,96,896]{2,1,0:T(8,128)(2,1)S(1)} %pad_maximum_fusion.refs_4_), channel_id=1, source_target_pairs={{0,3},{1,2},{2,1},{3,0},{4,7},{5,6},{6,5},{7,4},{8,11},{9,10},{10,... | collective-permute-start | bytes 1548296 | tf_op jit(solution)/shard_map/ppermute | solution.py:654
  43.6 1.5 collective-permute-done.12.refs_11_
  45.2 8.7 %collective-permute-done.8.refs_7_ = bf16[3,96,896]{2,1,0:T(8,128)(2,1)S(1)} collective-permute-done((bf16[3,96,896]{2,1,0:T(8,128)(2,1)S(1)}, bf16[3,96,896]{2,1,0:T(8,128)(2,1)S(1)}, u32[]{:S(2)}, u32[]{:S(2)}) %collective-permute-start.8) | collective-permute-done | bytes 516128 | tf_op jit(solution)/shard_map/ppermute | solution.py:654
  53.9 8.4 %collective-permute-done.7.refs_6_ = bf16[3,96,896]{2,1,0:T(8,128)(2,1)S(1)} collective-permute-done((bf16[3,96,896]{2,1,0:T(8,128)(2,1)S(1)}, bf16[3,96,896]{2,1,0:T(8,128)(2,1)S(1)}, u32[]{:S(2)}, u32[]{:S(2)}) %collective-permute-start.7) | collective-permute-done | bytes 516128 | tf_op jit(solution)/shard_map/ppermute | solution.py:654
  65.8 16.3 %forward_and_layer_one.1 = (bf16[197,384]{1,0:T(8,128)(2,1)S(1)}, bf16[197,384]{1,0:T(8,128)(2,1)S(1)}, bf16[197,384]{1,0:T(8,128)(2,1)S(1)}, bf16[4,4,48,1280]{...) custom-call(bf16[96,4736]{1,0:T(8,128)(2,1)} %copy-done.7, ...), custom_call_target="tpu_custom_call" | custom-call | tf_op jit(solution)/shard_map/forward_and_layer_one/pallas_call | solution.py:459
  85.4 8.7 %layer_zero_backward.1 = (f32[197,384]{1,0:T(8,128)S(1)}, bf16[4,4,48,1280]{3,2,1,0:T(8,128)(2,1)S(1)}, bf16[4,4,48,1280]{3,2,1,0:T(8,128)(2,1)}) custom-call(bf16[1,4,96,4736]{3,2,1,0:T(8,128)(2,1)} %get-tuple-element.64.refs_0_, f32[8,384]{1,0:T(8,128)S(1)} %get-tuple-element.65.refs_1_, bf16[197,384]{1,0:T(8,128)(2,1)S(1)} %get-tuple-element.66.refs_2_, ...), custom_call_target="tpu_custom_call" | custom-call | tf_op jit(solution)/shard_map/layer_zero_backward/pallas_call | solution.py:496
  95.3 3.7 %collective-permute-done.19.recv = bf16[4,4,48,1280]{3,2,1,0:T(8,128)(2,1)S(1)} collective-permute-done((bf16[4,4,48,1280]{3,2,1,0:T(8,128)(2,1)}, bf16[4,4,48,1280]{3,2,1,0:T(8,128)(2,1)S(1)}, u32[]{:S(2)}, u32[]{:S(2)}) %collective-permute-start.19) | collective-permute-done | bytes 1966112 | tf_op jit(solution)/shard_map/ppermute | solution.py:650
  107.5 6.9 %collective-permute-done.20.b = bf16[4,48,1280]{2,1,0:T(8,128)(2,1)S(1)} collective-permute-done((bf16[4,48,1280]{2,1,0:T(8,128)(2,1)S(1)}, bf16[4,48,1280]{2,1,0:T(8,128)(2,1)S(1)}, u32[]{:S(2)}, u32[]{:S(2)}) %collective-permute-start.20) | collective-permute-done | bytes 491552 | tf_op jit(solution)/shard_map/ppermute | solution.py:654
  115.2 1.7 collective-permute-start.29
  117.0 9.6 %collective-permute-done.21.c = bf16[4,48,1280]{2,1,0:T(8,128)(2,1)} collective-permute-done((bf16[4,48,1280]{2,1,0:T(8,128)(2,1)}, bf16[4,48,1280]{2,1,0:T(8,128)(2,1)}, u32[]{:S(2)}, u32[]{:S(2)}) %collective-permute-start.21) | collective-permute-done | bytes 491552 | tf_op jit(solution)/shard_map/ppermute | solution.py:654
  129.0 1.7 collective-permute-start.23
  130.7 4.8 %collective-permute-done.27.b = bf16[4,48,1280]{2,1,0:T(8,128)(2,1)S(1)} collective-permute-done((bf16[4,48,1280]{2,1,0:T(8,128)(2,1)}, bf16[4,48,1280]{2,1,0:T(8,128)(2,1)S(1)}, u32[]{:S(2)}, u32[]{:S(2)}) %collective-permute-start.27) | collective-permute-done | bytes 491552 | tf_op jit(solution)/shard_map/ppermute | solution.py:654
  135.5 3.3 %collective-permute-start.24 = (bf16[48,1280]{1,0:T(8,128)(2,1)S(1)}, bf16[48,1280]{1,0:T(8,128)(2,1)S(1)}, u32[]{:S(2)}, u32[]{:S(2)}) collective-permute-start(bf16[48,1280]{1,0:T(8,128)(2,1)S(1)} %get-tuple-element.82), channel_id=1, source_target_pairs={{0,8},{4,12},{8,0},{12,4},{1,9},{5,13},{9,1},{13,5},{2,10},{6,14},... | collective-permute-start | bytes 368648 | tf_op jit(solution)/shard_map/ppermute | solution.py:658
  138.9 7.7 %collective-permute-done.28.c = bf16[4,48,1280]{2,1,0:T(8,128)(2,1)S(1)} collective-permute-done((bf16[4,48,1280]{2,1,0:T(8,128)(2,1)}, bf16[4,48,1280]{2,1,0:T(8,128)(2,1)S(1)}, u32[]{:S(2)}, u32[]{:S(2)}) %collective-permute-start.28) | collective-permute-done | bytes 491552 | tf_op jit(solution)/shard_map/ppermute | solution.py:654
  146.9 2.1 %collective-permute-start.30 = (bf16[48,1280]{1,0:T(8,128)(2,1)S(1)}, bf16[48,1280]{1,0:T(8,128)(2,1)S(1)}, u32[]{:S(2)}, u32[]{:S(2)}) collective-permute-start(bf16[48,1280]{1,0:T(8,128)(2,1)S(1)} %get-tuple-element.91), channel_id=1, source_target_pairs={{0,4},{4,8},{8,12},{12,0},{1,5},{5,9},{9,13},{13,1},{2,6},{6,10},{... | collective-permute-start | bytes 368648 | tf_op jit(solution)/shard_map/ppermute | solution.py:658
  149.0 3.6 %collective-permute-start.31 = (bf16[48,1280]{1,0:T(8,128)(2,1)S(1)}, bf16[48,1280]{1,0:T(8,128)(2,1)S(1)}, u32[]{:S(2)}, u32[]{:S(2)}) collective-permute-start(bf16[48,1280]{1,0:T(8,128)(2,1)S(1)} %get-tuple-element.92), channel_id=1, source_target_pairs={{0,8},{4,12},{8,0},{12,4},{1,9},{5,13},{9,1},{13,5},{2,10},{6,14},... | collective-permute-start | bytes 368648 | tf_op jit(solution)/shard_map/ppermute | solution.py:658
  154.6 4.0 %collective-permute-done.30.refs_5_ = bf16[48,1280]{1,0:T(8,128)(2,1)S(1)} collective-permute-done((bf16[48,1280]{1,0:T(8,128)(2,1)S(1)}, bf16[48,1280]{1,0:T(8,128)(2,1)S(1)}, u32[]{:S(2)}, u32[]{:S(2)}) %collective-permute-start.30) | collective-permute-done | bytes 122912 | tf_op jit(solution)/shard_map/ppermute | solution.py:658
  158.6 3.8 %collective-permute-done.31.refs_6_ = bf16[48,1280]{1,0:T(8,128)(2,1)S(1)} collective-permute-done((bf16[48,1280]{1,0:T(8,128)(2,1)S(1)}, bf16[48,1280]{1,0:T(8,128)(2,1)S(1)}, u32[]{:S(2)}, u32[]{:S(2)}) %collective-permute-start.31) | collective-permute-done | bytes 122912 | tf_op jit(solution)/shard_map/ppermute | solution.py:658
  162.7 1.5 collective-permute-start.38
  164.9 1.5 collective-permute-start.34
  166.4 1.5 collective-permute-start.39
  168.4 1.4 collective-permute-done.38.refs_6_
  172.5 2.6 %collective-permute-done.39.refs_7_ = bf16[48,1280]{1,0:T(8,128)(2,1)S(1)} collective-permute-done((bf16[48,1280]{1,0:T(8,128)(2,1)S(1)}, bf16[48,1280]{1,0:T(8,128)(2,1)S(1)}, u32[]{:S(2)}, u32[]{:S(2)}) %collective-permute-start.39) | collective-permute-done | bytes 122912 | tf_op jit(solution)/shard_map/ppermute | solution.py:654
  175.1 2.1 %collective-permute-done.37.refs_5_ = bf16[48,1280]{1,0:T(8,128)(2,1)S(1)} collective-permute-done((bf16[48,1280]{1,0:T(8,128)(2,1)S(1)}, bf16[48,1280]{1,0:T(8,128)(2,1)S(1)}, u32[]{:S(2)}, u32[]{:S(2)}) %collective-permute-start.37) | collective-permute-done | bytes 122912 | tf_op jit(solution)/shard_map/ppermute | solution.py:654
  177.2 2.8 %unpack.1 = (f32[1,96,1152]{2,1,0:T(8,128)}, f32[1,96,384]{2,1,0:T(8,128)}, f32[1,96,1536]{2,1,0:T(8,128)}, f32[1,384,384]{2,1,0:T(8,128)}, f32[1,96]{1,0:T(1,12...) custom-call(bf16[48,1280]{1,0:T(8,128)(2,1)S(1)} %get-tuple-element., ...), custom_call_target="tpu_custom_call" | custom-call | tf_op jit(solution)/shard_map/unpack/pallas_call | solution.py:628
  (117 shorter events, 35.0 us)
Async XLA Ops:
  3.5 27.3 %collective-permute-start.1 = (bf16[96,1152]{1,0:T(8,128)(2,1)S(1)}, bf16[96,1152]{1,0:T(8,128)(2,1)S(1)}, u32[]{:S(2)}, u32[]{:S(2)}) collective-permute-start(bf16[96,1152]{1,0:T(8,128)(2,1)S(1)} %fusion.1), channel_id=1, source_target_pairs={{0,8},{4,12},{8,0},{12,4},{1,9},{5,13},{9,1},{13,5},{2,10},{6,14},... | collective-permute-start | bytes 663560 | tf_op jit(solution)/shard_map/ppermute | solution.py:658
  9.7 9.0 %collective-permute-start.5 = (bf16[96,896]{1,0:T(8,128)(2,1)S(1)}, bf16[96,896]{1,0:T(8,128)(2,1)S(1)}, u32[]{:S(2)}, u32[]{:S(2)}) collective-permute-start(bf16[96,896]{1,0:T(8,128)(2,1)S(1)} %constant_dynamic-slice_fusion), channel_id=1, source_target_pairs={{0,12},{4,0},{8,4},{12,8},{1,13},{5,1},{9,5},{13,9},{2,14},{6,2},{... | collective-permute-start | bytes 516104 | tf_op jit(solution)/shard_map/ppermute | solution.py:658
  11.1 27.0 %collective-permute-start.4 = (bf16[96,896]{1,0:T(8,128)(2,1)S(1)}, bf16[96,896]{1,0:T(8,128)(2,1)S(1)}, u32[]{:S(2)}, u32[]{:S(2)}) collective-permute-start(bf16[96,896]{1,0:T(8,128)(2,1)S(1)} %constant_dynamic-slice_fusion), channel_id=1, source_target_pairs={{0,8},{4,12},{8,0},{12,4},{1,9},{5,13},{9,1},{13,5},{2,10},{6,14},... | collective-permute-start | bytes 516104 | tf_op jit(solution)/shard_map/ppermute | solution.py:658
  12.8 25.3 %collective-permute-start.3 = (bf16[96,896]{1,0:T(8,128)(2,1)S(1)}, bf16[96,896]{1,0:T(8,128)(2,1)S(1)}, u32[]{:S(2)}, u32[]{:S(2)}) collective-permute-start(bf16[96,896]{1,0:T(8,128)(2,1)S(1)} %constant_dynamic-slice_fusion), channel_id=1, source_target_pairs={{0,4},{4,8},{8,12},{12,0},{1,5},{5,9},{9,13},{13,1},{2,6},{6,10},{... | collective-permute-start | bytes 516104 | tf_op jit(solution)/shard_map/ppermute | solution.py:658
  12.8 28.8 %collective-permute-start = (bf16[96,1152]{1,0:T(8,128)(2,1)S(1)}, bf16[96,1152]{1,0:T(8,128)(2,1)S(1)}, u32[]{:S(2)}, u32[]{:S(2)}) collective-permute-start(bf16[96,1152]{1,0:T(8,128)(2,1)S(1)} %fusion.1), channel_id=1, source_target_pairs={{0,4},{4,8},{8,12},{12,0},{1,5},{5,9},{9,13},{13,1},{2,6},{6,10},{... | collective-permute-start | bytes 663560 | tf_op jit(solution)/shard_map/ppermute | solution.py:658
  18.7 23.2 %collective-permute-start.2 = (bf16[96,1152]{1,0:T(8,128)(2,1)S(1)}, bf16[96,1152]{1,0:T(8,128)(2,1)S(1)}, u32[]{:S(2)}, u32[]{:S(2)}) collective-permute-start(bf16[96,1152]{1,0:T(8,128)(2,1)S(1)} %fusion.1), channel_id=1, source_target_pairs={{0,12},{4,0},{8,4},{12,8},{1,13},{5,1},{9,5},{13,9},{2,14},{6,2},{... | collective-permute-start | bytes 663560 | tf_op jit(solution)/shard_map/ppermute | solution.py:658
  30.7 11.2 %collective-permute-start.11 = (bf16[96,1152]{1,0:T(8,128)(2,1)S(1)}, bf16[96,1152]{1,0:T(8,128)(2,1)S(1)}, u32[]{:S(2)}, u32[]{:S(2)}) collective-permute-start(bf16[96,1152]{1,0:T(8,128)(2,1)S(1)} %collective-permute-done.1.refs_2_), channel_id=1, source_target_pairs={{0,16},{16,0},{1,17},{17,1},{2,18},{18,2},{3,19},{19,3},{4,20},{20... | collective-permute-start | bytes 663560 | tf_op jit(solution)/shard_map/ppermute | solution.py:650
  38.2 15.7 %collective-permute-start.8 = (bf16[3,96,896]{2,1,0:T(8,128)(2,1)S(1)}, bf16[3,96,896]{2,1,0:T(8,128)(2,1)S(1)}, u32[]{:S(2)}, u32[]{:S(2)}) collective-permute-start(bf16[3,96,896]{2,1,0:T(8,128)(2,1)S(1)} %pad_maximum_fusion.refs_4_), channel_id=1, source_target_pairs={{0,3},{1,2},{2,1},{3,0},{4,7},{5,6},{6,5},{7,4},{8,11},{9,10},{10,... | collective-permute-start | bytes 1548296 | tf_op jit(solution)/shard_map/ppermute | solution.py:654
  41.1 21.3 %collective-permute-start.7 = (bf16[3,96,896]{2,1,0:T(8,128)(2,1)S(1)}, bf16[3,96,896]{2,1,0:T(8,128)(2,1)S(1)}, u32[]{:S(2)}, u32[]{:S(2)}) collective-permute-start(bf16[3,96,896]{2,1,0:T(8,128)(2,1)S(1)} %pad_maximum_fusion.refs_4_), channel_id=1, source_target_pairs={{0,2},{1,3},{2,0},{3,1},{4,6},{5,7},{6,4},{7,5},{8,10},{9,11},{10,... | collective-permute-start | bytes 1548296 | tf_op jit(solution)/shard_map/ppermute | solution.py:654
  41.6 20.8 %collective-permute-start.6 = (bf16[3,96,896]{2,1,0:T(8,128)(2,1)S(1)}, bf16[3,96,896]{2,1,0:T(8,128)(2,1)S(1)}, u32[]{:S(2)}, u32[]{:S(2)}) collective-permute-start(bf16[3,96,896]{2,1,0:T(8,128)(2,1)S(1)} %pad_maximum_fusion.refs_4_), channel_id=1, source_target_pairs={{0,1},{1,0},{2,3},{3,2},{4,5},{5,4},{6,7},{7,6},{8,9},{9,8},{10,11... | collective-permute-start | bytes 1548296 | tf_op jit(solution)/shard_map/ppermute | solution.py:654
  42.0 21.0 %collective-permute-start.9 = (bf16[96,4736]{1,0:T(8,128)(2,1)S(1)}, bf16[96,4736]{1,0:T(8,128)(2,1)S(1)}, u32[]{:S(2)}, u32[]{:S(2)}) collective-permute-start(bf16[96,4736]{1,0:T(8,128)(2,1)S(1)} %maximum_dynamic-update-slice_fusion.refs_0_), channel_id=1, source_target_pairs={{0,16},{16,0},{1,17},{17,1},{2,18},{18,2},{3,19},{19,3},{4,20},{20... | collective-permute-start | bytes 2727944 | tf_op jit(solution)/shard_map/ppermute | solution.py:650
  45.0 17.9 %collective-permute-start.13 = (bf16[3,96,896]{2,1,0:T(8,128)(2,1)S(1)}, bf16[3,96,896]{2,1,0:T(8,128)(2,1)S(1)}, u32[]{:S(2)}, u32[]{:S(2)}) collective-permute-start(bf16[3,96,896]{2,1,0:T(8,128)(2,1)S(1)} %pad_maximum_fusion.refs_4_), channel_id=1, source_target_pairs={{0,16},{16,0},{1,17},{17,1},{2,18},{18,2},{3,19},{19,3},{4,20},{20... | collective-permute-start | bytes 1548296 | tf_op jit(solution)/shard_map/ppermute | solution.py:650
  53.9 9.1 %collective-permute-start.16 = (bf16[3,96,896]{2,1,0:T(8,128)(2,1)S(1)}, bf16[3,96,896]{2,1,0:T(8,128)(2,1)S(1)}, u32[]{:S(2)}, u32[]{:S(2)}) collective-permute-start(bf16[3,96,896]{2,1,0:T(8,128)(2,1)S(1)} %collective-permute-done.8.refs_7_), channel_id=1, source_target_pairs={{0,16},{16,0},{1,17},{17,1},{2,18},{18,2},{3,19},{19,3},{4,20},{20... | collective-permute-start | bytes 1548296 | tf_op jit(solution)/shard_map/ppermute | solution.py:650
  95.2 8.6 %collective-permute-start.26 = (bf16[4,4,48,1280]{3,2,1,0:T(8,128)(2,1)}, bf16[4,4,48,1280]{3,2,1,0:T(8,128)(2,1)S(1)}, u32[]{:S(2)}, u32[]{:S(2)}) collective-permute-start(bf16[4,4,48,1280]{3,2,1,0:T(8,128)(2,1)} %get-tuple-element.85), channel_id=1, source_target_pairs={{0,16},{16,0},{1,17},{17,1},{2,18},{18,2},{3,19},{19,3},{4,20},{20... | collective-permute-start | bytes 5898248 | tf_op jit(solution)/shard_map/ppermute | solution.py:650
  100.4 14.1 %collective-permute-start.20 = (bf16[4,48,1280]{2,1,0:T(8,128)(2,1)S(1)}, bf16[4,48,1280]{2,1,0:T(8,128)(2,1)S(1)}, u32[]{:S(2)}, u32[]{:S(2)}) collective-permute-start(bf16[4,48,1280]{2,1,0:T(8,128)(2,1)S(1)} %get-tuple-element.77), channel_id=1, source_target_pairs={{0,1},{1,0},{2,3},{3,2},{4,5},{5,4},{6,7},{7,6},{8,9},{9,8},{10,11... | collective-permute-start | bytes 1474568 | tf_op jit(solution)/shard_map/ppermute | solution.py:654
  101.6 24.9 %collective-permute-start.21 = (bf16[4,48,1280]{2,1,0:T(8,128)(2,1)}, bf16[4,48,1280]{2,1,0:T(8,128)(2,1)}, u32[]{:S(2)}, u32[]{:S(2)}) collective-permute-start(bf16[4,48,1280]{2,1,0:T(8,128)(2,1)} %get-tuple-element.78), channel_id=1, source_target_pairs={{0,2},{1,3},{2,0},{3,1},{4,6},{5,7},{6,4},{7,5},{8,10},{9,11},{10,... | collective-permute-start | bytes 1474568 | tf_op jit(solution)/shard_map/ppermute | solution.py:654
  102.7 23.9 %collective-permute-start.22 = (bf16[4,48,1280]{2,1,0:T(8,128)(2,1)}, bf16[4,48,1280]{2,1,0:T(8,128)(2,1)}, u32[]{:S(2)}, u32[]{:S(2)}) collective-permute-start(bf16[4,48,1280]{2,1,0:T(8,128)(2,1)} %get-tuple-element.79), channel_id=1, source_target_pairs={{0,3},{1,2},{2,1},{3,0},{4,7},{5,6},{6,5},{7,4},{8,11},{9,10},{10,... | collective-permute-start | bytes 1474568 | tf_op jit(solution)/shard_map/ppermute | solution.py:654
  105.3 30.3 %collective-permute-start.27 = (bf16[4,48,1280]{2,1,0:T(8,128)(2,1)}, bf16[4,48,1280]{2,1,0:T(8,128)(2,1)S(1)}, u32[]{:S(2)}, u32[]{:S(2)}) collective-permute-start(bf16[4,48,1280]{2,1,0:T(8,128)(2,1)} %get-tuple-element.87), channel_id=1, source_target_pairs={{0,1},{1,0},{2,3},{3,2},{4,5},{5,4},{6,7},{7,6},{8,9},{9,8},{10,11... | collective-permute-start | bytes 1474568 | tf_op jit(solution)/shard_map/ppermute | solution.py:654
  106.5 40.1 %collective-permute-start.28 = (bf16[4,48,1280]{2,1,0:T(8,128)(2,1)}, bf16[4,48,1280]{2,1,0:T(8,128)(2,1)S(1)}, u32[]{:S(2)}, u32[]{:S(2)}) collective-permute-start(bf16[4,48,1280]{2,1,0:T(8,128)(2,1)} %get-tuple-element.88), channel_id=1, source_target_pairs={{0,2},{1,3},{2,0},{3,1},{4,6},{5,7},{6,4},{7,5},{8,10},{9,11},{10,... | collective-permute-start | bytes 1474568 | tf_op jit(solution)/shard_map/ppermute | solution.py:654
  115.2 31.4 %collective-permute-start.29 = (bf16[4,48,1280]{2,1,0:T(8,128)(2,1)}, bf16[4,48,1280]{2,1,0:T(8,128)(2,1)S(1)}, u32[]{:S(2)}, u32[]{:S(2)}) collective-permute-start(bf16[4,48,1280]{2,1,0:T(8,128)(2,1)} %get-tuple-element.89), channel_id=1, source_target_pairs={{0,3},{1,2},{2,1},{3,0},{4,7},{5,6},{6,5},{7,4},{8,11},{9,10},{10,... | collective-permute-start | bytes 1474568 | tf_op jit(solution)/shard_map/ppermute | solution.py:654
  126.6 20.4 %collective-permute-start.17 = (bf16[197,384]{1,0:T(8,128)(2,1)S(1)}, bf16[197,384]{1,0:T(8,128)(2,1)S(1)}, u32[]{:S(2)}, u32[]{:S(2)}) collective-permute-start(bf16[197,384]{1,0:T(8,128)(2,1)S(1)} %broadcast_select_fusion), channel_id=1, source_target_pairs={{0,16},{16,0},{1,17},{17,1},{2,18},{18,2},{3,19},{19,3},{4,20},{20... | collective-permute-start | bytes 453896 | tf_op jit(solution)/shard_map/ppermute | solution.py:650
  129.0 20.0 %collective-permute-start.23 = (bf16[48,1280]{1,0:T(8,128)(2,1)S(1)}, bf16[48,1280]{1,0:T(8,128)(2,1)S(1)}, u32[]{:S(2)}, u32[]{:S(2)}) collective-permute-start(bf16[48,1280]{1,0:T(8,128)(2,1)S(1)} %get-tuple-element.81), channel_id=1, source_target_pairs={{0,4},{4,8},{8,12},{12,0},{1,5},{5,9},{9,13},{13,1},{2,6},{6,10},{... | collective-permute-start | bytes 368648 | tf_op jit(solution)/shard_map/ppermute | solution.py:658
  135.5 17.1 %collective-permute-start.24 = (bf16[48,1280]{1,0:T(8,128)(2,1)S(1)}, bf16[48,1280]{1,0:T(8,128)(2,1)S(1)}, u32[]{:S(2)}, u32[]{:S(2)}) collective-permute-start(bf16[48,1280]{1,0:T(8,128)(2,1)S(1)} %get-tuple-element.82), channel_id=1, source_target_pairs={{0,8},{4,12},{8,0},{12,4},{1,9},{5,13},{9,1},{13,5},{2,10},{6,14},... | collective-permute-start | bytes 368648 | tf_op jit(solution)/shard_map/ppermute | solution.py:658
  146.6 17.6 %collective-permute-start.18 = (f32[197,384]{1,0:T(8,128)S(1)}, f32[197,384]{1,0:T(8,128)S(1)}, u32[]{:S(2)}, u32[]{:S(2)}) collective-permute-start(f32[197,384]{1,0:T(8,128)S(1)} %convert_select_fusion.1), channel_id=1, source_target_pairs={{0,16},{16,0},{1,17},{17,1},{2,18},{18,2},{3,19},{19,3},{4,20},{20... | collective-permute-start | bytes 907784 | tf_op jit(solution)/shard_map/ppermute | solution.py:650
  146.7 7.9 %collective-permute-start.25 = (bf16[48,1280]{1,0:T(8,128)(2,1)S(1)}, bf16[48,1280]{1,0:T(8,128)(2,1)S(1)}, u32[]{:S(2)}, u32[]{:S(2)}) collective-permute-start(bf16[48,1280]{1,0:T(8,128)(2,1)S(1)} %get-tuple-element.83), channel_id=1, source_target_pairs={{0,12},{4,0},{8,4},{12,8},{1,13},{5,1},{9,5},{13,9},{2,14},{6,2},{... | collective-permute-start | bytes 368648 | tf_op jit(solution)/shard_map/ppermute | solution.py:658
  146.9 11.7 %collective-permute-start.30 = (bf16[48,1280]{1,0:T(8,128)(2,1)S(1)}, bf16[48,1280]{1,0:T(8,128)(2,1)S(1)}, u32[]{:S(2)}, u32[]{:S(2)}) collective-permute-start(bf16[48,1280]{1,0:T(8,128)(2,1)S(1)} %get-tuple-element.91), channel_id=1, source_target_pairs={{0,4},{4,8},{8,12},{12,0},{1,5},{5,9},{9,13},{13,1},{2,6},{6,10},{... | collective-permute-start | bytes 368648 | tf_op jit(solution)/shard_map/ppermute | solution.py:658
  149.0 13.4 %collective-permute-start.31 = (bf16[48,1280]{1,0:T(8,128)(2,1)S(1)}, bf16[48,1280]{1,0:T(8,128)(2,1)S(1)}, u32[]{:S(2)}, u32[]{:S(2)}) collective-permute-start(bf16[48,1280]{1,0:T(8,128)(2,1)S(1)} %get-tuple-element.92), channel_id=1, source_target_pairs={{0,8},{4,12},{8,0},{12,4},{1,9},{5,13},{9,1},{13,5},{2,10},{6,14},... | collective-permute-start | bytes 368648 | tf_op jit(solution)/shard_map/ppermute | solution.py:658
  152.6 9.8 %collective-permute-start.32 = (bf16[48,1280]{1,0:T(8,128)(2,1)S(1)}, bf16[48,1280]{1,0:T(8,128)(2,1)S(1)}, u32[]{:S(2)}, u32[]{:S(2)}) collective-permute-start(bf16[48,1280]{1,0:T(8,128)(2,1)S(1)} %get-tuple-element.93), channel_id=1, source_target_pairs={{0,12},{4,0},{8,4},{12,8},{1,13},{5,1},{9,5},{13,9},{2,14},{6,2},{... | collective-permute-start | bytes 368648 | tf_op jit(solution)/shard_map/ppermute | solution.py:658
  164.3 8.2 %collective-permute-start.36 = (bf16[48,1280]{1,0:T(8,128)(2,1)S(1)}, bf16[48,1280]{1,0:T(8,128)(2,1)S(1)}, u32[]{:S(2)}, u32[]{:S(2)}) collective-permute-start(bf16[48,1280]{1,0:T(8,128)(2,1)S(1)} %get-tuple-element.94.refs_0_), channel_id=1, source_target_pairs={{0,2},{1,3},{2,0},{3,1},{4,6},{5,7},{6,4},{7,5},{8,10},{9,11},{10,... | collective-permute-start | bytes 368648 | tf_op jit(solution)/shard_map/ppermute | solution.py:654
  164.9 7.6 %collective-permute-start.34 = (bf16[48,1280]{1,0:T(8,128)(2,1)S(1)}, bf16[48,1280]{1,0:T(8,128)(2,1)S(1)}, u32[]{:S(2)}, u32[]{:S(2)}) collective-permute-start(bf16[48,1280]{1,0:T(8,128)(2,1)S(1)} %get-tuple-element.94.refs_0_), channel_id=1, source_target_pairs={{0,1},{1,0},{2,3},{3,2},{4,5},{5,4},{6,7},{7,6},{8,9},{9,8},{10,11... | collective-permute-start | bytes 368648 | tf_op jit(solution)/shard_map/ppermute | solution.py:654
  166.4 8.7 %collective-permute-start.39 = (bf16[48,1280]{1,0:T(8,128)(2,1)S(1)}, bf16[48,1280]{1,0:T(8,128)(2,1)S(1)}, u32[]{:S(2)}, u32[]{:S(2)}) collective-permute-start(bf16[48,1280]{1,0:T(8,128)(2,1)S(1)} %collective-permute-done.33.refs_1_), channel_id=1, source_target_pairs={{0,3},{1,2},{2,1},{3,0},{4,7},{5,6},{6,5},{7,4},{8,11},{9,10},{10,... | collective-permute-start | bytes 368648 | tf_op jit(solution)/shard_map/ppermute | solution.py:654
  167.8 9.4 %collective-permute-start.37 = (bf16[48,1280]{1,0:T(8,128)(2,1)S(1)}, bf16[48,1280]{1,0:T(8,128)(2,1)S(1)}, u32[]{:S(2)}, u32[]{:S(2)}) collective-permute-start(bf16[48,1280]{1,0:T(8,128)(2,1)S(1)} %collective-permute-done.33.refs_1_), channel_id=1, source_target_pairs={{0,2},{1,3},{2,0},{3,1},{4,6},{5,7},{6,4},{7,5},{8,10},{9,11},{10,... | collective-permute-start | bytes 368648 | tf_op jit(solution)/shard_map/ppermute | solution.py:654
  (24 other events, 296.7 us)

commit v2 on v1

--- a/solution.py
+++ b/solution.py
@@ -14,7 +14,7 @@
 F32 = jnp.float32
 BF16 = jnp.bfloat16
 LANES = 128
-VMEM_LIMIT = 48 * 1024 * 1024
+MIB = 1024 * 1024
 
 BIAS_Q, BIAS_V, BIAS_OUT, BIAS_DOWN, GAIN_ONE, OFFSET_ONE, GAIN_TWO, OFFSET_TWO = range(8)
 
@@ -175,8 +175,8 @@
 ROWS = 96
 HALF = 48
 UP0, QKV0, OUT0, DOWN0, VEC0, PACKED = 0, 1536, 2688, 3072, 4608, 4736
-QUARTER = 896
-TAIL0, TAIL = 3584, 1152
+QUARTER = 1152
+PIECE_IN = QUARTER + LANES
 PIECE = 1280
 SEQ_ROWS = 208
 
@@ -276,19 +276,22 @@
 
 
 def start_copies(pieces, packed, layer, sems, shard, replica):
-    own, tail1, tail2, tail3, same, across_x, across_y, across_d = pieces
+    own, tiles, near, far, x_near, x_far, y_near, y_far, d_first, d_third, d_far = pieces
     copies = [(own, packed.at[layer, shard])]
-    for step, tail in ((1, tail1), (2, tail2), (3, tail3)):
-        copies.append((tail, packed.at[layer, lax.rem(shard + 4 - step, 4), :, pl.ds(TAIL0, TAIL)]))
-    for flip, group in ((0, same), (1, across_x), (2, across_y), (3, across_d)):
-        column = pl.multiple_of(lax.bitwise_xor(replica, flip) * QUARTER, LANES)
-        for step in (1, 2, 3):
-            copies.append(
-                (
-                    group.at[step - 1],
-                    packed.at[layer, lax.rem(shard + 4 - step, 4), :, pl.ds(column, QUARTER)],
-                )
-            )
+    for index, step in enumerate((1, 3, 2)):
+        owner = packed.at[layer, lax.rem(shard + 4 - step, 4)]
+        copies.append((tiles.at[index], owner.at[:, pl.ds(VEC0, LANES)]))
+    groups = (
+        (0, near.at[0], near.at[1], far),
+        (1, x_near.at[0], x_near.at[1], x_far),
+        (2, y_near.at[0], y_near.at[1], y_far),
+        (3, d_first, d_third, d_far),
+    )
+    for bits, first, third, second in groups:
+        column = pl.multiple_of(lax.bitwise_xor(replica, bits) * QUARTER, LANES)
+        for step, piece in ((1, first), (3, third), (2, second)):
+            owner = packed.at[layer, lax.rem(shard + 4 - step, 4)]
+            copies.append((piece, owner.at[:, pl.ds(column, QUARTER)]))
     return [
         pltpu.make_async_copy(source, target, sems.at[layer, index])
         for index, (source, target) in enumerate(copies)
@@ -296,8 +299,9 @@
 
 
 def main_kernel(seq, *refs):
-    mine, other = refs[0:8], refs[8:16]
-    patches, cotangent, live = refs[16:19]
+    mine, other = refs[0:11], refs[11:22]
+    patches, cotangent, live = refs[22:25]
+    refs = refs[25:]
     (
         out_one,
         out_two,
@@ -306,13 +310,8 @@
         send,
         kept_weights,
         kept_vectors,
-        qkv0,
-        p0,
-        attended0,
-        hidden0,
-        act0,
-        slope0,
-    ) = refs[19:32]
+    ) = refs[0:7]
+    kept_acts = refs[7:13]
     (
         packed,
         down,
@@ -320,18 +319,13 @@
         biases,
         rows_in,
         rows_mid,
-        qkv1,
-        p1,
-        attended1,
-        hidden1,
-        act1,
-        slope1,
         up_grad,
         qkv_grad,
         grads,
         sems,
         out_sems,
-    ) = refs[32:]
+    ) = refs[13:24]
+    acts0, acts1 = refs[24:30], refs[30:36]
     section, shard, replica = positions()
     for copy in start_copies(mine, packed, section, sems, shard, replica):
         copy.start()
@@ -357,14 +351,15 @@
         copy.start()
     kept_vectors[...] = vectors[0]
     x0 = rows_in[...]
-    acts0 = (qkv0, p0, attended0, hidden0, act0, slope0)
     result = layer_forward(x0, seq, weights0, vec0, bias_up0, acts0)
+    for index in range(6):
+        save.append(pltpu.make_async_copy(acts0[index], kept_acts[index], out_sems.at[3 + index]))
+        save[-1].start()
     out_one[...] = result[:seq].astype(BF16)
     live_rows = lax.broadcasted_iota(jnp.int32, (SEQ_ROWS, width), 0) < seq
     rows_mid[...] = jnp.where(live_rows, result.astype(BF16).astype(F32), 0.0)
 
     weights1, vec1, bias_up1 = ready(1)
-    acts1 = (qkv1, p1, attended1, hidden1, act1, slope1)
     result = layer_forward(rows_mid[...], seq, weights1, vec1, bias_up1, acts1)
     out_two[...] = result[:seq].astype(BF16)
 
@@ -386,17 +381,22 @@
 
 def last_kernel(seq, *refs):
     weights, vectors_in, grad_one, patches = refs[0:4]
-    acts = refs[4:10]
+    saved = refs[4:10]
     grad_out, keep, send = refs[10:13]
-    packed, down, rows_in, rows_grad, up_grad, qkv_grad, grads, sems, out_sems = refs[13:]
+    packed, down, rows_in, rows_grad, up_grad, qkv_grad, grads, sems, out_sems = refs[13:22]
+    acts = refs[22:28]
     section, shard, replica = positions()
-    load = pltpu.make_async_copy(weights, packed, sems.at[0])
-    load.start()
+    loads = [pltpu.make_async_copy(weights, packed, sems.at[6])]
+    for index in range(6):
+        loads.append(pltpu.make_async_copy(saved[index], acts[index], sems.at[index]))
+    for load in loads:
+        load.start()
     width = rows_in.shape[1]
     for buffer, source in ((rows_in, patches[section]), (rows_grad, grad_one[...])):
         buffer[seq - seq % 8 :] = jnp.zeros((SEQ_ROWS - seq + seq % 8, width), F32)
         buffer[:seq] = source.astype(F32)
-    load.wait()
+    for load in loads:
+        load.wait()
     for owner in range(4):
         for fold in range(4):
             at = (owner * 4 + fold) * ROWS
@@ -450,7 +450,8 @@
     ]
 
 
-PARAMS = pltpu.CompilerParams(vmem_limit_bytes=VMEM_LIMIT)
+def grant(mib):
+    return pltpu.CompilerParams(vmem_limit_bytes=mib * MIB)
 
 
 def run_main(mine, other, patches, cotangent, live, wide):
@@ -468,8 +469,8 @@
             shape((8, width), F32),
         ]
         + [shape(*a) for a in acts],
-        in_specs=anywhere(16) + vmem(2) + [pl.BlockSpec(memory_space=pltpu.SMEM)],
-        out_specs=vmem(3) + anywhere(3) + vmem(7),
+        in_specs=anywhere(22) + vmem(2) + [pl.BlockSpec(memory_space=pltpu.SMEM)],
+        out_specs=vmem(3) + anywhere(3) + vmem(1) + anywhere(6),
         scratch_shapes=[
             pltpu.VMEM((2, 4, ROWS, PACKED), BF16),
             pltpu.VMEM((2, wide, width), BF16),
@@ -477,16 +478,14 @@
             pltpu.VMEM((2, 1, wide), F32),
             pltpu.VMEM((SEQ_ROWS, width), F32),
             pltpu.VMEM((SEQ_ROWS, width), F32),
-        ]
-        + [pltpu.VMEM(*a) for a in acts]
-        + [
             pltpu.VMEM((SEQ_ROWS, wide), BF16),
             pltpu.VMEM((SEQ_ROWS, 3 * width), BF16),
             pltpu.VMEM((2, 4, 4, HALF, PIECE), BF16),
             pltpu.SemaphoreType.DMA((2, 16)),
-            pltpu.SemaphoreType.DMA((3,)),
-        ],
-        compiler_params=PARAMS,
+            pltpu.SemaphoreType.DMA((9,)),
+        ]
+        + [pltpu.VMEM(*a) for a in acts + acts],
+        compiler_params=grant(32),
         name="forward_and_layer_one",
     )(*mine, *other, patches, cotangent, live)
 
@@ -500,7 +499,7 @@
             shape((4, 4, HALF, PIECE), BF16),
             shape((4, 4, HALF, PIECE), BF16),
         ],
-        in_specs=anywhere(1) + vmem(9),
+        in_specs=anywhere(1) + vmem(3) + anywhere(6),
         out_specs=vmem(1) + anywhere(2),
         scratch_shapes=[
             pltpu.VMEM((1, 4, ROWS, PACKED), BF16),
@@ -510,96 +509,83 @@
             pltpu.VMEM((SEQ_ROWS, wide), BF16),
             pltpu.VMEM((SEQ_ROWS, 3 * width), BF16),
             pltpu.VMEM((2, 4, 4, HALF, PIECE), BF16),
-            pltpu.SemaphoreType.DMA((1,)),
+            pltpu.SemaphoreType.DMA((7,)),
             pltpu.SemaphoreType.DMA((2,)),
-        ],
-        compiler_params=PARAMS,
+        ]
+        + [pltpu.VMEM(*a) for a in act_shapes(width, wide)],
+        compiler_params=grant(20),
+        cost_estimate=pl.CostEstimate(flops=8_000_000_000, bytes_accessed=8_000_000, transcendentals=0),
         name="layer_zero_backward",
     )(weights, vectors, grad_one, patches, *acts)
 
 
-def pair_sum_kernel(keep, recv, *outs):
+def add(a, b):
+    return a.astype(F32) + b.astype(F32)
+
+
+def small_call(kernel, outs, name, *ins):
+    return pl.pallas_call(
+        kernel,
+        out_shape=[shape(dims, BF16) for dims in outs],
+        in_specs=vmem(len(ins)),
+        out_specs=vmem(len(outs)),
+        compiler_params=grant(12),
+        name=name,
+    )(*ins)
+
+
+def pair_sum_kernel(keep, recv, to_x, to_y, own, x_late, y_late):
     for place in range(4):
-        outs[place][...] = (keep[place].astype(F32) + recv[place].astype(F32)).astype(BF16)
-
-
-def pair_sum(keep, recv):
-    return pl.pallas_call(
-        pair_sum_kernel,
-        out_shape=[shape(keep.shape[1:], BF16)] * 4,
-        in_specs=vmem(2),
-        out_specs=vmem(4),
-        compiler_params=PARAMS,
-        name="sum_of_cores",
-    )(keep, recv)
-
-
-def plane_sum_kernel(a, b, c, d, *outs):
-    for place in range(4):
-        outs[place][...] = (
-            a[place].astype(F32) + b[place].astype(F32) + (c[place].astype(F32) + d[place].astype(F32))
-        ).astype(BF16)
-
-
-def plane_sum(parts):
-    return pl.pallas_call(
-        plane_sum_kernel,
-        out_shape=[shape(parts[0].shape[1:], BF16)] * 4,
-        in_specs=vmem(4),
-        out_specs=vmem(4),
-        compiler_params=PARAMS,
-        name="sum_of_plane",
-    )(*parts)
-
-
-def column_sum_kernel(*refs):
-    ins, (mine, other) = refs[:8], refs[8:]
-    section = lax.axis_index("section")
-    sums = []
-    for group in (ins[:4], ins[4:]):
-        a, b, c, d = (member[...].astype(F32) for member in group)
-        sums.append((a + b + (c + d)).astype(BF16))
-
-    @pl.when(section == 0)
-    def _():
-        mine[...] = sums[0]
-        other[...] = sums[1]
-
-    @pl.when(section == 1)
-    def _():
-        mine[...] = sums[1]
-        other[...] = sums[0]
-
-
-def column_sum(zero, one):
-    return pl.pallas_call(
-        column_sum_kernel,
-        out_shape=[shape(zero[0].shape, BF16)] * 2,
-        in_specs=vmem(8),
-        out_specs=vmem(2),
-        compiler_params=PARAMS,
-        name="sum_of_column",
-    )(*zero, *one)
+        own[place] = add(keep[0, place], recv[0, place]).astype(BF16)
+    for place in range(2):
+        to_x[0, place] = add(keep[1, place], recv[1, place]).astype(BF16)
+        to_x[1, place] = add(keep[3, place], recv[3, place]).astype(BF16)
+        to_y[0, place] = add(keep[2, 2 + place], recv[2, 2 + place]).astype(BF16)
+        to_y[1, place] = add(keep[3, 2 + place], recv[3, 2 + place]).astype(BF16)
+        x_late[place] = add(keep[1, 2 + place], recv[1, 2 + place]).astype(BF16)
+        y_late[place] = add(keep[2, place], recv[2, place]).astype(BF16)
+
+
+def relay_kernel(late, got, out):
+    for place in range(2):
+        out[place] = add(late[place], got[1, place]).astype(BF16)
+
+
+def plane_sum_kernel(own, got, late, one, two):
+    for place, out in enumerate((one, two)):
+        out[...] = (add(own[place], got[0, place]) + late[place].astype(F32)).astype(BF16)
+
+
+def column_sum_kernel(a, b, c, d, out):
+    out[...] = (add(a[...], b[...]) + add(c[...], d[...])).astype(BF16)
 
 
 def unpack_kernel(*refs):
-    pieces, (qkv, out, up, down), rest = refs[:8], refs[8:12], refs[12:21]
-    table, sems = refs[21:]
+    zero, one = refs[:8], refs[8:16]
+    (qkv, out, up, down), rest = refs[16:20], refs[20:29]
+    table, sems = refs[29:]
     section, _, replica = positions()
-    copies = []
-    for flip in range(4):
-        place = lax.bitwise_xor(replica, flip)
-        for half in range(2):
-            where = section if half == 0 else 1 - section
-            copies.append(
-                pltpu.make_async_copy(
-                    pieces[2 * flip + half], table.at[place, where], sems.at[2 * flip + half]
+
+    def copies_of(pieces):
+        copies = []
+        for bits in range(4):
+            place = lax.bitwise_xor(replica, bits)
+            for half in range(2):
+                where = section if half == 0 else 1 - section
+                index = 2 * bits + half
+                copies.append(
+                    pltpu.make_async_copy(pieces[index], table.at[place, where], sems.at[index])
                 )
-            )
-    for copy in copies:
-        copy.start()
-    for copy in copies:
-        copy.wait()
+        return copies
+
+    for layer, pieces in enumerate((zero, one)):
+
+        @pl.when(section == layer)
+        def _(pieces=pieces):
+            for copy in copies_of(pieces):
+                copy.start()
+            for copy in copies_of(pieces):
+                copy.wait()
 
     def put(target, row, column, start, count, at):
         while count:
@@ -624,7 +610,7 @@
     rest[8][...] = jnp.concatenate([tile[8 + k : 9 + k] for k in range(3)], 1)
 
 
-def unpack(pieces, width, wide):
+def unpack(zero, one, width, wide):
     return pl.pallas_call(
         unpack_kernel,
         out_shape=[
@@ -635,15 +621,15 @@
         ]
         + [shape((1, ROWS), F32)] * 8
         + [shape((1, 4 * ROWS), F32)],
-        in_specs=anywhere(8),
+        in_specs=anywhere(16),
         out_specs=vmem(13),
         scratch_shapes=[
             pltpu.VMEM((4, 2, HALF, PIECE), BF16),
             pltpu.SemaphoreType.DMA((8,)),
         ],
-        compiler_params=PARAMS,
+        compiler_params=grant(16),
         name="unpack",
-    )(*pieces)
+    )(*zero, *one)
 
 
 def swap(value):
@@ -658,48 +644,160 @@
     return lax.ppermute(value, "shard", [(place, (place + steps) % 4) for place in range(4)])
 
 
+def pack_kernel(*refs):
+    sources, (own, quarter) = refs[:13], refs[13:15]
+    staged, eight, bias_up, sems = refs[15:19]
+    _, _, replica = positions()
+    width = sources[2].shape[2]
+    targets = [
+        own.at[:, UP0:QKV0],
+        own.at[:, QKV0:OUT0],
+        own.at[:, OUT0:DOWN0],
+        staged,
+    ]
+    targets += [eight.at[index : index + 1] for index in range(8)] + [bias_up]
+    copies = [
+        pltpu.make_async_copy(source.at[0] if index < 4 else source, target, sems.at[index])
+        for index, (source, target) in enumerate(zip(sources, targets))
+    ]
+    for copy in copies:
+        copy.start()
+    for copy in copies:
+        copy.wait()
+    for fold in range(4):
+        own[:, DOWN0 + fold * width : DOWN0 + (fold + 1) * width] = staged[
+            fold * ROWS : (fold + 1) * ROWS
+        ]
+    padded = jnp.concatenate([eight[...], jnp.zeros((8, LANES - ROWS), F32)], 1)
+    up = [bias_up[:, k * LANES : (k + 1) * LANES] for k in range(3)]
+    tile = jnp.concatenate([padded] + up + [jnp.zeros((5, LANES), F32)], 0)
+    high = tile.astype(BF16)
+    low = tile - high.astype(F32)
+    own[0:16, VEC0:PACKED] = high
+    own[16:32, VEC0:PACKED] = low.astype(BF16)
+    own[32:, VEC0:PACKED] = jnp.zeros((ROWS - 32, LANES), BF16)
+    quarter[:, QUARTER:] = own[:, VEC0:PACKED]
+    for place in range(4):
+
+        @pl.when(replica == place)
+        def _(place=place):
+            quarter[:, :QUARTER] = own[:, place * QUARTER : (place + 1) * QUARTER]
+
+
+def pack(*arrays):
+    width = arrays[2].shape[2]
+    return pl.pallas_call(
+        pack_kernel,
+        out_shape=[shape(dims, BF16) for dims in ((ROWS, PACKED), (ROWS, PIECE_IN))],
+        in_specs=anywhere(13),
+        out_specs=vmem(2),
+        scratch_shapes=[
+            pltpu.VMEM((4 * ROWS, width), BF16),
+            pltpu.VMEM((8, ROWS), F32),
+            pltpu.VMEM((1, 4 * ROWS), F32),
+            pltpu.SemaphoreType.DMA((13,)),
+        ],
+        compiler_params=grant(60),
+        name="pack",
+    )(*arrays)
+
+
+def after(value, *earlier):
+    return lax.optimization_barrier((value,) + earlier)[0]
+
+
+def reduce_plane(keep, send):
+    half = (2,) + keep.shape[2:]
+    to_x, to_y, own, x_late, y_late = small_call(
+        pair_sum_kernel,
+        [(2,) + half, (2,) + half, keep.shape[1:], half, half],
+        "sum_of_cores",
+        keep,
+        swap(send),
+    )
+    return to_x, to_y, own, x_late, y_late
+
+
+def near_kernel(first, third, near, upper, lower):
+    near[0] = first[:, :QUARTER]
+    near[1] = third[:, :QUARTER]
+    upper[...] = first[:HALF]
+    lower[...] = third[HALF:]
+
+
+def far_kernel(first, third, upper, lower, far, tiles):
+    far[:HALF] = upper[:, :QUARTER]
+    far[HALF:] = lower[:, :QUARTER]
+    tiles[0] = first[:, QUARTER:]
+    tiles[1] = third[:, QUARTER:]
+    tiles[2, :HALF] = upper[:, QUARTER:]
+    tiles[2, HALF:] = lower[:, QUARTER:]
+
+
+def exchange_plane(to_x, to_y, own, x_late, y_late, got_x, got_y):
+    half, piece = x_late.shape, x_late.shape[1:]
+    (y_send,) = small_call(relay_kernel, [half], "relay", y_late, got_x)
+    (x_send,) = small_call(relay_kernel, [half], "relay", x_late, got_y)
+    late_y, late_x = flip(y_send, 2), flip(x_send, 1)
+    zero, one = small_call(plane_sum_kernel, [piece] * 2, "sum_of_plane", own[:2], got_x, late_y)
+    two, three = small_call(plane_sum_kernel, [piece] * 2, "sum_of_plane", own[2:], got_y, late_x)
+    column = small_call(
+        column_sum_kernel,
+        [piece],
+        "sum_of_column",
+        zero,
+        shift(one, 1),
+        shift(two, 2),
+        shift(three, 3),
+    )[0]
+    return column, late_x, late_y
+
+
+def spread(value):
+    pieces = [value] + [flip(value, bits) for bits in (1, 2, 3)]
+    return [member for piece in pieces for member in (piece, swap(piece))]
+
+
 def packed_local(patches, live_slots, cotangent, w_qkv, w_out, w_up, w_down, *small):
+    section, _, _ = positions()
+    width, wide = w_out.shape[2], w_up.shape[2]
     bias_q, bias_v, bias_out, bias_up, bias_down, gain_one, offset_one, gain_two, offset_two = small
-    section, _, replica = positions()
-    width, wide = w_out.shape[2], w_up.shape[2]
-    folded = [w_down[0, fold * ROWS : (fold + 1) * ROWS] for fold in range(4)]
-    eight = jnp.concatenate(
-        [bias_q, bias_v, bias_out, bias_down, gain_one, offset_one, gain_two, offset_two], 0
-    )
-    eight = jnp.pad(eight, ((0, 0), (0, LANES - ROWS)))
-    tile = jnp.concatenate([eight, bias_up.reshape(3, LANES), jnp.zeros((5, LANES), F32)], 0)
-    high = tile.astype(BF16)
-    low = (tile - high.astype(F32)).astype(BF16)
-    tile = jnp.concatenate([high, low, jnp.zeros((ROWS - 32, LANES), BF16)], 0)
-    own = jnp.concatenate([w_up[0], w_qkv[0], w_out[0]] + folded + [tile], 1)
-    tail = own[:, TAIL0:]
-    quarter = lax.dynamic_slice(own, (0, replica * QUARTER), (ROWS, QUARTER))
-
-    same = jnp.stack([shift(quarter, step) for step in (1, 2, 3)])
-    across = [flip(same, bits) for bits in (1, 2, 3)]
-    tails = [shift(tail, step) for step in (1, 2, 3)]
-    mine = [own] + tails + [same] + across
+    vectors = (bias_q, bias_v, bias_out, bias_down, gain_one, offset_one, gain_two, offset_two)
+    own, quarter = pack(w_up, w_qkv, w_out, w_down, *vectors, bias_up)
+    first, third = shift(quarter, 1), shift(quarter, 3)
+    half = (HALF, PIECE_IN)
+    near, upper, lower = small_call(
+        near_kernel, [(2, ROWS, QUARTER), half, half], "near", first, third
+    )
+    x_near, y_near = flip(near, 1), flip(near, 2)
+    far, tiles = small_call(
+        far_kernel,
+        [(ROWS, QUARTER), (3, ROWS, LANES)],
+        "far",
+        first,
+        third,
+        shift(upper, 1),
+        shift(lower, 3),
+    )
+    d_first, d_third = flip(y_near[0], 1), flip(x_near[1], 2)
+    far = after(far, x_near, y_near)
+    x_far, y_far, d_far = (flip(far, bits) for bits in (1, 2, 3))
+    mine = [own, tiles, near, far, x_near, x_far, y_near, y_far, d_first, d_third, d_far]
     other = [swap(member) for member in mine]
 
     (out_one, out_two, grad_one, keep1, send1, kept, vectors, *acts) = run_main(
         mine, other, patches, cotangent, live_slots, wide
     )
-
-    def reduce_plane(keep, send):
-        same, x, y, d = pair_sum(keep, swap(send))
-        parts = [same, flip(x, 1), flip(y, 2), flip(d, 3)]
-        chunks = plane_sum(parts)
-        return [chunks[0]] + [shift(chunks[step], step) for step in (1, 2, 3)]
-
-    one = reduce_plane(keep1, send1)
-    grad_zero, keep0, send0 = run_last(kept, vectors, grad_one, patches, acts, wide)
-    zero = reduce_plane(keep0, send0)
-    half_mine, half_other = column_sum(zero, one)
-    halves = [half_mine, swap(half_other)]
-    pieces = list(halves)
-    for bits in (1, 2, 3):
-        pieces += [flip(member, bits) for member in halves]
-    grad_qkv, grad_out, grad_up, grad_down, *rest = unpack(pieces, width, wide)
+    parts = reduce_plane(keep1, send1)
+    got = (flip(parts[0], 1), flip(parts[1], 2))
+    last = run_last(after(kept, *parts), vectors, grad_one, patches, acts, wide)
+    grad_zero, keep0, send0, *got = lax.optimization_barrier((*last, *got))
+    one, *_ = exchange_plane(*parts, *got)
+    parts = reduce_plane(keep0, send0)
+    zero, *late = exchange_plane(*parts, flip(parts[0], 1), flip(parts[1], 2))
+    one = spread(after(one, *late))
+    zero = spread(zero)
+    grad_qkv, grad_out, grad_up, grad_down, *rest = unpack(zero, one, width, wide)
 
     first = section == 0
     out_send = jnp.where(first, out_two, out_one)
@@ -841,7 +939,7 @@
             pltpu.VMEM((SEQ_ROWS, 3 * width), BF16),
         ]
         + [pltpu.VMEM(*a) for a in acts + acts],
-        compiler_params=PARAMS,
+        compiler_params=grant(56),
         name="both_layers",
     )(patches, cotangent, live_slots, *(whole(w) for w in (w_qkv, w_out, w_up, w_down)), vectors, biases)
 

time: 181 us -> 156 us (0.86)
  waiting for transfers between devices: 90.1 us -> 73.8 us
  local copies, waits for them, and re-layouts: 12 us -> 3.78 us
    ppermute x15 -> x21, waiting for transfers between devices: 53.2 us -> 40.4 us  [flip(): lax.ppermute(value, 'replica', [(place, place ^ bits) for place in range(...]
    unnamed x43 -> x32, local copies, waits for them, and re-layouts: 10.1 us -> 3.68 us
    ppermute x12 -> x10, waiting for transfers between devices: 28.7 us -> 22.6 us  [shift(): lax.ppermute(value, 'shard', [(place, (place + steps) % 4) for place in r...]
    ppermute x15 -> x21, starting transfers between devices: 17.2 us -> 22.4 us  [flip(): lax.ppermute(value, 'replica', [(place, place ^ bits) for place in range(...]
    ppermute x12 -> x10, starting transfers between devices: 23.4 us -> 18.5 us  [shift(): lax.ppermute(value, 'shard', [(place, (place + steps) % 4) for place in r...]
    ppermute x13 -> x23, waiting for transfers between devices: 8.16 us -> 10.8 us  [swap(): return lax.ppermute(value, 'section', [(0, 1), (1, 0)])]
    pallas_call x5 -> x15, Pallas kernels: 4.56 us -> 5.69 us  [the longest x14 3.25 us: small_call(): pl.pallas_call(kernel, out_shape=[shape(dims, BF16) for dims in outs], in...]
  transfers between devices with their start and end apart: 40 -> 54, of which waited for: 21 -> 27; matrix products, arithmetic and copies ran while one was open for 3% -> 2% of each run, Pallas kernels for 3% -> 6%
where the time goes in v2:
time: 156 us
  waiting for transfers between devices  73.8 us (47%)
  starting transfers between devices  44.4 us (28%)
  Pallas kernels  32.8 us (21%)
  local copies, waits for them, and re-layouts  3.78 us (2%)
    ppermute x21, waiting for transfers between devices, flip(): lax.ppermute(value, 'replica', [(place, place ^ bits) for place in range(...  40.4 us
    ppermute x10, waiting for transfers between devices, shift(): lax.ppermute(value, 'shard', [(place, (place + steps) % 4) for place in r...  22.6 us
    ppermute x21, starting transfers between devices, flip(): lax.ppermute(value, 'replica', [(place, place ^ bits) for place in range(...  22.4 us
    ppermute x10, starting transfers between devices, shift(): lax.ppermute(value, 'shard', [(place, (place + steps) % 4) for place in r...  18.5 us
    pallas_call x1, Pallas kernels, run_main(): pl.pallas_call(functools.partial(main_kernel, seq), out_shape=[shape((seq...  16 us
    ppermute x23, waiting for transfers between devices, swap(): return lax.ppermute(value, 'section', [(0, 1), (1, 0)])  10.8 us
    pallas_call x1, Pallas kernels, run_last(): pl.pallas_call(functools.partial(last_kernel, seq), out_shape=[shape((seq...  8.23 us
    unnamed x32, local copies, waits for them, and re-layouts  3.68 us
  transfers between devices with their start and end apart: 54, of which 27 were waited for; matrix products, arithmetic and copies ran while one was open for 2% of the time, Pallas kernels for 6%

profile of v2, /device:TPU:0, one launch (start us, length us, event | category | flops | bytes accessed | tf_op | source)
XLA Modules:
  0.0 156.3 jit_solution(13095520434705623023)
XLA Ops:
  0.7 2.4 %pack.1 = (bf16[96,4736]{1,0:T(8,128)(2,1)}, bf16[96,1280]{1,0:T(8,128)(2,1)}) custom-call(bf16[1,96,1536]{2,1,0:T(8,128)(2,1)} %refs_0_.1, bf16[1,96,1152]{2,1,0:T(8,128)(2,1)} %refs_1_.1, bf16[1,96,384]{2,1,0:T(8,128)(2,1)} %refs_2_.1, bf16[1,384,384]{2,1,0:T(8,128)(2,1)} %refs_3_.2, f32[1,96]{1,0:T(1,128)} %refs_4_.1, f32[1,96]{1,0:T(1,128)} %refs_5_.1, ...), custom_call_target="tpu_custom_call" | custom-call | tf_op jit(solution)/shard_map/pack/pallas_call | solution.py:689
  3.1 3.1 %collective-permute-start = (bf16[96,1280]{1,0:T(8,128)(2,1)}, bf16[96,1280]{1,0:T(8,128)(2,1)S(1)}, u32[]{:S(2)}, u32[]{:S(2)}) collective-permute-start(bf16[96,1280]{1,0:T(8,128)(2,1)} %get-tuple-element.78), channel_id=1, source_target_pairs={{0,4},{4,8},{8,12},{12,0},{1,5},{5,9},{9,13},{13,1},{2,6},{6,10},{... | collective-permute-start | bytes 737288 | tf_op jit(solution)/shard_map/ppermute | solution.py:644
  6.2 2.1 %collective-permute-start.1 = (bf16[96,1280]{1,0:T(8,128)(2,1)}, bf16[96,1280]{1,0:T(8,128)(2,1)S(1)}, u32[]{:S(2)}, u32[]{:S(2)}) collective-permute-start(bf16[96,1280]{1,0:T(8,128)(2,1)} %get-tuple-element.78), channel_id=1, source_target_pairs={{0,12},{4,0},{8,4},{12,8},{1,13},{5,1},{9,5},{13,9},{2,14},{6,2},{... | collective-permute-start | bytes 737288 | tf_op jit(solution)/shard_map/ppermute | solution.py:644
  8.3 7.0 %collective-permute-done.first = bf16[96,1280]{1,0:T(8,128)(2,1)S(1)} collective-permute-done((bf16[96,1280]{1,0:T(8,128)(2,1)}, bf16[96,1280]{1,0:T(8,128)(2,1)S(1)}, u32[]{:S(2)}, u32[]{:S(2)}) %collective-permute-start) | collective-permute-done | bytes 245792 | tf_op jit(solution)/shard_map/ppermute | solution.py:644
  15.3 3.8 %collective-permute-done.1.third = bf16[96,1280]{1,0:T(8,128)(2,1)S(1)} collective-permute-done((bf16[96,1280]{1,0:T(8,128)(2,1)}, bf16[96,1280]{1,0:T(8,128)(2,1)S(1)}, u32[]{:S(2)}, u32[]{:S(2)}) %collective-permute-start.1) | collective-permute-done | bytes 245792 | tf_op jit(solution)/shard_map/ppermute | solution.py:644
  19.2 1.6 collective-permute-start.4
  20.7 1.5 collective-permute-start.5
  23.4 2.7 %collective-permute-start.3 = (bf16[48,1280]{1,0:T(8,128)(2,1)S(1)}, bf16[48,1280]{1,0:T(8,128)(2,1)S(1)}, u32[]{:S(2)}, u32[]{:S(2)}) collective-permute-start(bf16[48,1280]{1,0:T(8,128)(2,1)S(1)} %get-tuple-element.80), channel_id=1, source_target_pairs={{0,12},{4,0},{8,4},{12,8},{1,13},{5,1},{9,5},{13,9},{2,14},{6,2},{... | collective-permute-start | bytes 368648 | tf_op jit(solution)/shard_map/ppermute | solution.py:644
  26.1 3.6 %collective-permute-done.2.upper = bf16[48,1280]{1,0:T(8,128)(2,1)S(1)} collective-permute-done((bf16[48,1280]{1,0:T(8,128)(2,1)S(1)}, bf16[48,1280]{1,0:T(8,128)(2,1)S(1)}, u32[]{:S(2)}, u32[]{:S(2)}) %collective-permute-start.2) | collective-permute-done | bytes 122912 | tf_op jit(solution)/shard_map/ppermute | solution.py:644
  32.4 1.5 collective-permute-start.7
  35.5 4.7 %collective-permute-done.6.refs_5_ = bf16[96,1152]{1,0:T(8,128)(2,1)S(1)} collective-permute-done((bf16[96,1152]{1,0:T(8,128)(2,1)S(1)}, bf16[96,1152]{1,0:T(8,128)(2,1)S(1)}, u32[]{:S(2)}, u32[]{:S(2)}) %collective-permute-start.6) | collective-permute-done | bytes 221216 | tf_op jit(solution)/shard_map/ppermute | solution.py:640
  42.3 1.9 %collective-permute-start.9 = (bf16[96,1152]{1,0:T(8,128)(2,1)S(1)}, bf16[96,1152]{1,0:T(8,128)(2,1)S(1)}, u32[]{:S(2)}, u32[]{:S(2)}) collective-permute-start(bf16[96,1152]{1,0:T(8,128)(2,1)S(1)} %slice_bitcast_fusion), channel_id=1, source_target_pairs={{0,2},{1,3},{2,0},{3,1},{4,6},{5,7},{6,4},{7,5},{8,10},{9,11},{10,... | collective-permute-start | bytes 663560 | tf_op jit(solution)/shard_map/ppermute | solution.py:640
  46.1 1.7 %collective-permute-done.8.refs_8_ = bf16[96,1152]{1,0:T(8,128)(2,1)S(1)} collective-permute-done((bf16[96,1152]{1,0:T(8,128)(2,1)S(1)}, bf16[96,1152]{1,0:T(8,128)(2,1)S(1)}, u32[]{:S(2)}, u32[]{:S(2)}) %collective-permute-start.8) | collective-permute-done | bytes 221216 | tf_op jit(solution)/shard_map/ppermute | solution.py:640
  51.2 16.0 %forward_and_layer_one.1 = (bf16[197,384]{1,0:T(8,128)(2,1)S(1)}, bf16[197,384]{1,0:T(8,128)(2,1)S(1)}, bf16[197,384]{1,0:T(8,128)(2,1)S(1)}, bf16[4,4,48,1280]{...) custom-call(bf16[96,4736]{1,0:T(8,128)(2,1)S(1)} %copy-done, ...), custom_call_target="tpu_custom_call" | custom-call | tf_op jit(solution)/shard_map/forward_and_layer_one/pallas_call | solution.py:460
  67.5 3.8 %collective-permute-done.23.recv = bf16[4,4,48,1280]{3,2,1,0:T(8,128)(2,1)S(1)} collective-permute-done((bf16[4,4,48,1280]{3,2,1,0:T(8,128)(2,1)S(1)}, bf16[4,4,48,1280]{3,2,1,0:T(8,128)(2,1)S(1)}, u32[]{:S(2)}, u32[]{:S(2)}) %collective-permute-start.23) | collective-permute-done | bytes 1966112 | tf_op jit(solution)/shard_map/ppermute | solution.py:636
  74.5 2.0 %collective-permute-start.25 = (bf16[2,2,48,1280]{3,2,1,0:T(8,128)(2,1)S(1)}, bf16[2,2,48,1280]{3,2,1,0:T(8,128)(2,1)S(1)}, u32[]{:S(2)}, u32[]{:S(2)}) collective-permute-start(bf16[2,2,48,1280]{3,2,1,0:T(8,128)(2,1)S(1)} %get-tuple-element.91), channel_id=1, source_target_pairs={{0,2},{1,3},{2,0},{3,1},{4,6},{5,7},{6,4},{7,5},{8,10},{9,11},{10,... | collective-permute-start | bytes 1474568 | tf_op jit(solution)/shard_map/ppermute | solution.py:640
  76.5 8.2 %layer_zero_backward.1 = (f32[197,384]{1,0:T(8,128)S(1)}, bf16[4,4,48,1280]{3,2,1,0:T(8,128)(2,1)S(1)}, bf16[4,4,48,1280]{3,2,1,0:T(8,128)(2,1)}) custom-call(bf16[1,4,96,4736]{3,2,1,0:T(8,128)(2,1)S(1)} %get-tuple-element.95.refs_0_, f32[8,384]{1,0:T(8,128)S(1)} %get-tuple-element.96.refs_1_, bf16[197,384]{1,0:T(8,128)(2,1)S(1)} %get-tuple-element.97.refs_2_, ...), custom_call_target="tpu_custom_call" | custom-call | flops 8000000000 | bytes 8000000 | tf_op jit(solution)/shard_map/layer_zero_backward/pallas_call | solution.py:495
  84.8 1.8 %collective-permute-done.24.got = bf16[2,2,48,1280]{3,2,1,0:T(8,128)(2,1)S(1)} collective-permute-done((bf16[2,2,48,1280]{3,2,1,0:T(8,128)(2,1)S(1)}, bf16[2,2,48,1280]{3,2,1,0:T(8,128)(2,1)S(1)}, u32[]{:S(2)}, u32[]{:S(2)}) %collective-permute-start.24) | collective-permute-done | bytes 491552 | tf_op jit(solution)/shard_map/ppermute | solution.py:640
  87.8 4.3 %collective-permute-done.27.recv = bf16[4,4,48,1280]{3,2,1,0:T(8,128)(2,1)} collective-permute-done((bf16[4,4,48,1280]{3,2,1,0:T(8,128)(2,1)}, bf16[4,4,48,1280]{3,2,1,0:T(8,128)(2,1)}, u32[]{:S(2)}, u32[]{:S(2)}) %collective-permute-start.27) | collective-permute-done | bytes 1966112 | tf_op jit(solution)/shard_map/ppermute | solution.py:636
  92.1 2.0 %sum_of_cores.3 = (bf16[2,2,48,1280]{3,2,1,0:T(8,128)(2,1)S(1)}, bf16[2,2,48,1280]{3,2,1,0:T(8,128)(2,1)S(1)}, bf16[4,48,1280]{2,1,0:T(8,128)(2,1)S(1)}, bf16[2,...) custom-call(bf16[4,4,48,1280]{3,2,1,0:T(8,128)(2,1)S(1)} %get-tuple-element.108.keep, ...), custom_call_target="tpu_custom_call" | custom-call | tf_op jit(solution)/shard_map/sum_of_cores/pallas_call | solution.py:527
  94.1 1.8 %collective-permute-start.31 = (bf16[2,2,48,1280]{3,2,1,0:T(8,128)(2,1)S(1)}, bf16[2,2,48,1280]{3,2,1,0:T(8,128)(2,1)S(1)}, u32[]{:S(2)}, u32[]{:S(2)}) collective-permute-start(bf16[2,2,48,1280]{3,2,1,0:T(8,128)(2,1)S(1)} %get-tuple-element.115), channel_id=1, source_target_pairs={{0,2},{1,3},{2,0},{3,1},{4,6},{5,7},{6,4},{7,5},{8,10},{9,11},{10,... | collective-permute-start | bytes 1474568 | tf_op jit(solution)/shard_map/ppermute | solution.py:640
  96.5 1.7 %collective-permute-start.44 = (bf16[2,48,1280]{2,1,0:T(8,128)(2,1)S(1)}, bf16[2,48,1280]{2,1,0:T(8,128)(2,1)S(1)}, u32[]{:S(2)}, u32[]{:S(2)}) collective-permute-start(bf16[2,48,1280]{2,1,0:T(8,128)(2,1)S(1)} %relay.7), channel_id=1, source_target_pairs={{0,1},{1,0},{2,3},{3,2},{4,5},{5,4},{6,7},{7,6},{8,9},{9,8},{10,11... | collective-permute-start | bytes 737288 | tf_op jit(solution)/shard_map/ppermute | solution.py:640
  98.6 15.5 %collective-permute-done.44.late = bf16[2,48,1280]{2,1,0:T(8,128)(2,1)S(1)} collective-permute-done((bf16[2,48,1280]{2,1,0:T(8,128)(2,1)S(1)}, bf16[2,48,1280]{2,1,0:T(8,128)(2,1)S(1)}, u32[]{:S(2)}, u32[]{:S(2)}) %collective-permute-start.44) | collective-permute-done | bytes 245792 | tf_op jit(solution)/shard_map/ppermute | solution.py:640
  114.3 5.1 %collective-permute-start.46 = (bf16[48,1280]{1,0:T(8,128)(2,1)S(1)}, bf16[48,1280]{1,0:T(8,128)(2,1)S(1)}, u32[]{:S(2)}, u32[]{:S(2)}) collective-permute-start(bf16[48,1280]{1,0:T(8,128)(2,1)S(1)} %get-tuple-element.124), channel_id=1, source_target_pairs={{0,12},{4,0},{8,4},{12,8},{1,13},{5,1},{9,5},{13,9},{2,14},{6,2},{... | collective-permute-start | bytes 368648 | tf_op jit(solution)/shard_map/ppermute | solution.py:644
  120.5 5.5 %collective-permute-done.32.late = bf16[2,48,1280]{2,1,0:T(8,128)(2,1)S(1)} collective-permute-done((bf16[2,48,1280]{2,1,0:T(8,128)(2,1)S(1)}, bf16[2,48,1280]{2,1,0:T(8,128)(2,1)S(1)}, u32[]{:S(2)}, u32[]{:S(2)}) %collective-permute-start.32) | collective-permute-done | bytes 245792 | tf_op jit(solution)/shard_map/ppermute | solution.py:640
  127.1 3.0 %collective-permute-start.34 = (bf16[48,1280]{1,0:T(8,128)(2,1)S(1)}, bf16[48,1280]{1,0:T(8,128)(2,1)S(1)}, u32[]{:S(2)}, u32[]{:S(2)}) collective-permute-start(bf16[48,1280]{1,0:T(8,128)(2,1)S(1)} %get-tuple-element.118), channel_id=1, source_target_pairs={{0,12},{4,0},{8,4},{12,8},{1,13},{5,1},{9,5},{13,9},{2,14},{6,2},{... | collective-permute-start | bytes 368648 | tf_op jit(solution)/shard_map/ppermute | solution.py:644
  130.8 3.4 %collective-permute-done.43.b = bf16[48,1280]{1,0:T(8,128)(2,1)S(1)} collective-permute-done((bf16[48,1280]{1,0:T(8,128)(2,1)S(1)}, bf16[48,1280]{1,0:T(8,128)(2,1)S(1)}, u32[]{:S(2)}, u32[]{:S(2)}) %collective-permute-start.43) | collective-permute-done | bytes 122912 | tf_op jit(solution)/shard_map/ppermute | solution.py:644
  134.6 4.1 %collective-permute-done.33.c = bf16[48,1280]{1,0:T(8,128)(2,1)S(1)} collective-permute-done((bf16[48,1280]{1,0:T(8,128)(2,1)S(1)}, bf16[48,1280]{1,0:T(8,128)(2,1)S(1)}, u32[]{:S(2)}, u32[]{:S(2)}) %collective-permute-start.33) | collective-permute-done | bytes 122912 | tf_op jit(solution)/shard_map/ppermute | solution.py:644
  138.7 2.7 %collective-permute-start.52 = (bf16[48,1280]{1,0:T(8,128)(2,1)S(1)}, bf16[48,1280]{1,0:T(8,128)(2,1)S(1)}, u32[]{:S(2)}, u32[]{:S(2)}) collective-permute-start(bf16[48,1280]{1,0:T(8,128)(2,1)S(1)} %sum_of_column.3.refs_8_), channel_id=1, source_target_pairs={{0,3},{1,2},{2,1},{3,0},{4,7},{5,6},{6,5},{7,4},{8,11},{9,10},{10,... | collective-permute-start | bytes 368648 | tf_op jit(solution)/shard_map/ppermute | solution.py:640
  143.4 1.5 collective-permute-done.50.refs_12_
  148.8 2.7 %collective-permute-done.38.refs_4_ = bf16[48,1280]{1,0:T(8,128)(2,1)S(1)} collective-permute-done((bf16[48,1280]{1,0:T(8,128)(2,1)S(1)}, bf16[48,1280]{1,0:T(8,128)(2,1)S(1)}, u32[]{:S(2)}, u32[]{:S(2)}) %collective-permute-start.38) | collective-permute-done | bytes 122912 | tf_op jit(solution)/shard_map/ppermute | solution.py:640
  153.2 2.9 %unpack.1 = (f32[1,96,1152]{2,1,0:T(8,128)}, f32[1,96,384]{2,1,0:T(8,128)}, f32[1,96,1536]{2,1,0:T(8,128)}, f32[1,384,384]{2,1,0:T(8,128)}, f32[1,96]{1,0:T(1,12...) custom-call(bf16[48,1280]{1,0:T(8,128)(2,1)S(1)} %sum_of_column.2.re, ...), custom_call_target="tpu_custom_call" | custom-call | tf_op jit(solution)/shard_map/unpack/pallas_call | solution.py:614
  (136 shorter events, 29.4 us)
Async XLA Ops:
  3.1 12.1 %collective-permute-start = (bf16[96,1280]{1,0:T(8,128)(2,1)}, bf16[96,1280]{1,0:T(8,128)(2,1)S(1)}, u32[]{:S(2)}, u32[]{:S(2)}) collective-permute-start(bf16[96,1280]{1,0:T(8,128)(2,1)} %get-tuple-element.78), channel_id=1, source_target_pairs={{0,4},{4,8},{8,12},{12,0},{1,5},{5,9},{9,13},{13,1},{2,6},{6,10},{... | collective-permute-start | bytes 737288 | tf_op jit(solution)/shard_map/ppermute | solution.py:644
  6.2 12.9 %collective-permute-start.1 = (bf16[96,1280]{1,0:T(8,128)(2,1)}, bf16[96,1280]{1,0:T(8,128)(2,1)S(1)}, u32[]{:S(2)}, u32[]{:S(2)}) collective-permute-start(bf16[96,1280]{1,0:T(8,128)(2,1)} %get-tuple-element.78), channel_id=1, source_target_pairs={{0,12},{4,0},{8,4},{12,8},{1,13},{5,1},{9,5},{13,9},{2,14},{6,2},{... | collective-permute-start | bytes 737288 | tf_op jit(solution)/shard_map/ppermute | solution.py:644
  19.2 11.5 %collective-permute-start.4 = (bf16[2,96,1152]{2,1,0:T(8,128)(2,1)S(1)}, bf16[2,96,1152]{2,1,0:T(8,128)(2,1)S(1)}, u32[]{:S(2)}, u32[]{:S(2)}) collective-permute-start(bf16[2,96,1152]{2,1,0:T(8,128)(2,1)S(1)} %get-tuple-element.82.refs_2_), channel_id=1, source_target_pairs={{0,1},{1,0},{2,3},{3,2},{4,5},{5,4},{6,7},{7,6},{8,9},{9,8},{10,11... | collective-permute-start | bytes 1327112 | tf_op jit(solution)/shard_map/ppermute | solution.py:640
  20.7 11.2 %collective-permute-start.5 = (bf16[2,96,1152]{2,1,0:T(8,128)(2,1)S(1)}, bf16[2,96,1152]{2,1,0:T(8,128)(2,1)S(1)}, u32[]{:S(2)}, u32[]{:S(2)}) collective-permute-start(bf16[2,96,1152]{2,1,0:T(8,128)(2,1)S(1)} %get-tuple-element.82.refs_2_), channel_id=1, source_target_pairs={{0,2},{1,3},{2,0},{3,1},{4,6},{5,7},{6,4},{7,5},{8,10},{9,11},{10,... | collective-permute-start | bytes 1327112 | tf_op jit(solution)/shard_map/ppermute | solution.py:640
  22.2 7.4 %collective-permute-start.2 = (bf16[48,1280]{1,0:T(8,128)(2,1)S(1)}, bf16[48,1280]{1,0:T(8,128)(2,1)S(1)}, u32[]{:S(2)}, u32[]{:S(2)}) collective-permute-start(bf16[48,1280]{1,0:T(8,128)(2,1)S(1)} %get-tuple-element.79), channel_id=1, source_target_pairs={{0,4},{4,8},{8,12},{12,0},{1,5},{5,9},{9,13},{13,1},{2,6},{6,10},{... | collective-permute-start | bytes 368648 | tf_op jit(solution)/shard_map/ppermute | solution.py:644
  23.4 7.0 %collective-permute-start.3 = (bf16[48,1280]{1,0:T(8,128)(2,1)S(1)}, bf16[48,1280]{1,0:T(8,128)(2,1)S(1)}, u32[]{:S(2)}, u32[]{:S(2)}) collective-permute-start(bf16[48,1280]{1,0:T(8,128)(2,1)S(1)} %get-tuple-element.80), channel_id=1, source_target_pairs={{0,12},{4,0},{8,4},{12,8},{1,13},{5,1},{9,5},{13,9},{2,14},{6,2},{... | collective-permute-start | bytes 368648 | tf_op jit(solution)/shard_map/ppermute | solution.py:644
  26.1 22.3 %collective-permute-start.11 = (bf16[96,4736]{1,0:T(8,128)(2,1)}, bf16[96,4736]{1,0:T(8,128)(2,1)S(1)}, u32[]{:S(2)}, u32[]{:S(2)}) collective-permute-start(bf16[96,4736]{1,0:T(8,128)(2,1)} %get-tuple-element.77.refs_0_), channel_id=1, source_target_pairs={{0,16},{16,0},{1,17},{17,1},{2,18},{18,2},{3,19},{19,3},{4,20},{20... | collective-permute-start | bytes 2727944 | tf_op jit(solution)/shard_map/ppermute | solution.py:636
  31.9 8.4 %collective-permute-start.6 = (bf16[96,1152]{1,0:T(8,128)(2,1)S(1)}, bf16[96,1152]{1,0:T(8,128)(2,1)S(1)}, u32[]{:S(2)}, u32[]{:S(2)}) collective-permute-start(bf16[96,1152]{1,0:T(8,128)(2,1)S(1)} %get-tuple-element.84.refs_3_), channel_id=1, source_target_pairs={{0,1},{1,0},{2,3},{3,2},{4,5},{5,4},{6,7},{7,6},{8,9},{9,8},{10,11... | collective-permute-start | bytes 663560 | tf_op jit(solution)/shard_map/ppermute | solution.py:640
  32.4 9.8 %collective-permute-start.7 = (bf16[96,1152]{1,0:T(8,128)(2,1)S(1)}, bf16[96,1152]{1,0:T(8,128)(2,1)S(1)}, u32[]{:S(2)}, u32[]{:S(2)}) collective-permute-start(bf16[96,1152]{1,0:T(8,128)(2,1)S(1)} %get-tuple-element.84.refs_3_), channel_id=1, source_target_pairs={{0,2},{1,3},{2,0},{3,1},{4,6},{5,7},{6,4},{7,5},{8,10},{9,11},{10,... | collective-permute-start | bytes 663560 | tf_op jit(solution)/shard_map/ppermute | solution.py:640
  34.0 11.6 %collective-permute-start.10 = (bf16[96,1152]{1,0:T(8,128)(2,1)S(1)}, bf16[96,1152]{1,0:T(8,128)(2,1)S(1)}, u32[]{:S(2)}, u32[]{:S(2)}) collective-permute-start(bf16[96,1152]{1,0:T(8,128)(2,1)S(1)} %get-tuple-element.84.refs_3_), channel_id=1, source_target_pairs={{0,3},{1,2},{2,1},{3,0},{4,7},{5,6},{6,5},{7,4},{8,11},{9,10},{10,... | collective-permute-start | bytes 663560 | tf_op jit(solution)/shard_map/ppermute | solution.py:640
  35.5 10.1 %collective-permute-start.14 = (bf16[96,1152]{1,0:T(8,128)(2,1)S(1)}, bf16[96,1152]{1,0:T(8,128)(2,1)S(1)}, u32[]{:S(2)}, u32[]{:S(2)}) collective-permute-start(bf16[96,1152]{1,0:T(8,128)(2,1)S(1)} %get-tuple-element.84.refs_3_), channel_id=1, source_target_pairs={{0,16},{16,0},{1,17},{17,1},{2,18},{18,2},{3,19},{19,3},{4,20},{20... | collective-permute-start | bytes 663560 | tf_op jit(solution)/shard_map/ppermute | solution.py:636
  40.3 7.6 %collective-permute-start.8 = (bf16[96,1152]{1,0:T(8,128)(2,1)S(1)}, bf16[96,1152]{1,0:T(8,128)(2,1)S(1)}, u32[]{:S(2)}, u32[]{:S(2)}) collective-permute-start(bf16[96,1152]{1,0:T(8,128)(2,1)S(1)} %slice_bitcast_fusion.1), channel_id=1, source_target_pairs={{0,1},{1,0},{2,3},{3,2},{4,5},{5,4},{6,7},{7,6},{8,9},{9,8},{10,11... | collective-permute-start | bytes 663560 | tf_op jit(solution)/shard_map/ppermute | solution.py:640
  73.3 13.3 %collective-permute-start.24 = (bf16[2,2,48,1280]{3,2,1,0:T(8,128)(2,1)S(1)}, bf16[2,2,48,1280]{3,2,1,0:T(8,128)(2,1)S(1)}, u32[]{:S(2)}, u32[]{:S(2)}) collective-permute-start(bf16[2,2,48,1280]{3,2,1,0:T(8,128)(2,1)S(1)} %get-tuple-element.90), channel_id=1, source_target_pairs={{0,1},{1,0},{2,3},{3,2},{4,5},{5,4},{6,7},{7,6},{8,9},{9,8},{10,11... | collective-permute-start | bytes 1474568 | tf_op jit(solution)/shard_map/ppermute | solution.py:640
  74.5 13.3 %collective-permute-start.25 = (bf16[2,2,48,1280]{3,2,1,0:T(8,128)(2,1)S(1)}, bf16[2,2,48,1280]{3,2,1,0:T(8,128)(2,1)S(1)}, u32[]{:S(2)}, u32[]{:S(2)}) collective-permute-start(bf16[2,2,48,1280]{3,2,1,0:T(8,128)(2,1)S(1)} %get-tuple-element.91), channel_id=1, source_target_pairs={{0,2},{1,3},{2,0},{3,1},{4,6},{5,7},{6,4},{7,5},{8,10},{9,11},{10,... | collective-permute-start | bytes 1474568 | tf_op jit(solution)/shard_map/ppermute | solution.py:640
  94.1 25.5 %collective-permute-start.31 = (bf16[2,2,48,1280]{3,2,1,0:T(8,128)(2,1)S(1)}, bf16[2,2,48,1280]{3,2,1,0:T(8,128)(2,1)S(1)}, u32[]{:S(2)}, u32[]{:S(2)}) collective-permute-start(bf16[2,2,48,1280]{3,2,1,0:T(8,128)(2,1)S(1)} %get-tuple-element.115), channel_id=1, source_target_pairs={{0,2},{1,3},{2,0},{3,1},{4,6},{5,7},{6,4},{7,5},{8,10},{9,11},{10,... | collective-permute-start | bytes 1474568 | tf_op jit(solution)/shard_map/ppermute | solution.py:640
  95.9 24.1 %collective-permute-start.28 = (bf16[2,2,48,1280]{3,2,1,0:T(8,128)(2,1)S(1)}, bf16[2,2,48,1280]{3,2,1,0:T(8,128)(2,1)S(1)}, u32[]{:S(2)}, u32[]{:S(2)}) collective-permute-start(bf16[2,2,48,1280]{3,2,1,0:T(8,128)(2,1)S(1)} %get-tuple-element.111), channel_id=1, source_target_pairs={{0,1},{1,0},{2,3},{3,2},{4,5},{5,4},{6,7},{7,6},{8,9},{9,8},{10,11... | collective-permute-start | bytes 1474568 | tf_op jit(solution)/shard_map/ppermute | solution.py:640
  96.3 37.9 %collective-permute-start.22 = (bf16[197,384]{1,0:T(8,128)(2,1)S(1)}, bf16[197,384]{1,0:T(8,128)(2,1)S(1)}, u32[]{:S(2)}, u32[]{:S(2)}) collective-permute-start(bf16[197,384]{1,0:T(8,128)(2,1)S(1)} %broadcast_select_fusion), channel_id=1, source_target_pairs={{0,16},{16,0},{1,17},{17,1},{2,18},{18,2},{3,19},{19,3},{4,20},{20... | collective-permute-start | bytes 453896 | tf_op jit(solution)/shard_map/ppermute | solution.py:636
  96.5 17.7 %collective-permute-start.44 = (bf16[2,48,1280]{2,1,0:T(8,128)(2,1)S(1)}, bf16[2,48,1280]{2,1,0:T(8,128)(2,1)S(1)}, u32[]{:S(2)}, u32[]{:S(2)}) collective-permute-start(bf16[2,48,1280]{2,1,0:T(8,128)(2,1)S(1)} %relay.7), channel_id=1, source_target_pairs={{0,1},{1,0},{2,3},{3,2},{4,5},{5,4},{6,7},{7,6},{8,9},{9,8},{10,11... | collective-permute-start | bytes 737288 | tf_op jit(solution)/shard_map/ppermute | solution.py:640
  98.2 16.1 %collective-permute-start.42 = (bf16[2,48,1280]{2,1,0:T(8,128)(2,1)S(1)}, bf16[2,48,1280]{2,1,0:T(8,128)(2,1)S(1)}, u32[]{:S(2)}, u32[]{:S(2)}) collective-permute-start(bf16[2,48,1280]{2,1,0:T(8,128)(2,1)S(1)} %relay.6), channel_id=1, source_target_pairs={{0,2},{1,3},{2,0},{3,1},{4,6},{5,7},{6,4},{7,5},{8,10},{9,11},{10,... | collective-permute-start | bytes 737288 | tf_op jit(solution)/shard_map/ppermute | solution.py:640
  114.2 12.9 %collective-permute-start.45 = (bf16[48,1280]{1,0:T(8,128)(2,1)S(1)}, bf16[48,1280]{1,0:T(8,128)(2,1)S(1)}, u32[]{:S(2)}, u32[]{:S(2)}) collective-permute-start(bf16[48,1280]{1,0:T(8,128)(2,1)S(1)} %get-tuple-element.123), channel_id=1, source_target_pairs={{0,8},{4,12},{8,0},{12,4},{1,9},{5,13},{9,1},{13,5},{2,10},{6,14},... | collective-permute-start | bytes 368648 | tf_op jit(solution)/shard_map/ppermute | solution.py:644
  114.3 15.8 %collective-permute-start.46 = (bf16[48,1280]{1,0:T(8,128)(2,1)S(1)}, bf16[48,1280]{1,0:T(8,128)(2,1)S(1)}, u32[]{:S(2)}, u32[]{:S(2)}) collective-permute-start(bf16[48,1280]{1,0:T(8,128)(2,1)S(1)} %get-tuple-element.124), channel_id=1, source_target_pairs={{0,12},{4,0},{8,4},{12,8},{1,13},{5,1},{9,5},{13,9},{2,14},{6,2},{... | collective-permute-start | bytes 368648 | tf_op jit(solution)/shard_map/ppermute | solution.py:644
  119.6 6.4 %collective-permute-start.32 = (bf16[2,48,1280]{2,1,0:T(8,128)(2,1)S(1)}, bf16[2,48,1280]{2,1,0:T(8,128)(2,1)S(1)}, u32[]{:S(2)}, u32[]{:S(2)}) collective-permute-start(bf16[2,48,1280]{2,1,0:T(8,128)(2,1)S(1)} %relay.5), channel_id=1, source_target_pairs={{0,1},{1,0},{2,3},{3,2},{4,5},{5,4},{6,7},{7,6},{8,9},{9,8},{10,11... | collective-permute-start | bytes 737288 | tf_op jit(solution)/shard_map/ppermute | solution.py:640
  120.0 6.3 %collective-permute-start.29 = (bf16[2,48,1280]{2,1,0:T(8,128)(2,1)S(1)}, bf16[2,48,1280]{2,1,0:T(8,128)(2,1)S(1)}, u32[]{:S(2)}, u32[]{:S(2)}) collective-permute-start(bf16[2,48,1280]{2,1,0:T(8,128)(2,1)S(1)} %relay.4), channel_id=1, source_target_pairs={{0,2},{1,3},{2,0},{3,1},{4,6},{5,7},{6,4},{7,5},{8,10},{9,11},{10,... | collective-permute-start | bytes 737288 | tf_op jit(solution)/shard_map/ppermute | solution.py:640
  126.0 8.2 %collective-permute-start.43 = (bf16[48,1280]{1,0:T(8,128)(2,1)S(1)}, bf16[48,1280]{1,0:T(8,128)(2,1)S(1)}, u32[]{:S(2)}, u32[]{:S(2)}) collective-permute-start(bf16[48,1280]{1,0:T(8,128)(2,1)S(1)} %get-tuple-element.121), channel_id=1, source_target_pairs={{0,4},{4,8},{8,12},{12,0},{1,5},{5,9},{9,13},{13,1},{2,6},{6,10},{... | collective-permute-start | bytes 368648 | tf_op jit(solution)/shard_map/ppermute | solution.py:644
  126.3 12.4 %collective-permute-start.33 = (bf16[48,1280]{1,0:T(8,128)(2,1)S(1)}, bf16[48,1280]{1,0:T(8,128)(2,1)S(1)}, u32[]{:S(2)}, u32[]{:S(2)}) collective-permute-start(bf16[48,1280]{1,0:T(8,128)(2,1)S(1)} %get-tuple-element.117), channel_id=1, source_target_pairs={{0,8},{4,12},{8,0},{12,4},{1,9},{5,13},{9,1},{13,5},{2,10},{6,14},... | collective-permute-start | bytes 368648 | tf_op jit(solution)/shard_map/ppermute | solution.py:644
  127.1 11.6 %collective-permute-start.34 = (bf16[48,1280]{1,0:T(8,128)(2,1)S(1)}, bf16[48,1280]{1,0:T(8,128)(2,1)S(1)}, u32[]{:S(2)}, u32[]{:S(2)}) collective-permute-start(bf16[48,1280]{1,0:T(8,128)(2,1)S(1)} %get-tuple-element.118), channel_id=1, source_target_pairs={{0,12},{4,0},{8,4},{12,8},{1,13},{5,1},{9,5},{13,9},{2,14},{6,2},{... | collective-permute-start | bytes 368648 | tf_op jit(solution)/shard_map/ppermute | solution.py:644
  130.1 11.3 %collective-permute-start.30 = (bf16[48,1280]{1,0:T(8,128)(2,1)S(1)}, bf16[48,1280]{1,0:T(8,128)(2,1)S(1)}, u32[]{:S(2)}, u32[]{:S(2)}) collective-permute-start(bf16[48,1280]{1,0:T(8,128)(2,1)S(1)} %get-tuple-element.114), channel_id=1, source_target_pairs={{0,4},{4,8},{8,12},{12,0},{1,5},{5,9},{9,13},{13,1},{2,6},{6,10},{... | collective-permute-start | bytes 368648 | tf_op jit(solution)/shard_map/ppermute | solution.py:644
  134.2 8.4 %collective-permute-start.26 = (f32[197,384]{1,0:T(8,128)S(1)}, f32[197,384]{1,0:T(8,128)S(1)}, u32[]{:S(2)}, u32[]{:S(2)}) collective-permute-start(f32[197,384]{1,0:T(8,128)S(1)} %convert_select_fusion.1), channel_id=1, source_target_pairs={{0,16},{16,0},{1,17},{17,1},{2,18},{18,2},{3,19},{19,3},{4,20},{20... | collective-permute-start | bytes 907784 | tf_op jit(solution)/shard_map/ppermute | solution.py:636
  134.3 9.1 %collective-permute-start.48 = (bf16[48,1280]{1,0:T(8,128)(2,1)S(1)}, bf16[48,1280]{1,0:T(8,128)(2,1)S(1)}, u32[]{:S(2)}, u32[]{:S(2)}) collective-permute-start(bf16[48,1280]{1,0:T(8,128)(2,1)S(1)} %sum_of_column.3.refs_8_), channel_id=1, source_target_pairs={{0,1},{1,0},{2,3},{3,2},{4,5},{5,4},{6,7},{7,6},{8,9},{9,8},{10,11... | collective-permute-start | bytes 368648 | tf_op jit(solution)/shard_map/ppermute | solution.py:640
  138.7 7.4 %collective-permute-start.52 = (bf16[48,1280]{1,0:T(8,128)(2,1)S(1)}, bf16[48,1280]{1,0:T(8,128)(2,1)S(1)}, u32[]{:S(2)}, u32[]{:S(2)}) collective-permute-start(bf16[48,1280]{1,0:T(8,128)(2,1)S(1)} %sum_of_column.3.refs_8_), channel_id=1, source_target_pairs={{0,3},{1,2},{2,1},{3,0},{4,7},{5,6},{6,5},{7,4},{8,11},{9,10},{10,... | collective-permute-start | bytes 368648 | tf_op jit(solution)/shard_map/ppermute | solution.py:640
  143.4 8.1 %collective-permute-start.38 = (bf16[48,1280]{1,0:T(8,128)(2,1)S(1)}, bf16[48,1280]{1,0:T(8,128)(2,1)S(1)}, u32[]{:S(2)}, u32[]{:S(2)}) collective-permute-start(bf16[48,1280]{1,0:T(8,128)(2,1)S(1)} %sum_of_column.2.refs_0_), channel_id=1, source_target_pairs={{0,2},{1,3},{2,0},{3,1},{4,6},{5,7},{6,4},{7,5},{8,10},{9,11},{10,... | collective-permute-start | bytes 368648 | tf_op jit(solution)/shard_map/ppermute | solution.py:640
  144.9 6.6 %collective-permute-start.40 = (bf16[48,1280]{1,0:T(8,128)(2,1)S(1)}, bf16[48,1280]{1,0:T(8,128)(2,1)S(1)}, u32[]{:S(2)}, u32[]{:S(2)}) collective-permute-start(bf16[48,1280]{1,0:T(8,128)(2,1)S(1)} %sum_of_column.2.refs_0_), channel_id=1, source_target_pairs={{0,3},{1,2},{2,1},{3,0},{4,7},{5,6},{6,5},{7,4},{8,11},{9,10},{10,... | collective-permute-start | bytes 368648 | tf_op jit(solution)/shard_map/ppermute | solution.py:640
  (36 other events, 340.8 us)

commit v3 on v2

--- a/solution.py
+++ b/solution.py
@@ -303,8 +303,8 @@
     patches, cotangent, live = refs[22:25]
     refs = refs[25:]
     (
-        out_one,
-        out_two,
+        out_mine,
+        out_other,
         grad_one,
         keep,
         send,
@@ -355,14 +355,30 @@
     for index in range(6):
         save.append(pltpu.make_async_copy(acts0[index], kept_acts[index], out_sems.at[3 + index]))
         save[-1].start()
-    out_one[...] = result[:seq].astype(BF16)
     live_rows = lax.broadcasted_iota(jnp.int32, (SEQ_ROWS, width), 0) < seq
     rows_mid[...] = jnp.where(live_rows, result.astype(BF16).astype(F32), 0.0)
 
+    @pl.when(section == 0)
+    def _():
+        out_mine[...] = rows_mid[:seq].astype(BF16)
+
+    @pl.when(section == 1)
+    def _():
+        out_other[...] = rows_mid[:seq].astype(BF16)
+
     weights1, vec1, bias_up1 = ready(1)
     result = layer_forward(rows_mid[...], seq, weights1, vec1, bias_up1, acts1)
-    out_two[...] = result[:seq].astype(BF16)
-
+    rows_in[...] = result
+
+    @pl.when(section == 1)
+    def _():
+        out_mine[...] = rows_in[:seq].astype(BF16)
+
+    @pl.when(section == 0)
+    def _():
+        out_other[...] = rows_in[:seq].astype(BF16)
+
+    rows_in[seq - seq % 8 :] = jnp.zeros((SEQ_ROWS - seq + seq % 8, width), F32)
     rows_in[:seq] = cotangent[section].astype(F32) * live[section].astype(F32)
     put = PackedPut(grads, shard, replica)
     grad_x = layer_backward(
@@ -382,9 +398,9 @@
 def last_kernel(seq, *refs):
     weights, vectors_in, grad_one, patches = refs[0:4]
     saved = refs[4:10]
-    grad_out, keep, send = refs[10:13]
-    packed, down, rows_in, rows_grad, up_grad, qkv_grad, grads, sems, out_sems = refs[13:22]
-    acts = refs[22:28]
+    grad_mine, grad_other, keep, send = refs[10:14]
+    packed, down, rows_in, rows_grad, up_grad, qkv_grad, grads, sems, out_sems = refs[14:23]
+    acts = refs[23:29]
     section, shard, replica = positions()
     loads = [pltpu.make_async_copy(weights, packed, sems.at[6])]
     for index in range(6):
@@ -415,13 +431,24 @@
         qkv_grad,
         put,
     )
-    grad_out[...] = grad_x[:seq]
     copies = [
         pltpu.make_async_copy(grads.at[section], keep, out_sems.at[0]),
         pltpu.make_async_copy(grads.at[1 - section], send, out_sems.at[1]),
     ]
     for copy in copies:
         copy.start()
+    rows_in[...] = grad_x
+
+    @pl.when(section == 0)
+    def _():
+        grad_mine[...] = rows_in[:seq]
+        grad_other[...] = grad_one[...].astype(F32)
+
+    @pl.when(section == 1)
+    def _():
+        grad_mine[...] = grad_one[...].astype(F32)
+        grad_other[...] = rows_in[:seq]
+
     for copy in copies:
         copy.wait()
 
@@ -496,11 +523,12 @@
         functools.partial(last_kernel, seq),
         out_shape=[
             shape((seq, width), F32),
+            shape((seq, width), F32),
             shape((4, 4, HALF, PIECE), BF16),
             shape((4, 4, HALF, PIECE), BF16),
         ],
         in_specs=anywhere(1) + vmem(3) + anywhere(6),
-        out_specs=vmem(1) + anywhere(2),
+        out_specs=vmem(2) + anywhere(2),
         scratch_shapes=[
             pltpu.VMEM((1, 4, ROWS, PACKED), BF16),
             pltpu.VMEM((1, wide, width), BF16),
@@ -546,18 +574,52 @@
         y_late[place] = add(keep[2, place], recv[2, place]).astype(BF16)
 
 
+def whole_sum_kernel(keep, recv, to_x, to_y, own, opposite):
+    for place in range(4):
+        own[place] = add(keep[0, place], recv[0, place]).astype(BF16)
+        to_x[place] = add(keep[1, place], recv[1, place]).astype(BF16)
+        to_y[place] = add(keep[2, place], recv[2, place]).astype(BF16)
+        opposite[place] = add(keep[3, place], recv[3, place]).astype(BF16)
+
+
+def whole_plane_kernel(own, got_x, got_y, opposite, out):
+    shard = lax.axis_index("shard")
+    for place in range(4):
+        owner = lax.rem(shard + place, 4)
+        value = add(own[place], got_x[place]) + got_y[place].astype(F32)
+        out[owner, 0] = value.astype(BF16)
+        out[owner, 1] = opposite[place]
+
+
+def pair_column_kernel(parts, out):
+    for index in range(2):
+        value = add(parts[0, index], parts[1, index]) + add(parts[2, index], parts[3, index])
+        out[index] = value.astype(BF16)
+
+
+def join_kernel(*refs):
+    pieces, outs = refs[:8], refs[8:]
+    for bits in range(4):
+        for half in range(2):
+            value = add(pieces[2 * bits + half][0], pieces[2 * (3 - bits) + half][1])
+            outs[2 * bits + half][...] = value.astype(BF16)
+
+
 def relay_kernel(late, got, out):
     for place in range(2):
         out[place] = add(late[place], got[1, place]).astype(BF16)
 
 
-def plane_sum_kernel(own, got, late, one, two):
-    for place, out in enumerate((one, two)):
-        out[...] = (add(own[place], got[0, place]) + late[place].astype(F32)).astype(BF16)
-
-
-def column_sum_kernel(a, b, c, d, out):
-    out[...] = (add(a[...], b[...]) + add(c[...], d[...])).astype(BF16)
+def plane_sum_kernel(own, got_x, got_y, late_y, late_x, out):
+    shard = lax.axis_index("shard")
+    for first, got, late in ((0, got_x, late_y), (2, got_y, late_x)):
+        for place in range(2):
+            value = add(own[first + place], got[0, place]) + late[place].astype(F32)
+            out[lax.rem(shard + first + place, 4)] = value.astype(BF16)
+
+
+def column_sum_kernel(parts, out):
+    out[...] = (add(parts[0], parts[1]) + add(parts[2], parts[3])).astype(BF16)
 
 
 def unpack_kernel(*refs):
@@ -566,7 +628,7 @@
     table, sems = refs[29:]
     section, _, replica = positions()
 
-    def copies_of(pieces):
+    def copies_of(pieces, target):
         copies = []
         for bits in range(4):
             place = lax.bitwise_xor(replica, bits)
@@ -574,7 +636,7 @@
                 where = section if half == 0 else 1 - section
                 index = 2 * bits + half
                 copies.append(
-                    pltpu.make_async_copy(pieces[index], table.at[place, where], sems.at[index])
+                    pltpu.make_async_copy(pieces[index], target.at[place, where], sems.at[index])
                 )
         return copies
 
@@ -582,9 +644,9 @@
 
         @pl.when(section == layer)
         def _(pieces=pieces):
-            for copy in copies_of(pieces):
+            for copy in copies_of(pieces, table):
                 copy.start()
-            for copy in copies_of(pieces):
+            for copy in copies_of(pieces, table):
                 copy.wait()
 
     def put(target, row, column, start, count, at):
@@ -734,32 +796,52 @@
     tiles[2, HALF:] = lower[:, QUARTER:]
 
 
-def exchange_plane(to_x, to_y, own, x_late, y_late, got_x, got_y):
-    half, piece = x_late.shape, x_late.shape[1:]
+def relay(parts, got_x, got_y):
+    _, _, own, x_late, y_late = parts
+    half = x_late.shape
     (y_send,) = small_call(relay_kernel, [half], "relay", y_late, got_x)
     (x_send,) = small_call(relay_kernel, [half], "relay", x_late, got_y)
-    late_y, late_x = flip(y_send, 2), flip(x_send, 1)
-    zero, one = small_call(plane_sum_kernel, [piece] * 2, "sum_of_plane", own[:2], got_x, late_y)
-    two, three = small_call(plane_sum_kernel, [piece] * 2, "sum_of_plane", own[2:], got_y, late_x)
-    column = small_call(
-        column_sum_kernel,
-        [piece],
-        "sum_of_column",
-        zero,
-        shift(one, 1),
-        shift(two, 2),
-        shift(three, 3),
-    )[0]
-    return column, late_x, late_y
+    return flip(y_send, 2), flip(x_send, 1)
+
+
+def sum_column(parts):
+    return small_call(column_sum_kernel, [parts.shape[1:]], "sum_of_column", parts)[0]
 
 
 def spread(value):
-    pieces = [value] + [flip(value, bits) for bits in (1, 2, 3)]
+    return [value] + [flip(value, bits) for bits in (1, 2, 3)]
+
+
+def both_halves(pieces):
     return [member for piece in pieces for member in (piece, swap(piece))]
 
 
+def rows_kernel(out_mine, out_other, grad_mine, grad_other, outs, grads):
+    section = lax.axis_index("section")
+    for slot in range(2):
+
+        @pl.when(section == slot)
+        def _(slot=slot):
+            outs[:, slot, :] = out_mine[...].astype(F32).astype(BF16)
+            outs[:, 1 - slot, :] = out_other[...]
+            grads[:, slot, :] = grad_mine[...]
+            grads[:, 1 - slot, :] = grad_other[...]
+
+
+def rows_of_slots(out_mine, out_other, grad_mine, grad_other):
+    seq, width = out_mine.shape
+    outs, grads = pl.pallas_call(
+        rows_kernel,
+        out_shape=[shape((seq, 2, width), BF16), shape((seq, 2, width), F32)],
+        in_specs=vmem(4),
+        out_specs=vmem(2),
+        compiler_params=grant(12),
+        name="rows_of_slots",
+    )(out_mine, out_other, grad_mine, grad_other)
+    return outs, grads
+
+
 def packed_local(patches, live_slots, cotangent, w_qkv, w_out, w_up, w_down, *small):
-    section, _, _ = positions()
     width, wide = w_out.shape[2], w_up.shape[2]
     bias_q, bias_v, bias_out, bias_up, bias_down, gain_one, offset_one, gain_two, offset_two = small
     vectors = (bias_q, bias_v, bias_out, bias_down, gain_one, offset_one, gain_two, offset_two)
@@ -779,37 +861,48 @@
         shift(upper, 1),
         shift(lower, 3),
     )
-    d_first, d_third = flip(y_near[0], 1), flip(x_near[1], 2)
-    far = after(far, x_near, y_near)
-    x_far, y_far, d_far = (flip(far, bits) for bits in (1, 2, 3))
+    far_now, x_now, y_now = lax.optimization_barrier((far, x_near, y_near))
+    x_far, y_far, d_far = (flip(far_now, bits) for bits in (1, 2, 3))
+    d_first, d_third = flip(y_now[0], 1), flip(x_now[1], 2)
     mine = [own, tiles, near, far, x_near, x_far, y_near, y_far, d_first, d_third, d_far]
     other = [swap(member) for member in mine]
 
-    (out_one, out_two, grad_one, keep1, send1, kept, vectors, *acts) = run_main(
+    (out_mine, out_other, grad_one, keep1, send1, kept, vectors, *acts) = run_main(
         mine, other, patches, cotangent, live_slots, wide
     )
-    parts = reduce_plane(keep1, send1)
-    got = (flip(parts[0], 1), flip(parts[1], 2))
-    last = run_last(after(kept, *parts), vectors, grad_one, patches, acts, wide)
-    grad_zero, keep0, send0, *got = lax.optimization_barrier((*last, *got))
-    one, *_ = exchange_plane(*parts, *got)
-    parts = reduce_plane(keep0, send0)
-    zero, *late = exchange_plane(*parts, flip(parts[0], 1), flip(parts[1], 2))
-    one = spread(after(one, *late))
-    zero = spread(zero)
-    grad_qkv, grad_out, grad_up, grad_down, *rest = unpack(zero, one, width, wide)
-
-    first = section == 0
-    out_send = jnp.where(first, out_two, out_one)
-    out_recv = swap(out_send)
-    layer_outputs = jnp.stack(
-        [jnp.where(first, out_one, out_recv), jnp.where(first, out_recv, out_two)]
-    )[None]
-    grad_one32 = grad_one.astype(F32)
-    grad_recv = swap(jnp.where(first, grad_one32, grad_zero))
-    input_grads = jnp.stack(
-        [jnp.where(first, grad_zero, grad_recv), jnp.where(first, grad_recv, grad_one32)]
-    )[None]
+    whole, piece = keep1.shape[1:], keep1.shape[2:]
+    to_x, to_y, own1, opposite = small_call(
+        whole_sum_kernel, [whole] * 4, "sum_of_cores", keep1, swap(send1)
+    )
+    got1 = (flip(to_x, 1), flip(to_y, 2))
+    kept = after(kept, to_x, to_y, own1, opposite)
+    last = run_last(kept, vectors, grad_one, patches, acts, wide)
+    grad_mine, grad_other, keep0, send0, *got1 = lax.optimization_barrier((*last, *got1))
+    (sums1,) = small_call(
+        whole_plane_kernel, [(4, 2) + piece], "sum_of_plane", own1, *got1, opposite
+    )
+    column1 = lax.all_to_all(sums1, "shard", 0, 0, tiled=True)
+    parts0 = reduce_plane(after(keep0, sums1), send0)
+    got0 = (flip(parts0[0], 1), flip(parts0[1], 2))
+    rows = rows_of_slots(out_mine, swap(out_other), grad_mine, swap(grad_other))
+    *got0, outs, grads = lax.optimization_barrier((*got0, *rows))
+    layer_outputs, input_grads = outs.transpose(1, 0, 2)[None], grads.transpose(1, 0, 2)[None]
+    late0 = relay(parts0, *got0)
+    (sums0,) = small_call(
+        plane_sum_kernel, [parts0[2].shape], "sum_of_plane", parts0[2], *got0, *late0
+    )
+    column0 = lax.all_to_all(sums0, "shard", 0, 0, tiled=True)
+    (one,) = small_call(
+        pair_column_kernel, [(2,) + piece], "sum_of_column", after(column1, sums0)
+    )
+    one = spread(one)
+    column0 = after(column0, *one[1:])
+    zero = spread(sum_column(column0))
+    one = small_call(join_kernel, [piece] * 8, "join", *both_halves(one))
+    grad_qkv, grad_out, grad_up, grad_down, *rest = unpack(
+        both_halves(zero), one, width, wide
+    )
+
     (g_q, g_v, g_o, g_d, g_g1, g_o1, g_g2, g_o2, g_up) = rest
     return (
         layer_outputs,

time: 156 us -> 150 us (0.962)
  waiting for transfers between devices: 73.8 us -> 65.8 us
  Pallas kernels: 32.8 us -> 36.6 us
  local copies, waits for them, and re-layouts: 3.78 us -> 0.86 us
    ppermute x10 -> x4, starting transfers between devices: 18.5 us -> 8.93 us  [shift(): lax.ppermute(value, 'shard', [(place, (place + steps) % 4) for place in r...]
    all_to_all x0 -> x2, starting transfers between devices: none -> 7.95 us  [the longest x1 4.44 us: packed_local(): column0 = lax.all_to_all(sums0, 'shard', 0, 0, tiled=True)]
    ppermute x10 -> x4, waiting for transfers between devices: 22.6 us -> 15.6 us  [shift(): lax.ppermute(value, 'shard', [(place, (place + steps) % 4) for place in r...]
    ppermute x23, waiting for transfers between devices: 10.8 us -> 7.17 us  [swap(): return lax.ppermute(value, 'section', [(0, 1), (1, 0)])]
    ppermute x21 -> x19, starting transfers between devices: 22.4 us -> 25.5 us  [flip(): lax.ppermute(value, 'replica', [(place, place ^ bits) for place in range(...]
    unnamed x32 -> x18, local copies, waits for them, and re-layouts: 3.68 us -> 0.82 us
    ppermute x21 -> x19, waiting for transfers between devices: 40.4 us -> 43 us  [flip(): lax.ppermute(value, 'replica', [(place, place ^ bits) for place in range(...]
    pallas_call x14 -> x11, Pallas kernels: 3.25 us -> 5.22 us  [small_call(): pl.pallas_call(kernel, out_shape=[shape(dims, BF16) for dims in outs], in...]
  transfers between devices with their start and end apart: 54 -> 48, of which waited for: 27 -> 30; matrix products, arithmetic and copies ran while one was open for 2% -> 0% of each run, Pallas kernels for 6% -> 10%
where the time goes in v3:
time: 150 us
  waiting for transfers between devices  65.8 us (44%)
  starting transfers between devices  45.4 us (30%)
  Pallas kernels  36.6 us (24%)
    ppermute x19, waiting for transfers between devices, flip(): lax.ppermute(value, 'replica', [(place, place ^ bits) for place in range(...  43 us
    ppermute x19, starting transfers between devices, flip(): lax.ppermute(value, 'replica', [(place, place ^ bits) for place in range(...  25.5 us
    pallas_call x1, Pallas kernels, run_main(): pl.pallas_call(functools.partial(main_kernel, seq), out_shape=[shape((seq...  16.5 us
    ppermute x4, waiting for transfers between devices, shift(): lax.ppermute(value, 'shard', [(place, (place + steps) % 4) for place in r...  15.6 us
    ppermute x4, starting transfers between devices, shift(): lax.ppermute(value, 'shard', [(place, (place + steps) % 4) for place in r...  8.93 us
    pallas_call x1, Pallas kernels, run_last(): pl.pallas_call(functools.partial(last_kernel, seq), out_shape=[shape((seq...  8.1 us
    ppermute x23, waiting for transfers between devices, swap(): return lax.ppermute(value, 'section', [(0, 1), (1, 0)])  7.17 us
    pallas_call x11, Pallas kernels, small_call(): pl.pallas_call(kernel, out_shape=[shape(dims, BF16) for dims in outs], in...  5.22 us
  transfers between devices with their start and end apart: 48, of which 30 were waited for; matrix products, arithmetic and copies ran while one was open for 0% of the time, Pallas kernels for 10%

profile of v3, /device:TPU:0, one launch (start us, length us, event | category | flops | bytes accessed | tf_op | source)
XLA Modules:
  0.0 149.6 jit_solution(5821360100730859045)
XLA Ops:
  0.7 2.4 %pack.1 = (bf16[96,4736]{1,0:T(8,128)(2,1)}, bf16[96,1280]{1,0:T(8,128)(2,1)}) custom-call(bf16[1,96,1536]{2,1,0:T(8,128)(2,1)} %refs_0_.1, bf16[1,96,1152]{2,1,0:T(8,128)(2,1)} %refs_1_.1, bf16[1,96,384]{2,1,0:T(8,128)(2,1)} %refs_2_.1, bf16[1,384,384]{2,1,0:T(8,128)(2,1)} %refs_3_.2, f32[1,96]{1,0:T(1,128)} %refs_4_.1, f32[1,96]{1,0:T(1,128)} %refs_5_.1, ...), custom_call_target="tpu_custom_call" | custom-call | tf_op jit(solution)/shard_map/pack/pallas_call | solution.py:751
  3.1 5.1 %collective-permute-start.1 = (bf16[96,1280]{1,0:T(8,128)(2,1)}, bf16[96,1280]{1,0:T(8,128)(2,1)S(1)}, u32[]{:S(2)}, u32[]{:S(2)}) collective-permute-start(bf16[96,1280]{1,0:T(8,128)(2,1)} %get-tuple-element.89), channel_id=1, source_target_pairs={{0,12},{4,0},{8,4},{12,8},{1,13},{5,1},{9,5},{13,9},{2,14},{6,2},{... | collective-permute-start | bytes 737288 | tf_op jit(solution)/shard_map/ppermute | solution.py:706
  8.2 6.7 %collective-permute-done.1.third = bf16[96,1280]{1,0:T(8,128)(2,1)S(1)} collective-permute-done((bf16[96,1280]{1,0:T(8,128)(2,1)}, bf16[96,1280]{1,0:T(8,128)(2,1)S(1)}, u32[]{:S(2)}, u32[]{:S(2)}) %collective-permute-start.1) | collective-permute-done | bytes 245792 | tf_op jit(solution)/shard_map/ppermute | solution.py:706
  14.9 4.9 %collective-permute-done.first = bf16[96,1280]{1,0:T(8,128)(2,1)S(1)} collective-permute-done((bf16[96,1280]{1,0:T(8,128)(2,1)}, bf16[96,1280]{1,0:T(8,128)(2,1)S(1)}, u32[]{:S(2)}, u32[]{:S(2)}) %collective-permute-start) | collective-permute-done | bytes 245792 | tf_op jit(solution)/shard_map/ppermute | solution.py:706
  19.9 1.6 %collective-permute-start.5 = (bf16[2,96,1152]{2,1,0:T(8,128)(2,1)S(1)}, bf16[2,96,1152]{2,1,0:T(8,128)(2,1)S(1)}, u32[]{:S(2)}, u32[]{:S(2)}) collective-permute-start(bf16[2,96,1152]{2,1,0:T(8,128)(2,1)S(1)} %get-tuple-element.93.refs_2_), channel_id=1, source_target_pairs={{0,2},{1,3},{2,0},{3,1},{4,6},{5,7},{6,4},{7,5},{8,10},{9,11},{10,... | collective-permute-start | bytes 1327112 | tf_op jit(solution)/shard_map/ppermute | solution.py:702
  21.5 1.5 collective-permute-start.4
  23.0 1.6 %collective-permute-start.2 = (bf16[48,1280]{1,0:T(8,128)(2,1)S(1)}, bf16[48,1280]{1,0:T(8,128)(2,1)S(1)}, u32[]{:S(2)}, u32[]{:S(2)}) collective-permute-start(bf16[48,1280]{1,0:T(8,128)(2,1)S(1)} %get-tuple-element.90), channel_id=1, source_target_pairs={{0,4},{4,8},{8,12},{12,0},{1,5},{5,9},{9,13},{13,1},{2,6},{6,10},{... | collective-permute-start | bytes 368648 | tf_op jit(solution)/shard_map/ppermute | solution.py:706
  24.6 2.2 %collective-permute-start.3 = (bf16[48,1280]{1,0:T(8,128)(2,1)S(1)}, bf16[48,1280]{1,0:T(8,128)(2,1)S(1)}, u32[]{:S(2)}, u32[]{:S(2)}) collective-permute-start(bf16[48,1280]{1,0:T(8,128)(2,1)S(1)} %get-tuple-element.91), channel_id=1, source_target_pairs={{0,12},{4,0},{8,4},{12,8},{1,13},{5,1},{9,5},{13,9},{2,14},{6,2},{... | collective-permute-start | bytes 368648 | tf_op jit(solution)/shard_map/ppermute | solution.py:706
  26.8 3.1 %collective-permute-done.2.upper = bf16[48,1280]{1,0:T(8,128)(2,1)S(1)} collective-permute-done((bf16[48,1280]{1,0:T(8,128)(2,1)S(1)}, bf16[48,1280]{1,0:T(8,128)(2,1)S(1)}, u32[]{:S(2)}, u32[]{:S(2)}) %collective-permute-start.2) | collective-permute-done | bytes 122912 | tf_op jit(solution)/shard_map/ppermute | solution.py:706
  32.9 1.6 %collective-permute-start.8 = (bf16[96,1152]{1,0:T(8,128)(2,1)S(1)}, bf16[96,1152]{1,0:T(8,128)(2,1)S(1)}, u32[]{:S(2)}, u32[]{:S(2)}) collective-permute-start(bf16[96,1152]{1,0:T(8,128)(2,1)S(1)} %slice_bitcast_fusion.1), channel_id=1, source_target_pairs={{0,1},{1,0},{2,3},{3,2},{4,5},{5,4},{6,7},{7,6},{8,9},{9,8},{10,11... | collective-permute-start | bytes 663560 | tf_op jit(solution)/shard_map/ppermute | solution.py:702
  34.4 1.6 %collective-permute-start.10 = (bf16[96,1152]{1,0:T(8,128)(2,1)S(1)}, bf16[96,1152]{1,0:T(8,128)(2,1)S(1)}, u32[]{:S(2)}, u32[]{:S(2)}) collective-permute-start(bf16[96,1152]{1,0:T(8,128)(2,1)S(1)} %get-tuple-element.95.refs_3_), channel_id=1, source_target_pairs={{0,3},{1,2},{2,1},{3,0},{4,7},{5,6},{6,5},{7,4},{8,11},{9,10},{10,... | collective-permute-start | bytes 663560 | tf_op jit(solution)/shard_map/ppermute | solution.py:702
  36.0 3.4 %collective-permute-done.9.refs_9_ = bf16[96,1152]{1,0:T(8,128)(2,1)S(1)} collective-permute-done((bf16[96,1152]{1,0:T(8,128)(2,1)S(1)}, bf16[96,1152]{1,0:T(8,128)(2,1)S(1)}, u32[]{:S(2)}, u32[]{:S(2)}) %collective-permute-start.9) | collective-permute-done | bytes 221216 | tf_op jit(solution)/shard_map/ppermute | solution.py:702
  42.7 4.0 %collective-permute-done.10.refs_10_ = bf16[96,1152]{1,0:T(8,128)(2,1)S(1)} collective-permute-done((bf16[96,1152]{1,0:T(8,128)(2,1)S(1)}, bf16[96,1152]{1,0:T(8,128)(2,1)S(1)}, u32[]{:S(2)}, u32[]{:S(2)}) %collective-permute-start.10) | collective-permute-done | bytes 221216 | tf_op jit(solution)/shard_map/ppermute | solution.py:702
  46.7 2.3 %collective-permute-done.7.refs_7_ = bf16[96,1152]{1,0:T(8,128)(2,1)S(1)} collective-permute-done((bf16[96,1152]{1,0:T(8,128)(2,1)S(1)}, bf16[96,1152]{1,0:T(8,128)(2,1)S(1)}, u32[]{:S(2)}, u32[]{:S(2)}) %collective-permute-start.7) | collective-permute-done | bytes 221216 | tf_op jit(solution)/shard_map/ppermute | solution.py:702
  52.2 16.5 %forward_and_layer_one.1 = (bf16[197,384]{1,0:T(8,128)(2,1)S(1)}, bf16[197,384]{1,0:T(8,128)(2,1)S(1)}, bf16[197,384]{1,0:T(8,128)(2,1)S(1)}, bf16[4,4,48,1280]{...) custom-call(bf16[96,4736]{1,0:T(8,128)(2,1)S(1)} %copy-done, ...), custom_call_target="tpu_custom_call" | custom-call | tf_op jit(solution)/shard_map/forward_and_layer_one/pallas_call | solution.py:487
  69.0 3.8 %collective-permute-done.22.recv = bf16[4,4,48,1280]{3,2,1,0:T(8,128)(2,1)S(1)} collective-permute-done((bf16[4,4,48,1280]{3,2,1,0:T(8,128)(2,1)S(1)}, bf16[4,4,48,1280]{3,2,1,0:T(8,128)(2,1)S(1)}, u32[]{:S(2)}, u32[]{:S(2)}) %collective-permute-start.22) | collective-permute-done | bytes 1966112 | tf_op jit(solution)/shard_map/ppermute | solution.py:698
  73.3 1.6 %collective-permute-start.23 = (bf16[4,48,1280]{2,1,0:T(8,128)(2,1)S(1)}, bf16[4,48,1280]{2,1,0:T(8,128)(2,1)S(1)}, u32[]{:S(2)}, u32[]{:S(2)}) collective-permute-start(bf16[4,48,1280]{2,1,0:T(8,128)(2,1)S(1)} %get-tuple-element.101), channel_id=1, source_target_pairs={{0,1},{1,0},{2,3},{3,2},{4,5},{5,4},{6,7},{7,6},{8,9},{9,8},{10,11... | collective-permute-start | bytes 1474568 | tf_op jit(solution)/shard_map/ppermute | solution.py:702
  74.8 2.0 %collective-permute-start.24 = (bf16[4,48,1280]{2,1,0:T(8,128)(2,1)S(1)}, bf16[4,48,1280]{2,1,0:T(8,128)(2,1)S(1)}, u32[]{:S(2)}, u32[]{:S(2)}) collective-permute-start(bf16[4,48,1280]{2,1,0:T(8,128)(2,1)S(1)} %get-tuple-element.102), channel_id=1, source_target_pairs={{0,2},{1,3},{2,0},{3,1},{4,6},{5,7},{6,4},{7,5},{8,10},{9,11},{10,... | collective-permute-start | bytes 1474568 | tf_op jit(solution)/shard_map/ppermute | solution.py:702
  76.8 8.1 %layer_zero_backward.1 = (f32[197,384]{1,0:T(8,128)S(1)}, f32[197,384]{1,0:T(8,128)S(1)}, bf16[4,4,48,1280]{3,2,1,0:T(8,128)(2,1)S(1)}, bf16[4,4,48,1280]{3,2,1,0:T(8,128)(2,1)}) custom-call(bf16[1,4,96,4736]{3,2,1,0:T(8,128)(2,1)S(1)} %get-tuple-element.105.refs_0_, f32[8,384]{1,0:T(8,128)S(1)} %get-tuple-element.106.refs_1_, ...), custom_call_target="tpu_custom_call" | custom-call | flops 8000000000 | bytes 8000000 | tf_op jit(solution)/shard_map/layer_zero_backward/pallas_call | solution.py:522
  89.2 3.5 %all-to-all-start.1 = ((bf16[4,2,48,1280]{3,2,1,0:T(8,128)(2,1)}), bf16[4,2,48,1280]{3,2,1,0:T(8,128)(2,1)S(1)}, u32[]{:S(2)}, u32[]{:S(2)}) async-start(bf16[4,2,48,1280]{3,2,1,0:T(8,128)(2,1)} %sum_of_plane.2), calls=%async_computation.1 | async-start | bytes 1966080 | tf_op jit(solution)/shard_map/all_to_all | solution.py:884
  92.8 2.0 %sum_of_cores.3 = (bf16[2,2,48,1280]{3,2,1,0:T(8,128)(2,1)S(1)}, bf16[2,2,48,1280]{3,2,1,0:T(8,128)(2,1)S(1)}, bf16[4,48,1280]{2,1,0:T(8,128)(2,1)S(1)}, bf16[2,...) custom-call(bf16[4,4,48,1280]{3,2,1,0:T(8,128)(2,1)S(1)} %get-tuple-element.121.keep, ...), custom_call_target="tpu_custom_call" | custom-call | tf_op jit(solution)/shard_map/sum_of_cores/pallas_call | solution.py:555
  100.4 8.1 %collective-permute-done.26.got.got_x = bf16[2,2,48,1280]{3,2,1,0:T(8,128)(2,1)S(1)} collective-permute-done((bf16[2,2,48,1280]{3,2,1,0:T(8,128)(2,1)S(1)}, bf16[2,2,48,1280]{3,2,1,0:T(8,128)(2,1)S(1)}, u32[]{:S(2)}, u32[]{:S(2)}) %collective-permute-start.26) | collective-permute-done | bytes 491552 | tf_op jit(solution)/shard_map/ppermute | solution.py:702
  110.4 1.8 %collective-permute-start.30 = (bf16[2,48,1280]{2,1,0:T(8,128)(2,1)S(1)}, bf16[2,48,1280]{2,1,0:T(8,128)(2,1)S(1)}, u32[]{:S(2)}, u32[]{:S(2)}) collective-permute-start(bf16[2,48,1280]{2,1,0:T(8,128)(2,1)S(1)} %relay.2), channel_id=1, source_target_pairs={{0,2},{1,3},{2,0},{3,1},{4,6},{5,7},{6,4},{7,5},{8,10},{9,11},{10,... | collective-permute-start | bytes 737288 | tf_op jit(solution)/shard_map/ppermute | solution.py:702
  112.2 4.0 %collective-permute-done.31.late_x = bf16[2,48,1280]{2,1,0:T(8,128)(2,1)S(1)} collective-permute-done((bf16[2,48,1280]{2,1,0:T(8,128)(2,1)S(1)}, bf16[2,48,1280]{2,1,0:T(8,128)(2,1)S(1)}, u32[]{:S(2)}, u32[]{:S(2)}) %collective-permute-start.31) | collective-permute-done | bytes 245792 | tf_op jit(solution)/shard_map/ppermute | solution.py:702
  118.4 4.4 %all-to-all-start = ((bf16[4,48,1280]{2,1,0:T(8,128)(2,1)}), bf16[4,48,1280]{2,1,0:T(8,128)(2,1)S(1)}, u32[]{:S(2)}, u32[]{:S(2)}) async-start(bf16[4,48,1280]{2,1,0:T(8,128)(2,1)} %sum_of_plane.3), calls=%async_computation | async-start | bytes 983040 | tf_op jit(solution)/shard_map/all_to_all | solution.py:894
  123.0 1.8 %collective-permute-start.34 = (bf16[2,48,1280]{2,1,0:T(8,128)(2,1)S(1)}, bf16[2,48,1280]{2,1,0:T(8,128)(2,1)S(1)}, u32[]{:S(2)}, u32[]{:S(2)}) collective-permute-start(bf16[2,48,1280]{2,1,0:T(8,128)(2,1)S(1)} %sum_of_column.2.refs_0_), channel_id=1, source_target_pairs={{0,3},{1,2},{2,1},{3,0},{4,7},{5,6},{6,5},{7,4},{8,11},{9,10},{10,... | collective-permute-start | bytes 737288 | tf_op jit(solution)/shard_map/ppermute | solution.py:702
  126.6 6.2 %collective-permute-done.34.refs_6_ = bf16[2,48,1280]{2,1,0:T(8,128)(2,1)S(1)} collective-permute-done((bf16[2,48,1280]{2,1,0:T(8,128)(2,1)S(1)}, bf16[2,48,1280]{2,1,0:T(8,128)(2,1)S(1)}, u32[]{:S(2)}, u32[]{:S(2)}) %collective-permute-start.34) | collective-permute-done | bytes 245792 | tf_op jit(solution)/shard_map/ppermute | solution.py:702
  132.8 2.6 %collective-permute-done.33.refs_4_ = bf16[2,48,1280]{2,1,0:T(8,128)(2,1)S(1)} collective-permute-done((bf16[2,48,1280]{2,1,0:T(8,128)(2,1)S(1)}, bf16[2,48,1280]{2,1,0:T(8,128)(2,1)S(1)}, u32[]{:S(2)}, u32[]{:S(2)}) %collective-permute-start.33) | collective-permute-done | bytes 245792 | tf_op jit(solution)/shard_map/ppermute | solution.py:702
  136.0 1.8 %collective-permute-start.40 = (bf16[48,1280]{1,0:T(8,128)(2,1)S(1)}, bf16[48,1280]{1,0:T(8,128)(2,1)S(1)}, u32[]{:S(2)}, u32[]{:S(2)}) collective-permute-start(bf16[48,1280]{1,0:T(8,128)(2,1)S(1)} %sum_of_column.3.refs_0_), channel_id=1, source_target_pairs={{0,3},{1,2},{2,1},{3,0},{4,7},{5,6},{6,5},{7,4},{8,11},{9,10},{10,... | collective-permute-start | bytes 368648 | tf_op jit(solution)/shard_map/ppermute | solution.py:702
  139.5 3.6 %collective-permute-done.40.refs_6_ = bf16[48,1280]{1,0:T(8,128)(2,1)S(1)} collective-permute-done((bf16[48,1280]{1,0:T(8,128)(2,1)S(1)}, bf16[48,1280]{1,0:T(8,128)(2,1)S(1)}, u32[]{:S(2)}, u32[]{:S(2)}) %collective-permute-start.40) | collective-permute-done | bytes 122912 | tf_op jit(solution)/shard_map/ppermute | solution.py:702
  143.1 2.0 %collective-permute-done.38.refs_4_ = bf16[48,1280]{1,0:T(8,128)(2,1)S(1)} collective-permute-done((bf16[48,1280]{1,0:T(8,128)(2,1)S(1)}, bf16[48,1280]{1,0:T(8,128)(2,1)S(1)}, u32[]{:S(2)}, u32[]{:S(2)}) %collective-permute-start.38) | collective-permute-done | bytes 122912 | tf_op jit(solution)/shard_map/ppermute | solution.py:702
  146.6 2.8 %unpack.1 = (f32[1,96,1152]{2,1,0:T(8,128)}, f32[1,96,384]{2,1,0:T(8,128)}, f32[1,96,1536]{2,1,0:T(8,128)}, f32[1,384,384]{2,1,0:T(8,128)}, f32[1,96]{1,0:T(1,12...) custom-call(bf16[48,1280]{1,0:T(8,128)(2,1)S(1)} %sum_of_column.3.re, ...), custom_call_target="tpu_custom_call" | custom-call | tf_op jit(solution)/shard_map/unpack/pallas_call | solution.py:676
  (100 shorter events, 29.9 us)
Async XLA Ops:
  3.1 11.8 %collective-permute-start.1 = (bf16[96,1280]{1,0:T(8,128)(2,1)}, bf16[96,1280]{1,0:T(8,128)(2,1)S(1)}, u32[]{:S(2)}, u32[]{:S(2)}) collective-permute-start(bf16[96,1280]{1,0:T(8,128)(2,1)} %get-tuple-element.89), channel_id=1, source_target_pairs={{0,12},{4,0},{8,4},{12,8},{1,13},{5,1},{9,5},{13,9},{2,14},{6,2},{... | collective-permute-start | bytes 737288 | tf_op jit(solution)/shard_map/ppermute | solution.py:706
  8.2 11.6 %collective-permute-start = (bf16[96,1280]{1,0:T(8,128)(2,1)}, bf16[96,1280]{1,0:T(8,128)(2,1)S(1)}, u32[]{:S(2)}, u32[]{:S(2)}) collective-permute-start(bf16[96,1280]{1,0:T(8,128)(2,1)} %get-tuple-element.89), channel_id=1, source_target_pairs={{0,4},{4,8},{8,12},{12,0},{1,5},{5,9},{9,13},{13,1},{2,6},{6,10},{... | collective-permute-start | bytes 737288 | tf_op jit(solution)/shard_map/ppermute | solution.py:706
  19.9 11.1 %collective-permute-start.5 = (bf16[2,96,1152]{2,1,0:T(8,128)(2,1)S(1)}, bf16[2,96,1152]{2,1,0:T(8,128)(2,1)S(1)}, u32[]{:S(2)}, u32[]{:S(2)}) collective-permute-start(bf16[2,96,1152]{2,1,0:T(8,128)(2,1)S(1)} %get-tuple-element.93.refs_2_), channel_id=1, source_target_pairs={{0,2},{1,3},{2,0},{3,1},{4,6},{5,7},{6,4},{7,5},{8,10},{9,11},{10,... | collective-permute-start | bytes 1327112 | tf_op jit(solution)/shard_map/ppermute | solution.py:702
  21.5 10.8 %collective-permute-start.4 = (bf16[2,96,1152]{2,1,0:T(8,128)(2,1)S(1)}, bf16[2,96,1152]{2,1,0:T(8,128)(2,1)S(1)}, u32[]{:S(2)}, u32[]{:S(2)}) collective-permute-start(bf16[2,96,1152]{2,1,0:T(8,128)(2,1)S(1)} %get-tuple-element.93.refs_2_), channel_id=1, source_target_pairs={{0,1},{1,0},{2,3},{3,2},{4,5},{5,4},{6,7},{7,6},{8,9},{9,8},{10,11... | collective-permute-start | bytes 1327112 | tf_op jit(solution)/shard_map/ppermute | solution.py:702
  23.0 6.9 %collective-permute-start.2 = (bf16[48,1280]{1,0:T(8,128)(2,1)S(1)}, bf16[48,1280]{1,0:T(8,128)(2,1)S(1)}, u32[]{:S(2)}, u32[]{:S(2)}) collective-permute-start(bf16[48,1280]{1,0:T(8,128)(2,1)S(1)} %get-tuple-element.90), channel_id=1, source_target_pairs={{0,4},{4,8},{8,12},{12,0},{1,5},{5,9},{9,13},{13,1},{2,6},{6,10},{... | collective-permute-start | bytes 368648 | tf_op jit(solution)/shard_map/ppermute | solution.py:706
  24.6 6.2 %collective-permute-start.3 = (bf16[48,1280]{1,0:T(8,128)(2,1)S(1)}, bf16[48,1280]{1,0:T(8,128)(2,1)S(1)}, u32[]{:S(2)}, u32[]{:S(2)}) collective-permute-start(bf16[48,1280]{1,0:T(8,128)(2,1)S(1)} %get-tuple-element.91), channel_id=1, source_target_pairs={{0,12},{4,0},{8,4},{12,8},{1,13},{5,1},{9,5},{13,9},{2,14},{6,2},{... | collective-permute-start | bytes 368648 | tf_op jit(solution)/shard_map/ppermute | solution.py:706
  26.8 23.0 %collective-permute-start.11 = (bf16[96,4736]{1,0:T(8,128)(2,1)}, bf16[96,4736]{1,0:T(8,128)(2,1)S(1)}, u32[]{:S(2)}, u32[]{:S(2)}) collective-permute-start(bf16[96,4736]{1,0:T(8,128)(2,1)} %get-tuple-element.88.refs_0_), channel_id=1, source_target_pairs={{0,16},{16,0},{1,17},{17,1},{2,18},{18,2},{3,19},{19,3},{4,20},{20... | collective-permute-start | bytes 2727944 | tf_op jit(solution)/shard_map/ppermute | solution.py:698
  32.3 7.2 %collective-permute-start.9 = (bf16[96,1152]{1,0:T(8,128)(2,1)S(1)}, bf16[96,1152]{1,0:T(8,128)(2,1)S(1)}, u32[]{:S(2)}, u32[]{:S(2)}) collective-permute-start(bf16[96,1152]{1,0:T(8,128)(2,1)S(1)} %slice_bitcast_fusion), channel_id=1, source_target_pairs={{0,2},{1,3},{2,0},{3,1},{4,6},{5,7},{6,4},{7,5},{8,10},{9,11},{10,... | collective-permute-start | bytes 663560 | tf_op jit(solution)/shard_map/ppermute | solution.py:702
  32.9 8.4 %collective-permute-start.8 = (bf16[96,1152]{1,0:T(8,128)(2,1)S(1)}, bf16[96,1152]{1,0:T(8,128)(2,1)S(1)}, u32[]{:S(2)}, u32[]{:S(2)}) collective-permute-start(bf16[96,1152]{1,0:T(8,128)(2,1)S(1)} %slice_bitcast_fusion.1), channel_id=1, source_target_pairs={{0,1},{1,0},{2,3},{3,2},{4,5},{5,4},{6,7},{7,6},{8,9},{9,8},{10,11... | collective-permute-start | bytes 663560 | tf_op jit(solution)/shard_map/ppermute | solution.py:702
  34.4 15.9 %collective-permute-start.17 = (bf16[2,96,1152]{2,1,0:T(8,128)(2,1)S(1)}, bf16[2,96,1152]{2,1,0:T(8,128)(2,1)S(1)}, u32[]{:S(2)}, u32[]{:S(2)}) collective-permute-start(bf16[2,96,1152]{2,1,0:T(8,128)(2,1)S(1)} %collective-permute-done.5.refs_6_), channel_id=1, source_target_pairs={{0,16},{16,0},{1,17},{17,1},{2,18},{18,2},{3,19},{19,3},{4,20},{20... | collective-permute-start | bytes 1327112 | tf_op jit(solution)/shard_map/ppermute | solution.py:698
  34.4 12.3 %collective-permute-start.10 = (bf16[96,1152]{1,0:T(8,128)(2,1)S(1)}, bf16[96,1152]{1,0:T(8,128)(2,1)S(1)}, u32[]{:S(2)}, u32[]{:S(2)}) collective-permute-start(bf16[96,1152]{1,0:T(8,128)(2,1)S(1)} %get-tuple-element.95.refs_3_), channel_id=1, source_target_pairs={{0,3},{1,2},{2,1},{3,0},{4,7},{5,6},{6,5},{7,4},{8,11},{9,10},{10,... | collective-permute-start | bytes 663560 | tf_op jit(solution)/shard_map/ppermute | solution.py:702
  39.4 9.6 %collective-permute-start.7 = (bf16[96,1152]{1,0:T(8,128)(2,1)S(1)}, bf16[96,1152]{1,0:T(8,128)(2,1)S(1)}, u32[]{:S(2)}, u32[]{:S(2)}) collective-permute-start(bf16[96,1152]{1,0:T(8,128)(2,1)S(1)} %get-tuple-element.95.refs_3_), channel_id=1, source_target_pairs={{0,2},{1,3},{2,0},{3,1},{4,6},{5,7},{6,4},{7,5},{8,10},{9,11},{10,... | collective-permute-start | bytes 663560 | tf_op jit(solution)/shard_map/ppermute | solution.py:702
  41.2 8.6 %collective-permute-start.6 = (bf16[96,1152]{1,0:T(8,128)(2,1)S(1)}, bf16[96,1152]{1,0:T(8,128)(2,1)S(1)}, u32[]{:S(2)}, u32[]{:S(2)}) collective-permute-start(bf16[96,1152]{1,0:T(8,128)(2,1)S(1)} %get-tuple-element.95.refs_3_), channel_id=1, source_target_pairs={{0,1},{1,0},{2,3},{3,2},{4,5},{5,4},{6,7},{7,6},{8,9},{9,8},{10,11... | collective-permute-start | bytes 663560 | tf_op jit(solution)/shard_map/ppermute | solution.py:702
  73.3 13.4 %collective-permute-start.23 = (bf16[4,48,1280]{2,1,0:T(8,128)(2,1)S(1)}, bf16[4,48,1280]{2,1,0:T(8,128)(2,1)S(1)}, u32[]{:S(2)}, u32[]{:S(2)}) collective-permute-start(bf16[4,48,1280]{2,1,0:T(8,128)(2,1)S(1)} %get-tuple-element.101), channel_id=1, source_target_pairs={{0,1},{1,0},{2,3},{3,2},{4,5},{5,4},{6,7},{7,6},{8,9},{9,8},{10,11... | collective-permute-start | bytes 1474568 | tf_op jit(solution)/shard_map/ppermute | solution.py:702
  74.8 13.2 %collective-permute-start.24 = (bf16[4,48,1280]{2,1,0:T(8,128)(2,1)S(1)}, bf16[4,48,1280]{2,1,0:T(8,128)(2,1)S(1)}, u32[]{:S(2)}, u32[]{:S(2)}) collective-permute-start(bf16[4,48,1280]{2,1,0:T(8,128)(2,1)S(1)} %get-tuple-element.102), channel_id=1, source_target_pairs={{0,2},{1,3},{2,0},{3,1},{4,6},{5,7},{6,4},{7,5},{8,10},{9,11},{10,... | collective-permute-start | bytes 1474568 | tf_op jit(solution)/shard_map/ppermute | solution.py:702
  88.0 4.7 %collective-permute-start.25 = (bf16[4,4,48,1280]{3,2,1,0:T(8,128)(2,1)}, bf16[4,4,48,1280]{3,2,1,0:T(8,128)(2,1)}, u32[]{:S(2)}, u32[]{:S(2)}) collective-permute-start(bf16[4,4,48,1280]{3,2,1,0:T(8,128)(2,1)} %get-tuple-element.122), channel_id=1, source_target_pairs={{0,16},{16,0},{1,17},{17,1},{2,18},{18,2},{3,19},{19,3},{4,20},{20... | collective-permute-start | bytes 5898248 | tf_op jit(solution)/shard_map/ppermute | solution.py:698
  89.2 29.2 %all-to-all-start.1 = ((bf16[4,2,48,1280]{3,2,1,0:T(8,128)(2,1)}), bf16[4,2,48,1280]{3,2,1,0:T(8,128)(2,1)S(1)}, u32[]{:S(2)}, u32[]{:S(2)}) async-start(bf16[4,2,48,1280]{3,2,1,0:T(8,128)(2,1)} %sum_of_plane.2), calls=%async_computation.1 | async-start | bytes 1966080 | tf_op jit(solution)/shard_map/all_to_all | solution.py:884
  94.8 13.7 %collective-permute-start.26 = (bf16[2,2,48,1280]{3,2,1,0:T(8,128)(2,1)S(1)}, bf16[2,2,48,1280]{3,2,1,0:T(8,128)(2,1)S(1)}, u32[]{:S(2)}, u32[]{:S(2)}) collective-permute-start(bf16[2,2,48,1280]{3,2,1,0:T(8,128)(2,1)S(1)} %get-tuple-element.123), channel_id=1, source_target_pairs={{0,1},{1,0},{2,3},{3,2},{4,5},{5,4},{6,7},{7,6},{8,9},{9,8},{10,11... | collective-permute-start | bytes 1474568 | tf_op jit(solution)/shard_map/ppermute | solution.py:702
  95.8 13.1 %collective-permute-start.27 = (bf16[2,2,48,1280]{3,2,1,0:T(8,128)(2,1)S(1)}, bf16[2,2,48,1280]{3,2,1,0:T(8,128)(2,1)S(1)}, u32[]{:S(2)}, u32[]{:S(2)}) collective-permute-start(bf16[2,2,48,1280]{3,2,1,0:T(8,128)(2,1)S(1)} %get-tuple-element.124), channel_id=1, source_target_pairs={{0,2},{1,3},{2,0},{3,1},{4,6},{5,7},{6,4},{7,5},{8,10},{9,11},{10,... | collective-permute-start | bytes 1474568 | tf_op jit(solution)/shard_map/ppermute | solution.py:702
  108.9 7.3 %collective-permute-start.31 = (bf16[2,48,1280]{2,1,0:T(8,128)(2,1)S(1)}, bf16[2,48,1280]{2,1,0:T(8,128)(2,1)S(1)}, u32[]{:S(2)}, u32[]{:S(2)}) collective-permute-start(bf16[2,48,1280]{2,1,0:T(8,128)(2,1)S(1)} %relay.3), channel_id=1, source_target_pairs={{0,1},{1,0},{2,3},{3,2},{4,5},{5,4},{6,7},{7,6},{8,9},{9,8},{10,11... | collective-permute-start | bytes 737288 | tf_op jit(solution)/shard_map/ppermute | solution.py:702
  110.4 7.1 %collective-permute-start.30 = (bf16[2,48,1280]{2,1,0:T(8,128)(2,1)S(1)}, bf16[2,48,1280]{2,1,0:T(8,128)(2,1)S(1)}, u32[]{:S(2)}, u32[]{:S(2)}) collective-permute-start(bf16[2,48,1280]{2,1,0:T(8,128)(2,1)S(1)} %relay.2), channel_id=1, source_target_pairs={{0,2},{1,3},{2,0},{3,1},{4,6},{5,7},{6,4},{7,5},{8,10},{9,11},{10,... | collective-permute-start | bytes 737288 | tf_op jit(solution)/shard_map/ppermute | solution.py:702
  118.4 17.5 %all-to-all-start = ((bf16[4,48,1280]{2,1,0:T(8,128)(2,1)}), bf16[4,48,1280]{2,1,0:T(8,128)(2,1)S(1)}, u32[]{:S(2)}, u32[]{:S(2)}) async-start(bf16[4,48,1280]{2,1,0:T(8,128)(2,1)} %sum_of_plane.3), calls=%async_computation | async-start | bytes 983040 | tf_op jit(solution)/shard_map/all_to_all | solution.py:894
  123.0 9.8 %collective-permute-start.34 = (bf16[2,48,1280]{2,1,0:T(8,128)(2,1)S(1)}, bf16[2,48,1280]{2,1,0:T(8,128)(2,1)S(1)}, u32[]{:S(2)}, u32[]{:S(2)}) collective-permute-start(bf16[2,48,1280]{2,1,0:T(8,128)(2,1)S(1)} %sum_of_column.2.refs_0_), channel_id=1, source_target_pairs={{0,3},{1,2},{2,1},{3,0},{4,7},{5,6},{6,5},{7,4},{8,11},{9,10},{10,... | collective-permute-start | bytes 737288 | tf_op jit(solution)/shard_map/ppermute | solution.py:702
  124.9 10.5 %collective-permute-start.33 = (bf16[2,48,1280]{2,1,0:T(8,128)(2,1)S(1)}, bf16[2,48,1280]{2,1,0:T(8,128)(2,1)S(1)}, u32[]{:S(2)}, u32[]{:S(2)}) collective-permute-start(bf16[2,48,1280]{2,1,0:T(8,128)(2,1)S(1)} %sum_of_column.2.refs_0_), channel_id=1, source_target_pairs={{0,2},{1,3},{2,0},{3,1},{4,6},{5,7},{6,4},{7,5},{8,10},{9,11},{10,... | collective-permute-start | bytes 737288 | tf_op jit(solution)/shard_map/ppermute | solution.py:702
  125.1 10.6 %collective-permute-start.32 = (bf16[2,48,1280]{2,1,0:T(8,128)(2,1)S(1)}, bf16[2,48,1280]{2,1,0:T(8,128)(2,1)S(1)}, u32[]{:S(2)}, u32[]{:S(2)}) collective-permute-start(bf16[2,48,1280]{2,1,0:T(8,128)(2,1)S(1)} %sum_of_column.2.refs_0_), channel_id=1, source_target_pairs={{0,1},{1,0},{2,3},{3,2},{4,5},{5,4},{6,7},{7,6},{8,9},{9,8},{10,11... | collective-permute-start | bytes 737288 | tf_op jit(solution)/shard_map/ppermute | solution.py:702
  126.6 11.2 %collective-permute-start.42 = (bf16[2,48,1280]{2,1,0:T(8,128)(2,1)S(1)}, bf16[2,48,1280]{2,1,0:T(8,128)(2,1)S(1)}, u32[]{:S(2)}, u32[]{:S(2)}) collective-permute-start(bf16[2,48,1280]{2,1,0:T(8,128)(2,1)S(1)} %sum_of_column.2.refs_0_), channel_id=1, source_target_pairs={{0,16},{16,0},{1,17},{17,1},{2,18},{18,2},{3,19},{19,3},{4,20},{20... | collective-permute-start | bytes 737288 | tf_op jit(solution)/shard_map/ppermute | solution.py:698
  132.8 5.3 %collective-permute-start.45 = (bf16[2,48,1280]{2,1,0:T(8,128)(2,1)S(1)}, bf16[2,48,1280]{2,1,0:T(8,128)(2,1)S(1)}, u32[]{:S(2)}, u32[]{:S(2)}) collective-permute-start(bf16[2,48,1280]{2,1,0:T(8,128)(2,1)S(1)} %collective-permute-done.34.refs_6_), channel_id=1, source_target_pairs={{0,16},{16,0},{1,17},{17,1},{2,18},{18,2},{3,19},{19,3},{4,20},{20... | collective-permute-start | bytes 737288 | tf_op jit(solution)/shard_map/ppermute | solution.py:698
  135.7 9.9 %collective-permute-start.43 = (bf16[2,48,1280]{2,1,0:T(8,128)(2,1)S(1)}, bf16[2,48,1280]{2,1,0:T(8,128)(2,1)S(1)}, u32[]{:S(2)}, u32[]{:S(2)}) collective-permute-start(bf16[2,48,1280]{2,1,0:T(8,128)(2,1)S(1)} %collective-permute-done.32.refs_2_), channel_id=1, source_target_pairs={{0,16},{16,0},{1,17},{17,1},{2,18},{18,2},{3,19},{19,3},{4,20},{20... | collective-permute-start | bytes 737288 | tf_op jit(solution)/shard_map/ppermute | solution.py:698
  136.0 7.2 %collective-permute-start.40 = (bf16[48,1280]{1,0:T(8,128)(2,1)S(1)}, bf16[48,1280]{1,0:T(8,128)(2,1)S(1)}, u32[]{:S(2)}, u32[]{:S(2)}) collective-permute-start(bf16[48,1280]{1,0:T(8,128)(2,1)S(1)} %sum_of_column.3.refs_0_), channel_id=1, source_target_pairs={{0,3},{1,2},{2,1},{3,0},{4,7},{5,6},{6,5},{7,4},{8,11},{9,10},{10,... | collective-permute-start | bytes 368648 | tf_op jit(solution)/shard_map/ppermute | solution.py:702
  137.8 7.4 %collective-permute-start.38 = (bf16[48,1280]{1,0:T(8,128)(2,1)S(1)}, bf16[48,1280]{1,0:T(8,128)(2,1)S(1)}, u32[]{:S(2)}, u32[]{:S(2)}) collective-permute-start(bf16[48,1280]{1,0:T(8,128)(2,1)S(1)} %sum_of_column.3.refs_0_), channel_id=1, source_target_pairs={{0,2},{1,3},{2,0},{3,1},{4,6},{5,7},{6,4},{7,5},{8,10},{9,11},{10,... | collective-permute-start | bytes 368648 | tf_op jit(solution)/shard_map/ppermute | solution.py:702
  138.1 7.1 %collective-permute-start.36 = (bf16[48,1280]{1,0:T(8,128)(2,1)S(1)}, bf16[48,1280]{1,0:T(8,128)(2,1)S(1)}, u32[]{:S(2)}, u32[]{:S(2)}) collective-permute-start(bf16[48,1280]{1,0:T(8,128)(2,1)S(1)} %sum_of_column.3.refs_0_), channel_id=1, source_target_pairs={{0,1},{1,0},{2,3},{3,2},{4,5},{5,4},{6,7},{7,6},{8,9},{9,8},{10,11... | collective-permute-start | bytes 368648 | tf_op jit(solution)/shard_map/ppermute | solution.py:702
  139.5 6.3 %collective-permute-start.35 = (bf16[48,1280]{1,0:T(8,128)(2,1)S(1)}, bf16[48,1280]{1,0:T(8,128)(2,1)S(1)}, u32[]{:S(2)}, u32[]{:S(2)}) collective-permute-start(bf16[48,1280]{1,0:T(8,128)(2,1)S(1)} %sum_of_column.3.refs_0_), channel_id=1, source_target_pairs={{0,16},{16,0},{1,17},{17,1},{2,18},{18,2},{3,19},{19,3},{4,20},{20... | collective-permute-start | bytes 368648 | tf_op jit(solution)/shard_map/ppermute | solution.py:698
  (24 other events, 256.0 us)

commit v4 on v3

--- a/solution.py
+++ b/solution.py
@@ -307,11 +307,12 @@
         out_other,
         grad_one,
         keep,
-        send,
+        send_near,
+        send_rest,
         kept_weights,
         kept_vectors,
-    ) = refs[0:7]
-    kept_acts = refs[7:13]
+    ) = refs[0:8]
+    kept_acts = refs[8:14]
     (
         packed,
         down,
@@ -324,8 +325,8 @@
         grads,
         sems,
         out_sems,
-    ) = refs[13:24]
-    acts0, acts1 = refs[24:30], refs[30:36]
+    ) = refs[14:25]
+    acts0, acts1 = refs[25:31], refs[31:37]
     section, shard, replica = positions()
     for copy in start_copies(mine, packed, section, sems, shard, replica):
         copy.start()
@@ -386,8 +387,10 @@
     )
     grad_one[...] = grad_x[:seq].astype(BF16)
     copies = [
-        pltpu.make_async_copy(grads.at[section], keep, out_sems.at[1]),
-        pltpu.make_async_copy(grads.at[1 - section], send, out_sems.at[2]),
+        pltpu.make_async_copy(grads.at[1 - section, 1:3], send_near, out_sems.at[1]),
+        pltpu.make_async_copy(grads.at[section], keep, out_sems.at[2]),
+        pltpu.make_async_copy(grads.at[1 - section, 0], send_rest.at[0], out_sems.at[9]),
+        pltpu.make_async_copy(grads.at[1 - section, 3], send_rest.at[1], out_sems.at[10]),
     ]
     for copy in copies:
         copy.start()
@@ -491,13 +494,14 @@
             shape((seq, width), BF16),
             shape((seq, width), BF16),
             shape((4, 4, HALF, PIECE), BF16),
-            shape((4, 4, HALF, PIECE), BF16),
+            shape((2, 4, HALF, PIECE), BF16),
+            shape((2, 4, HALF, PIECE), BF16),
             shape((1, 4, ROWS, PACKED), BF16),
             shape((8, width), F32),
         ]
         + [shape(*a) for a in acts],
         in_specs=anywhere(22) + vmem(2) + [pl.BlockSpec(memory_space=pltpu.SMEM)],
-        out_specs=vmem(3) + anywhere(3) + vmem(1) + anywhere(6),
+        out_specs=vmem(6) + anywhere(1) + vmem(1) + anywhere(6),
         scratch_shapes=[
             pltpu.VMEM((2, 4, ROWS, PACKED), BF16),
             pltpu.VMEM((2, wide, width), BF16),
@@ -509,7 +513,7 @@
             pltpu.VMEM((SEQ_ROWS, 3 * width), BF16),
             pltpu.VMEM((2, 4, 4, HALF, PIECE), BF16),
             pltpu.SemaphoreType.DMA((2, 16)),
-            pltpu.SemaphoreType.DMA((9,)),
+            pltpu.SemaphoreType.DMA((11,)),
         ]
         + [pltpu.VMEM(*a) for a in acts + acts],
         compiler_params=grant(32),
@@ -574,21 +578,19 @@
         y_late[place] = add(keep[2, place], recv[2, place]).astype(BF16)
 
 
-def whole_sum_kernel(keep, recv, to_x, to_y, own, opposite):
+def near_sum_kernel(keep, recv, to_x, to_y):
     for place in range(4):
-        own[place] = add(keep[0, place], recv[0, place]).astype(BF16)
-        to_x[place] = add(keep[1, place], recv[1, place]).astype(BF16)
-        to_y[place] = add(keep[2, place], recv[2, place]).astype(BF16)
-        opposite[place] = add(keep[3, place], recv[3, place]).astype(BF16)
-
-
-def whole_plane_kernel(own, got_x, got_y, opposite, out):
+        to_x[place] = add(keep[1, place], recv[0, place]).astype(BF16)
+        to_y[place] = add(keep[2, place], recv[1, place]).astype(BF16)
+
+
+def whole_plane_kernel(keep, recv, got_x, got_y, out):
     shard = lax.axis_index("shard")
     for place in range(4):
         owner = lax.rem(shard + place, 4)
-        value = add(own[place], got_x[place]) + got_y[place].astype(F32)
+        value = add(keep[0, place], recv[0, place]) + add(got_x[place], got_y[place])
         out[owner, 0] = value.astype(BF16)
-        out[owner, 1] = opposite[place]
+        out[owner, 1] = add(keep[3, place], recv[1, place]).astype(BF16)
 
 
 def pair_column_kernel(parts, out):
@@ -867,19 +869,19 @@
     mine = [own, tiles, near, far, x_near, x_far, y_near, y_far, d_first, d_third, d_far]
     other = [swap(member) for member in mine]
 
-    (out_mine, out_other, grad_one, keep1, send1, kept, vectors, *acts) = run_main(
+    (out_mine, out_other, grad_one, keep1, near1, rest1, kept, vectors, *acts) = run_main(
         mine, other, patches, cotangent, live_slots, wide
     )
     whole, piece = keep1.shape[1:], keep1.shape[2:]
-    to_x, to_y, own1, opposite = small_call(
-        whole_sum_kernel, [whole] * 4, "sum_of_cores", keep1, swap(send1)
-    )
+    to_x, to_y = small_call(near_sum_kernel, [whole] * 2, "sum_of_cores", keep1, swap(near1))
     got1 = (flip(to_x, 1), flip(to_y, 2))
-    kept = after(kept, to_x, to_y, own1, opposite)
+    kept = after(kept, to_x, to_y)
     last = run_last(kept, vectors, grad_one, patches, acts, wide)
-    grad_mine, grad_other, keep0, send0, *got1 = lax.optimization_barrier((*last, *got1))
+    grad_mine, grad_other, keep0, send0, recv1, *got1 = lax.optimization_barrier(
+        (*last, swap(rest1), *got1)
+    )
     (sums1,) = small_call(
-        whole_plane_kernel, [(4, 2) + piece], "sum_of_plane", own1, *got1, opposite
+        whole_plane_kernel, [(4, 2) + piece], "sum_of_plane", keep1, recv1, *got1
     )
     column1 = lax.all_to_all(sums1, "shard", 0, 0, tiled=True)
     parts0 = reduce_plane(after(keep0, sums1), send0)

time: 150 us -> 149 us (level)
  waiting for transfers between devices: 65.8 us -> 64 us
    ppermute x23 -> x24, waiting for transfers between devices: 7.17 us -> 5.44 us  [swap(): return lax.ppermute(value, 'section', [(0, 1), (1, 0)])]
    ppermute x23 -> x24, starting transfers between devices: 2.99 us -> 3.31 us  [swap(): return lax.ppermute(value, 'section', [(0, 1), (1, 0)])]
  transfers between devices with their start and end apart: 48 -> 49, of which waited for: 30 -> 30; matrix products, arithmetic and copies ran while one was open for 0% -> 0% of each run, Pallas kernels for 10% -> 10%
where the time goes in v4:
time: 149 us
  waiting for transfers between devices  64 us (43%)
  starting transfers between devices  45.7 us (31%)
  Pallas kernels  37.3 us (25%)
    ppermute x19, waiting for transfers between devices, flip(): lax.ppermute(value, 'replica', [(place, place ^ bits) for place in range(...  43 us
    ppermute x19, starting transfers between devices, flip(): lax.ppermute(value, 'replica', [(place, place ^ bits) for place in range(...  25.5 us
    pallas_call x1, Pallas kernels, run_main(): pl.pallas_call(functools.partial(main_kernel, seq), out_shape=[shape((seq...  17.3 us
    ppermute x4, waiting for transfers between devices, shift(): lax.ppermute(value, 'shard', [(place, (place + steps) % 4) for place in r...  15.6 us
    ppermute x4, starting transfers between devices, shift(): lax.ppermute(value, 'shard', [(place, (place + steps) % 4) for place in r...  8.93 us
    pallas_call x1, Pallas kernels, run_last(): pl.pallas_call(functools.partial(last_kernel, seq), out_shape=[shape((seq...  8.09 us
    ppermute x24, waiting for transfers between devices, swap(): return lax.ppermute(value, 'section', [(0, 1), (1, 0)])  5.44 us
    pallas_call x11, Pallas kernels, small_call(): pl.pallas_call(kernel, out_shape=[shape(dims, BF16) for dims in outs], in...  5.15 us
  transfers between devices with their start and end apart: 49, of which 30 were waited for; matrix products, arithmetic and copies ran while one was open for 0% of the time, Pallas kernels for 10%

profile of v4, /device:TPU:0, one launch (start us, length us, event | category | flops | bytes accessed | tf_op | source)
XLA Modules:
  0.0 148.9 jit_solution(11539380205987991034)
XLA Ops:
  0.7 2.4 %pack.1 = (bf16[96,4736]{1,0:T(8,128)(2,1)}, bf16[96,1280]{1,0:T(8,128)(2,1)}) custom-call(bf16[1,96,1536]{2,1,0:T(8,128)(2,1)} %refs_0_.1, bf16[1,96,1152]{2,1,0:T(8,128)(2,1)} %refs_1_.1, bf16[1,96,384]{2,1,0:T(8,128)(2,1)} %refs_2_.1, bf16[1,384,384]{2,1,0:T(8,128)(2,1)} %refs_3_.2, f32[1,96]{1,0:T(1,128)} %refs_4_.1, f32[1,96]{1,0:T(1,128)} %refs_5_.1, ...), custom_call_target="tpu_custom_call" | custom-call | tf_op jit(solution)/shard_map/pack/pallas_call | solution.py:753
  3.1 5.1 %collective-permute-start.1 = (bf16[96,1280]{1,0:T(8,128)(2,1)}, bf16[96,1280]{1,0:T(8,128)(2,1)S(1)}, u32[]{:S(2)}, u32[]{:S(2)}) collective-permute-start(bf16[96,1280]{1,0:T(8,128)(2,1)} %get-tuple-element.89), channel_id=1, source_target_pairs={{0,12},{4,0},{8,4},{12,8},{1,13},{5,1},{9,5},{13,9},{2,14},{6,2},{... | collective-permute-start | bytes 737288 | tf_op jit(solution)/shard_map/ppermute | solution.py:708
  8.2 6.7 %collective-permute-done.1.third = bf16[96,1280]{1,0:T(8,128)(2,1)S(1)} collective-permute-done((bf16[96,1280]{1,0:T(8,128)(2,1)}, bf16[96,1280]{1,0:T(8,128)(2,1)S(1)}, u32[]{:S(2)}, u32[]{:S(2)}) %collective-permute-start.1) | collective-permute-done | bytes 245792 | tf_op jit(solution)/shard_map/ppermute | solution.py:708
  14.9 4.9 %collective-permute-done.first = bf16[96,1280]{1,0:T(8,128)(2,1)S(1)} collective-permute-done((bf16[96,1280]{1,0:T(8,128)(2,1)}, bf16[96,1280]{1,0:T(8,128)(2,1)S(1)}, u32[]{:S(2)}, u32[]{:S(2)}) %collective-permute-start) | collective-permute-done | bytes 245792 | tf_op jit(solution)/shard_map/ppermute | solution.py:708
  19.9 1.6 %collective-permute-start.5 = (bf16[2,96,1152]{2,1,0:T(8,128)(2,1)S(1)}, bf16[2,96,1152]{2,1,0:T(8,128)(2,1)S(1)}, u32[]{:S(2)}, u32[]{:S(2)}) collective-permute-start(bf16[2,96,1152]{2,1,0:T(8,128)(2,1)S(1)} %get-tuple-element.93.refs_2_), channel_id=1, source_target_pairs={{0,2},{1,3},{2,0},{3,1},{4,6},{5,7},{6,4},{7,5},{8,10},{9,11},{10,... | collective-permute-start | bytes 1327112 | tf_op jit(solution)/shard_map/ppermute | solution.py:704
  21.5 1.5 %collective-permute-start.4 = (bf16[2,96,1152]{2,1,0:T(8,128)(2,1)S(1)}, bf16[2,96,1152]{2,1,0:T(8,128)(2,1)S(1)}, u32[]{:S(2)}, u32[]{:S(2)}) collective-permute-start(bf16[2,96,1152]{2,1,0:T(8,128)(2,1)S(1)} %get-tuple-element.93.refs_2_), channel_id=1, source_target_pairs={{0,1},{1,0},{2,3},{3,2},{4,5},{5,4},{6,7},{7,6},{8,9},{9,8},{10,11... | collective-permute-start | bytes 1327112 | tf_op jit(solution)/shard_map/ppermute | solution.py:704
  23.0 1.6 %collective-permute-start.2 = (bf16[48,1280]{1,0:T(8,128)(2,1)S(1)}, bf16[48,1280]{1,0:T(8,128)(2,1)S(1)}, u32[]{:S(2)}, u32[]{:S(2)}) collective-permute-start(bf16[48,1280]{1,0:T(8,128)(2,1)S(1)} %get-tuple-element.90), channel_id=1, source_target_pairs={{0,4},{4,8},{8,12},{12,0},{1,5},{5,9},{9,13},{13,1},{2,6},{6,10},{... | collective-permute-start | bytes 368648 | tf_op jit(solution)/shard_map/ppermute | solution.py:708
  24.6 2.2 %collective-permute-start.3 = (bf16[48,1280]{1,0:T(8,128)(2,1)S(1)}, bf16[48,1280]{1,0:T(8,128)(2,1)S(1)}, u32[]{:S(2)}, u32[]{:S(2)}) collective-permute-start(bf16[48,1280]{1,0:T(8,128)(2,1)S(1)} %get-tuple-element.91), channel_id=1, source_target_pairs={{0,12},{4,0},{8,4},{12,8},{1,13},{5,1},{9,5},{13,9},{2,14},{6,2},{... | collective-permute-start | bytes 368648 | tf_op jit(solution)/shard_map/ppermute | solution.py:708
  26.8 3.1 %collective-permute-done.2.upper = bf16[48,1280]{1,0:T(8,128)(2,1)S(1)} collective-permute-done((bf16[48,1280]{1,0:T(8,128)(2,1)S(1)}, bf16[48,1280]{1,0:T(8,128)(2,1)S(1)}, u32[]{:S(2)}, u32[]{:S(2)}) %collective-permute-start.2) | collective-permute-done | bytes 122912 | tf_op jit(solution)/shard_map/ppermute | solution.py:708
  32.9 1.6 %collective-permute-start.8 = (bf16[96,1152]{1,0:T(8,128)(2,1)S(1)}, bf16[96,1152]{1,0:T(8,128)(2,1)S(1)}, u32[]{:S(2)}, u32[]{:S(2)}) collective-permute-start(bf16[96,1152]{1,0:T(8,128)(2,1)S(1)} %slice_bitcast_fusion.1), channel_id=1, source_target_pairs={{0,1},{1,0},{2,3},{3,2},{4,5},{5,4},{6,7},{7,6},{8,9},{9,8},{10,11... | collective-permute-start | bytes 663560 | tf_op jit(solution)/shard_map/ppermute | solution.py:704
  34.4 1.6 %collective-permute-start.10 = (bf16[96,1152]{1,0:T(8,128)(2,1)S(1)}, bf16[96,1152]{1,0:T(8,128)(2,1)S(1)}, u32[]{:S(2)}, u32[]{:S(2)}) collective-permute-start(bf16[96,1152]{1,0:T(8,128)(2,1)S(1)} %get-tuple-element.95.refs_3_), channel_id=1, source_target_pairs={{0,3},{1,2},{2,1},{3,0},{4,7},{5,6},{6,5},{7,4},{8,11},{9,10},{10,... | collective-permute-start | bytes 663560 | tf_op jit(solution)/shard_map/ppermute | solution.py:704
  36.0 3.4 %collective-permute-done.9.refs_9_ = bf16[96,1152]{1,0:T(8,128)(2,1)S(1)} collective-permute-done((bf16[96,1152]{1,0:T(8,128)(2,1)S(1)}, bf16[96,1152]{1,0:T(8,128)(2,1)S(1)}, u32[]{:S(2)}, u32[]{:S(2)}) %collective-permute-start.9) | collective-permute-done | bytes 221216 | tf_op jit(solution)/shard_map/ppermute | solution.py:704
  42.7 4.0 %collective-permute-done.10.refs_10_ = bf16[96,1152]{1,0:T(8,128)(2,1)S(1)} collective-permute-done((bf16[96,1152]{1,0:T(8,128)(2,1)S(1)}, bf16[96,1152]{1,0:T(8,128)(2,1)S(1)}, u32[]{:S(2)}, u32[]{:S(2)}) %collective-permute-start.10) | collective-permute-done | bytes 221216 | tf_op jit(solution)/shard_map/ppermute | solution.py:704
  46.7 2.3 %collective-permute-done.7.refs_7_ = bf16[96,1152]{1,0:T(8,128)(2,1)S(1)} collective-permute-done((bf16[96,1152]{1,0:T(8,128)(2,1)S(1)}, bf16[96,1152]{1,0:T(8,128)(2,1)S(1)}, u32[]{:S(2)}, u32[]{:S(2)}) %collective-permute-start.7) | collective-permute-done | bytes 221216 | tf_op jit(solution)/shard_map/ppermute | solution.py:704
  52.2 17.3 %forward_and_layer_one.1 = (bf16[197,384]{1,0:T(8,128)(2,1)S(1)}, bf16[197,384]{1,0:T(8,128)(2,1)S(1)}, bf16[197,384]{1,0:T(8,128)(2,1)S(1)}, bf16[4,4,48,1280]{...) custom-call(bf16[96,4736]{1,0:T(8,128)(2,1)S(1)} %copy-done, ...), custom_call_target="tpu_custom_call" | custom-call | tf_op jit(solution)/shard_map/forward_and_layer_one/pallas_call | solution.py:490
  70.1 2.1 %collective-permute-done.22.recv = bf16[2,4,48,1280]{3,2,1,0:T(8,128)(2,1)S(1)} collective-permute-done((bf16[2,4,48,1280]{3,2,1,0:T(8,128)(2,1)S(1)}, bf16[2,4,48,1280]{3,2,1,0:T(8,128)(2,1)S(1)}, u32[]{:S(2)}, u32[]{:S(2)}) %collective-permute-start.22) | collective-permute-done | bytes 983072 | tf_op jit(solution)/shard_map/ppermute | solution.py:700
  72.4 1.6 %collective-permute-start.24 = (bf16[4,48,1280]{2,1,0:T(8,128)(2,1)S(1)}, bf16[4,48,1280]{2,1,0:T(8,128)(2,1)S(1)}, u32[]{:S(2)}, u32[]{:S(2)}) collective-permute-start(bf16[4,48,1280]{2,1,0:T(8,128)(2,1)S(1)} %get-tuple-element.101), channel_id=1, source_target_pairs={{0,1},{1,0},{2,3},{3,2},{4,5},{5,4},{6,7},{7,6},{8,9},{9,8},{10,11... | collective-permute-start | bytes 1474568 | tf_op jit(solution)/shard_map/ppermute | solution.py:704
  74.0 2.0 %collective-permute-start.25 = (bf16[4,48,1280]{2,1,0:T(8,128)(2,1)S(1)}, bf16[4,48,1280]{2,1,0:T(8,128)(2,1)S(1)}, u32[]{:S(2)}, u32[]{:S(2)}) collective-permute-start(bf16[4,48,1280]{2,1,0:T(8,128)(2,1)S(1)} %get-tuple-element.102), channel_id=1, source_target_pairs={{0,2},{1,3},{2,0},{3,1},{4,6},{5,7},{6,4},{7,5},{8,10},{9,11},{10,... | collective-permute-start | bytes 1474568 | tf_op jit(solution)/shard_map/ppermute | solution.py:704
  75.9 8.1 %layer_zero_backward.1 = (f32[197,384]{1,0:T(8,128)S(1)}, f32[197,384]{1,0:T(8,128)S(1)}, bf16[4,4,48,1280]{3,2,1,0:T(8,128)(2,1)S(1)}, bf16[4,4,48,1280]{3,2,1,0:T(8,128)(2,1)}) custom-call(bf16[1,4,96,4736]{3,2,1,0:T(8,128)(2,1)S(1)} %get-tuple-element.103.refs_0_, f32[8,384]{1,0:T(8,128)S(1)} %get-tuple-element.104.refs_1_, ...), custom_call_target="tpu_custom_call" | custom-call | flops 8000000000 | bytes 8000000 | tf_op jit(solution)/shard_map/layer_zero_backward/pallas_call | solution.py:526
  88.5 3.5 %all-to-all-start.1 = ((bf16[4,2,48,1280]{3,2,1,0:T(8,128)(2,1)}), bf16[4,2,48,1280]{3,2,1,0:T(8,128)(2,1)S(1)}, u32[]{:S(2)}, u32[]{:S(2)}) async-start(bf16[4,2,48,1280]{3,2,1,0:T(8,128)(2,1)} %sum_of_plane.2), calls=%async_computation.1 | async-start | bytes 1966080 | tf_op jit(solution)/shard_map/all_to_all | solution.py:886
  92.1 2.0 %sum_of_cores.3 = (bf16[2,2,48,1280]{3,2,1,0:T(8,128)(2,1)S(1)}, bf16[2,2,48,1280]{3,2,1,0:T(8,128)(2,1)S(1)}, bf16[4,48,1280]{2,1,0:T(8,128)(2,1)S(1)}, bf16[2,...) custom-call(bf16[4,4,48,1280]{3,2,1,0:T(8,128)(2,1)S(1)} %get-tuple-element.121.keep, ...), custom_call_target="tpu_custom_call" | custom-call | tf_op jit(solution)/shard_map/sum_of_cores/pallas_call | solution.py:559
  99.7 8.1 %collective-permute-done.27.got.got_x = bf16[2,2,48,1280]{3,2,1,0:T(8,128)(2,1)S(1)} collective-permute-done((bf16[2,2,48,1280]{3,2,1,0:T(8,128)(2,1)S(1)}, bf16[2,2,48,1280]{3,2,1,0:T(8,128)(2,1)S(1)}, u32[]{:S(2)}, u32[]{:S(2)}) %collective-permute-start.27) | collective-permute-done | bytes 491552 | tf_op jit(solution)/shard_map/ppermute | solution.py:704
  109.7 1.8 %collective-permute-start.31 = (bf16[2,48,1280]{2,1,0:T(8,128)(2,1)S(1)}, bf16[2,48,1280]{2,1,0:T(8,128)(2,1)S(1)}, u32[]{:S(2)}, u32[]{:S(2)}) collective-permute-start(bf16[2,48,1280]{2,1,0:T(8,128)(2,1)S(1)} %relay.2), channel_id=1, source_target_pairs={{0,2},{1,3},{2,0},{3,1},{4,6},{5,7},{6,4},{7,5},{8,10},{9,11},{10,... | collective-permute-start | bytes 737288 | tf_op jit(solution)/shard_map/ppermute | solution.py:704
  111.5 4.0 %collective-permute-done.32.late_x = bf16[2,48,1280]{2,1,0:T(8,128)(2,1)S(1)} collective-permute-done((bf16[2,48,1280]{2,1,0:T(8,128)(2,1)S(1)}, bf16[2,48,1280]{2,1,0:T(8,128)(2,1)S(1)}, u32[]{:S(2)}, u32[]{:S(2)}) %collective-permute-start.32) | collective-permute-done | bytes 245792 | tf_op jit(solution)/shard_map/ppermute | solution.py:704
  117.8 4.4 %all-to-all-start = ((bf16[4,48,1280]{2,1,0:T(8,128)(2,1)}), bf16[4,48,1280]{2,1,0:T(8,128)(2,1)S(1)}, u32[]{:S(2)}, u32[]{:S(2)}) async-start(bf16[4,48,1280]{2,1,0:T(8,128)(2,1)} %sum_of_plane.3), calls=%async_computation | async-start | bytes 983040 | tf_op jit(solution)/shard_map/all_to_all | solution.py:896
  122.3 1.8 %collective-permute-start.35 = (bf16[2,48,1280]{2,1,0:T(8,128)(2,1)S(1)}, bf16[2,48,1280]{2,1,0:T(8,128)(2,1)S(1)}, u32[]{:S(2)}, u32[]{:S(2)}) collective-permute-start(bf16[2,48,1280]{2,1,0:T(8,128)(2,1)S(1)} %sum_of_column.2.refs_0_), channel_id=1, source_target_pairs={{0,3},{1,2},{2,1},{3,0},{4,7},{5,6},{6,5},{7,4},{8,11},{9,10},{10,... | collective-permute-start | bytes 737288 | tf_op jit(solution)/shard_map/ppermute | solution.py:704
  125.9 6.2 %collective-permute-done.35.refs_6_ = bf16[2,48,1280]{2,1,0:T(8,128)(2,1)S(1)} collective-permute-done((bf16[2,48,1280]{2,1,0:T(8,128)(2,1)S(1)}, bf16[2,48,1280]{2,1,0:T(8,128)(2,1)S(1)}, u32[]{:S(2)}, u32[]{:S(2)}) %collective-permute-start.35) | collective-permute-done | bytes 245792 | tf_op jit(solution)/shard_map/ppermute | solution.py:704
  132.1 2.6 %collective-permute-done.34.refs_4_ = bf16[2,48,1280]{2,1,0:T(8,128)(2,1)S(1)} collective-permute-done((bf16[2,48,1280]{2,1,0:T(8,128)(2,1)S(1)}, bf16[2,48,1280]{2,1,0:T(8,128)(2,1)S(1)}, u32[]{:S(2)}, u32[]{:S(2)}) %collective-permute-start.34) | collective-permute-done | bytes 245792 | tf_op jit(solution)/shard_map/ppermute | solution.py:704
  135.3 1.8 %collective-permute-start.41 = (bf16[48,1280]{1,0:T(8,128)(2,1)S(1)}, bf16[48,1280]{1,0:T(8,128)(2,1)S(1)}, u32[]{:S(2)}, u32[]{:S(2)}) collective-permute-start(bf16[48,1280]{1,0:T(8,128)(2,1)S(1)} %sum_of_column.3.refs_0_), channel_id=1, source_target_pairs={{0,3},{1,2},{2,1},{3,0},{4,7},{5,6},{6,5},{7,4},{8,11},{9,10},{10,... | collective-permute-start | bytes 368648 | tf_op jit(solution)/shard_map/ppermute | solution.py:704
  138.8 3.6 %collective-permute-done.41.refs_6_ = bf16[48,1280]{1,0:T(8,128)(2,1)S(1)} collective-permute-done((bf16[48,1280]{1,0:T(8,128)(2,1)S(1)}, bf16[48,1280]{1,0:T(8,128)(2,1)S(1)}, u32[]{:S(2)}, u32[]{:S(2)}) %collective-permute-start.41) | collective-permute-done | bytes 122912 | tf_op jit(solution)/shard_map/ppermute | solution.py:704
  142.4 2.0 %collective-permute-done.39.refs_4_ = bf16[48,1280]{1,0:T(8,128)(2,1)S(1)} collective-permute-done((bf16[48,1280]{1,0:T(8,128)(2,1)S(1)}, bf16[48,1280]{1,0:T(8,128)(2,1)S(1)}, u32[]{:S(2)}, u32[]{:S(2)}) %collective-permute-start.39) | collective-permute-done | bytes 122912 | tf_op jit(solution)/shard_map/ppermute | solution.py:704
  145.9 2.8 %unpack.1 = (f32[1,96,1152]{2,1,0:T(8,128)}, f32[1,96,384]{2,1,0:T(8,128)}, f32[1,96,1536]{2,1,0:T(8,128)}, f32[1,384,384]{2,1,0:T(8,128)}, f32[1,96]{1,0:T(1,12...) custom-call(bf16[48,1280]{1,0:T(8,128)(2,1)S(1)} %sum_of_column.3.re, ...), custom_call_target="tpu_custom_call" | custom-call | tf_op jit(solution)/shard_map/unpack/pallas_call | solution.py:678
  (102 shorter events, 30.1 us)
Async XLA Ops:
  3.1 11.8 %collective-permute-start.1 = (bf16[96,1280]{1,0:T(8,128)(2,1)}, bf16[96,1280]{1,0:T(8,128)(2,1)S(1)}, u32[]{:S(2)}, u32[]{:S(2)}) collective-permute-start(bf16[96,1280]{1,0:T(8,128)(2,1)} %get-tuple-element.89), channel_id=1, source_target_pairs={{0,12},{4,0},{8,4},{12,8},{1,13},{5,1},{9,5},{13,9},{2,14},{6,2},{... | collective-permute-start | bytes 737288 | tf_op jit(solution)/shard_map/ppermute | solution.py:708
  8.2 11.6 %collective-permute-start = (bf16[96,1280]{1,0:T(8,128)(2,1)}, bf16[96,1280]{1,0:T(8,128)(2,1)S(1)}, u32[]{:S(2)}, u32[]{:S(2)}) collective-permute-start(bf16[96,1280]{1,0:T(8,128)(2,1)} %get-tuple-element.89), channel_id=1, source_target_pairs={{0,4},{4,8},{8,12},{12,0},{1,5},{5,9},{9,13},{13,1},{2,6},{6,10},{... | collective-permute-start | bytes 737288 | tf_op jit(solution)/shard_map/ppermute | solution.py:708
  19.9 11.1 %collective-permute-start.5 = (bf16[2,96,1152]{2,1,0:T(8,128)(2,1)S(1)}, bf16[2,96,1152]{2,1,0:T(8,128)(2,1)S(1)}, u32[]{:S(2)}, u32[]{:S(2)}) collective-permute-start(bf16[2,96,1152]{2,1,0:T(8,128)(2,1)S(1)} %get-tuple-element.93.refs_2_), channel_id=1, source_target_pairs={{0,2},{1,3},{2,0},{3,1},{4,6},{5,7},{6,4},{7,5},{8,10},{9,11},{10,... | collective-permute-start | bytes 1327112 | tf_op jit(solution)/shard_map/ppermute | solution.py:704
  21.5 10.8 %collective-permute-start.4 = (bf16[2,96,1152]{2,1,0:T(8,128)(2,1)S(1)}, bf16[2,96,1152]{2,1,0:T(8,128)(2,1)S(1)}, u32[]{:S(2)}, u32[]{:S(2)}) collective-permute-start(bf16[2,96,1152]{2,1,0:T(8,128)(2,1)S(1)} %get-tuple-element.93.refs_2_), channel_id=1, source_target_pairs={{0,1},{1,0},{2,3},{3,2},{4,5},{5,4},{6,7},{7,6},{8,9},{9,8},{10,11... | collective-permute-start | bytes 1327112 | tf_op jit(solution)/shard_map/ppermute | solution.py:704
  23.0 6.9 %collective-permute-start.2 = (bf16[48,1280]{1,0:T(8,128)(2,1)S(1)}, bf16[48,1280]{1,0:T(8,128)(2,1)S(1)}, u32[]{:S(2)}, u32[]{:S(2)}) collective-permute-start(bf16[48,1280]{1,0:T(8,128)(2,1)S(1)} %get-tuple-element.90), channel_id=1, source_target_pairs={{0,4},{4,8},{8,12},{12,0},{1,5},{5,9},{9,13},{13,1},{2,6},{6,10},{... | collective-permute-start | bytes 368648 | tf_op jit(solution)/shard_map/ppermute | solution.py:708
  24.6 6.2 %collective-permute-start.3 = (bf16[48,1280]{1,0:T(8,128)(2,1)S(1)}, bf16[48,1280]{1,0:T(8,128)(2,1)S(1)}, u32[]{:S(2)}, u32[]{:S(2)}) collective-permute-start(bf16[48,1280]{1,0:T(8,128)(2,1)S(1)} %get-tuple-element.91), channel_id=1, source_target_pairs={{0,12},{4,0},{8,4},{12,8},{1,13},{5,1},{9,5},{13,9},{2,14},{6,2},{... | collective-permute-start | bytes 368648 | tf_op jit(solution)/shard_map/ppermute | solution.py:708
  26.8 23.0 %collective-permute-start.11 = (bf16[96,4736]{1,0:T(8,128)(2,1)}, bf16[96,4736]{1,0:T(8,128)(2,1)S(1)}, u32[]{:S(2)}, u32[]{:S(2)}) collective-permute-start(bf16[96,4736]{1,0:T(8,128)(2,1)} %get-tuple-element.88.refs_0_), channel_id=1, source_target_pairs={{0,16},{16,0},{1,17},{17,1},{2,18},{18,2},{3,19},{19,3},{4,20},{20... | collective-permute-start | bytes 2727944 | tf_op jit(solution)/shard_map/ppermute | solution.py:700
  32.3 7.2 %collective-permute-start.9 = (bf16[96,1152]{1,0:T(8,128)(2,1)S(1)}, bf16[96,1152]{1,0:T(8,128)(2,1)S(1)}, u32[]{:S(2)}, u32[]{:S(2)}) collective-permute-start(bf16[96,1152]{1,0:T(8,128)(2,1)S(1)} %slice_bitcast_fusion), channel_id=1, source_target_pairs={{0,2},{1,3},{2,0},{3,1},{4,6},{5,7},{6,4},{7,5},{8,10},{9,11},{10,... | collective-permute-start | bytes 663560 | tf_op jit(solution)/shard_map/ppermute | solution.py:704
  32.9 8.4 %collective-permute-start.8 = (bf16[96,1152]{1,0:T(8,128)(2,1)S(1)}, bf16[96,1152]{1,0:T(8,128)(2,1)S(1)}, u32[]{:S(2)}, u32[]{:S(2)}) collective-permute-start(bf16[96,1152]{1,0:T(8,128)(2,1)S(1)} %slice_bitcast_fusion.1), channel_id=1, source_target_pairs={{0,1},{1,0},{2,3},{3,2},{4,5},{5,4},{6,7},{7,6},{8,9},{9,8},{10,11... | collective-permute-start | bytes 663560 | tf_op jit(solution)/shard_map/ppermute | solution.py:704
  34.4 15.9 %collective-permute-start.17 = (bf16[2,96,1152]{2,1,0:T(8,128)(2,1)S(1)}, bf16[2,96,1152]{2,1,0:T(8,128)(2,1)S(1)}, u32[]{:S(2)}, u32[]{:S(2)}) collective-permute-start(bf16[2,96,1152]{2,1,0:T(8,128)(2,1)S(1)} %collective-permute-done.5.refs_6_), channel_id=1, source_target_pairs={{0,16},{16,0},{1,17},{17,1},{2,18},{18,2},{3,19},{19,3},{4,20},{20... | collective-permute-start | bytes 1327112 | tf_op jit(solution)/shard_map/ppermute | solution.py:700
  34.4 12.3 %collective-permute-start.10 = (bf16[96,1152]{1,0:T(8,128)(2,1)S(1)}, bf16[96,1152]{1,0:T(8,128)(2,1)S(1)}, u32[]{:S(2)}, u32[]{:S(2)}) collective-permute-start(bf16[96,1152]{1,0:T(8,128)(2,1)S(1)} %get-tuple-element.95.refs_3_), channel_id=1, source_target_pairs={{0,3},{1,2},{2,1},{3,0},{4,7},{5,6},{6,5},{7,4},{8,11},{9,10},{10,... | collective-permute-start | bytes 663560 | tf_op jit(solution)/shard_map/ppermute | solution.py:704
  39.4 9.6 %collective-permute-start.7 = (bf16[96,1152]{1,0:T(8,128)(2,1)S(1)}, bf16[96,1152]{1,0:T(8,128)(2,1)S(1)}, u32[]{:S(2)}, u32[]{:S(2)}) collective-permute-start(bf16[96,1152]{1,0:T(8,128)(2,1)S(1)} %get-tuple-element.95.refs_3_), channel_id=1, source_target_pairs={{0,2},{1,3},{2,0},{3,1},{4,6},{5,7},{6,4},{7,5},{8,10},{9,11},{10,... | collective-permute-start | bytes 663560 | tf_op jit(solution)/shard_map/ppermute | solution.py:704
  41.2 8.6 %collective-permute-start.6 = (bf16[96,1152]{1,0:T(8,128)(2,1)S(1)}, bf16[96,1152]{1,0:T(8,128)(2,1)S(1)}, u32[]{:S(2)}, u32[]{:S(2)}) collective-permute-start(bf16[96,1152]{1,0:T(8,128)(2,1)S(1)} %get-tuple-element.95.refs_3_), channel_id=1, source_target_pairs={{0,1},{1,0},{2,3},{3,2},{4,5},{5,4},{6,7},{7,6},{8,9},{9,8},{10,11... | collective-permute-start | bytes 663560 | tf_op jit(solution)/shard_map/ppermute | solution.py:704
  69.8 15.0 %collective-permute-start.23 = (bf16[2,4,48,1280]{3,2,1,0:T(8,128)(2,1)S(1)}, bf16[2,4,48,1280]{3,2,1,0:T(8,128)(2,1)S(1)}, u32[]{:S(2)}, u32[]{:S(2)}) collective-permute-start(bf16[2,4,48,1280]{3,2,1,0:T(8,128)(2,1)S(1)} %get-tuple-element.116), channel_id=1, source_target_pairs={{0,16},{16,0},{1,17},{17,1},{2,18},{18,2},{3,19},{19,3},{4,20},{20... | collective-permute-start | bytes 2949128 | tf_op jit(solution)/shard_map/ppermute | solution.py:700
  72.4 13.4 %collective-permute-start.24 = (bf16[4,48,1280]{2,1,0:T(8,128)(2,1)S(1)}, bf16[4,48,1280]{2,1,0:T(8,128)(2,1)S(1)}, u32[]{:S(2)}, u32[]{:S(2)}) collective-permute-start(bf16[4,48,1280]{2,1,0:T(8,128)(2,1)S(1)} %get-tuple-element.101), channel_id=1, source_target_pairs={{0,1},{1,0},{2,3},{3,2},{4,5},{5,4},{6,7},{7,6},{8,9},{9,8},{10,11... | collective-permute-start | bytes 1474568 | tf_op jit(solution)/shard_map/ppermute | solution.py:704
  74.0 13.2 %collective-permute-start.25 = (bf16[4,48,1280]{2,1,0:T(8,128)(2,1)S(1)}, bf16[4,48,1280]{2,1,0:T(8,128)(2,1)S(1)}, u32[]{:S(2)}, u32[]{:S(2)}) collective-permute-start(bf16[4,48,1280]{2,1,0:T(8,128)(2,1)S(1)} %get-tuple-element.102), channel_id=1, source_target_pairs={{0,2},{1,3},{2,0},{3,1},{4,6},{5,7},{6,4},{7,5},{8,10},{9,11},{10,... | collective-permute-start | bytes 1474568 | tf_op jit(solution)/shard_map/ppermute | solution.py:704
  88.5 29.2 %all-to-all-start.1 = ((bf16[4,2,48,1280]{3,2,1,0:T(8,128)(2,1)}), bf16[4,2,48,1280]{3,2,1,0:T(8,128)(2,1)S(1)}, u32[]{:S(2)}, u32[]{:S(2)}) async-start(bf16[4,2,48,1280]{3,2,1,0:T(8,128)(2,1)} %sum_of_plane.2), calls=%async_computation.1 | async-start | bytes 1966080 | tf_op jit(solution)/shard_map/all_to_all | solution.py:886
  94.1 13.7 %collective-permute-start.27 = (bf16[2,2,48,1280]{3,2,1,0:T(8,128)(2,1)S(1)}, bf16[2,2,48,1280]{3,2,1,0:T(8,128)(2,1)S(1)}, u32[]{:S(2)}, u32[]{:S(2)}) collective-permute-start(bf16[2,2,48,1280]{3,2,1,0:T(8,128)(2,1)S(1)} %get-tuple-element.123), channel_id=1, source_target_pairs={{0,1},{1,0},{2,3},{3,2},{4,5},{5,4},{6,7},{7,6},{8,9},{9,8},{10,11... | collective-permute-start | bytes 1474568 | tf_op jit(solution)/shard_map/ppermute | solution.py:704
  95.1 13.1 %collective-permute-start.28 = (bf16[2,2,48,1280]{3,2,1,0:T(8,128)(2,1)S(1)}, bf16[2,2,48,1280]{3,2,1,0:T(8,128)(2,1)S(1)}, u32[]{:S(2)}, u32[]{:S(2)}) collective-permute-start(bf16[2,2,48,1280]{3,2,1,0:T(8,128)(2,1)S(1)} %get-tuple-element.124), channel_id=1, source_target_pairs={{0,2},{1,3},{2,0},{3,1},{4,6},{5,7},{6,4},{7,5},{8,10},{9,11},{10,... | collective-permute-start | bytes 1474568 | tf_op jit(solution)/shard_map/ppermute | solution.py:704
  108.2 7.3 %collective-permute-start.32 = (bf16[2,48,1280]{2,1,0:T(8,128)(2,1)S(1)}, bf16[2,48,1280]{2,1,0:T(8,128)(2,1)S(1)}, u32[]{:S(2)}, u32[]{:S(2)}) collective-permute-start(bf16[2,48,1280]{2,1,0:T(8,128)(2,1)S(1)} %relay.3), channel_id=1, source_target_pairs={{0,1},{1,0},{2,3},{3,2},{4,5},{5,4},{6,7},{7,6},{8,9},{9,8},{10,11... | collective-permute-start | bytes 737288 | tf_op jit(solution)/shard_map/ppermute | solution.py:704
  109.7 7.1 %collective-permute-start.31 = (bf16[2,48,1280]{2,1,0:T(8,128)(2,1)S(1)}, bf16[2,48,1280]{2,1,0:T(8,128)(2,1)S(1)}, u32[]{:S(2)}, u32[]{:S(2)}) collective-permute-start(bf16[2,48,1280]{2,1,0:T(8,128)(2,1)S(1)} %relay.2), channel_id=1, source_target_pairs={{0,2},{1,3},{2,0},{3,1},{4,6},{5,7},{6,4},{7,5},{8,10},{9,11},{10,... | collective-permute-start | bytes 737288 | tf_op jit(solution)/shard_map/ppermute | solution.py:704
  117.8 17.5 %all-to-all-start = ((bf16[4,48,1280]{2,1,0:T(8,128)(2,1)}), bf16[4,48,1280]{2,1,0:T(8,128)(2,1)S(1)}, u32[]{:S(2)}, u32[]{:S(2)}) async-start(bf16[4,48,1280]{2,1,0:T(8,128)(2,1)} %sum_of_plane.3), calls=%async_computation | async-start | bytes 983040 | tf_op jit(solution)/shard_map/all_to_all | solution.py:896
  122.3 9.8 %collective-permute-start.35 = (bf16[2,48,1280]{2,1,0:T(8,128)(2,1)S(1)}, bf16[2,48,1280]{2,1,0:T(8,128)(2,1)S(1)}, u32[]{:S(2)}, u32[]{:S(2)}) collective-permute-start(bf16[2,48,1280]{2,1,0:T(8,128)(2,1)S(1)} %sum_of_column.2.refs_0_), channel_id=1, source_target_pairs={{0,3},{1,2},{2,1},{3,0},{4,7},{5,6},{6,5},{7,4},{8,11},{9,10},{10,... | collective-permute-start | bytes 737288 | tf_op jit(solution)/shard_map/ppermute | solution.py:704
  124.2 10.5 %collective-permute-start.34 = (bf16[2,48,1280]{2,1,0:T(8,128)(2,1)S(1)}, bf16[2,48,1280]{2,1,0:T(8,128)(2,1)S(1)}, u32[]{:S(2)}, u32[]{:S(2)}) collective-permute-start(bf16[2,48,1280]{2,1,0:T(8,128)(2,1)S(1)} %sum_of_column.2.refs_0_), channel_id=1, source_target_pairs={{0,2},{1,3},{2,0},{3,1},{4,6},{5,7},{6,4},{7,5},{8,10},{9,11},{10,... | collective-permute-start | bytes 737288 | tf_op jit(solution)/shard_map/ppermute | solution.py:704
  124.4 10.6 %collective-permute-start.33 = (bf16[2,48,1280]{2,1,0:T(8,128)(2,1)S(1)}, bf16[2,48,1280]{2,1,0:T(8,128)(2,1)S(1)}, u32[]{:S(2)}, u32[]{:S(2)}) collective-permute-start(bf16[2,48,1280]{2,1,0:T(8,128)(2,1)S(1)} %sum_of_column.2.refs_0_), channel_id=1, source_target_pairs={{0,1},{1,0},{2,3},{3,2},{4,5},{5,4},{6,7},{7,6},{8,9},{9,8},{10,11... | collective-permute-start | bytes 737288 | tf_op jit(solution)/shard_map/ppermute | solution.py:704
  125.9 11.2 %collective-permute-start.43 = (bf16[2,48,1280]{2,1,0:T(8,128)(2,1)S(1)}, bf16[2,48,1280]{2,1,0:T(8,128)(2,1)S(1)}, u32[]{:S(2)}, u32[]{:S(2)}) collective-permute-start(bf16[2,48,1280]{2,1,0:T(8,128)(2,1)S(1)} %sum_of_column.2.refs_0_), channel_id=1, source_target_pairs={{0,16},{16,0},{1,17},{17,1},{2,18},{18,2},{3,19},{19,3},{4,20},{20... | collective-permute-start | bytes 737288 | tf_op jit(solution)/shard_map/ppermute | solution.py:700
  132.1 5.3 %collective-permute-start.46 = (bf16[2,48,1280]{2,1,0:T(8,128)(2,1)S(1)}, bf16[2,48,1280]{2,1,0:T(8,128)(2,1)S(1)}, u32[]{:S(2)}, u32[]{:S(2)}) collective-permute-start(bf16[2,48,1280]{2,1,0:T(8,128)(2,1)S(1)} %collective-permute-done.35.refs_6_), channel_id=1, source_target_pairs={{0,16},{16,0},{1,17},{17,1},{2,18},{18,2},{3,19},{19,3},{4,20},{20... | collective-permute-start | bytes 737288 | tf_op jit(solution)/shard_map/ppermute | solution.py:700
  135.0 9.9 %collective-permute-start.44 = (bf16[2,48,1280]{2,1,0:T(8,128)(2,1)S(1)}, bf16[2,48,1280]{2,1,0:T(8,128)(2,1)S(1)}, u32[]{:S(2)}, u32[]{:S(2)}) collective-permute-start(bf16[2,48,1280]{2,1,0:T(8,128)(2,1)S(1)} %collective-permute-done.33.refs_2_), channel_id=1, source_target_pairs={{0,16},{16,0},{1,17},{17,1},{2,18},{18,2},{3,19},{19,3},{4,20},{20... | collective-permute-start | bytes 737288 | tf_op jit(solution)/shard_map/ppermute | solution.py:700
  135.3 7.2 %collective-permute-start.41 = (bf16[48,1280]{1,0:T(8,128)(2,1)S(1)}, bf16[48,1280]{1,0:T(8,128)(2,1)S(1)}, u32[]{:S(2)}, u32[]{:S(2)}) collective-permute-start(bf16[48,1280]{1,0:T(8,128)(2,1)S(1)} %sum_of_column.3.refs_0_), channel_id=1, source_target_pairs={{0,3},{1,2},{2,1},{3,0},{4,7},{5,6},{6,5},{7,4},{8,11},{9,10},{10,... | collective-permute-start | bytes 368648 | tf_op jit(solution)/shard_map/ppermute | solution.py:704
  137.1 7.4 %collective-permute-start.39 = (bf16[48,1280]{1,0:T(8,128)(2,1)S(1)}, bf16[48,1280]{1,0:T(8,128)(2,1)S(1)}, u32[]{:S(2)}, u32[]{:S(2)}) collective-permute-start(bf16[48,1280]{1,0:T(8,128)(2,1)S(1)} %sum_of_column.3.refs_0_), channel_id=1, source_target_pairs={{0,2},{1,3},{2,0},{3,1},{4,6},{5,7},{6,4},{7,5},{8,10},{9,11},{10,... | collective-permute-start | bytes 368648 | tf_op jit(solution)/shard_map/ppermute | solution.py:704
  137.4 7.1 %collective-permute-start.37 = (bf16[48,1280]{1,0:T(8,128)(2,1)S(1)}, bf16[48,1280]{1,0:T(8,128)(2,1)S(1)}, u32[]{:S(2)}, u32[]{:S(2)}) collective-permute-start(bf16[48,1280]{1,0:T(8,128)(2,1)S(1)} %sum_of_column.3.refs_0_), channel_id=1, source_target_pairs={{0,1},{1,0},{2,3},{3,2},{4,5},{5,4},{6,7},{7,6},{8,9},{9,8},{10,11... | collective-permute-start | bytes 368648 | tf_op jit(solution)/shard_map/ppermute | solution.py:704
  138.8 6.3 %collective-permute-start.36 = (bf16[48,1280]{1,0:T(8,128)(2,1)S(1)}, bf16[48,1280]{1,0:T(8,128)(2,1)S(1)}, u32[]{:S(2)}, u32[]{:S(2)}) collective-permute-start(bf16[48,1280]{1,0:T(8,128)(2,1)S(1)} %sum_of_column.3.refs_0_), channel_id=1, source_target_pairs={{0,16},{16,0},{1,17},{17,1},{2,18},{18,2},{3,19},{19,3},{4,20},{20... | collective-permute-start | bytes 368648 | tf_op jit(solution)/shard_map/ppermute | solution.py:700
  (25 other events, 269.4 us)

commit v5 on v4

--- a/solution.py
+++ b/solution.py
@@ -532,7 +532,7 @@
             shape((4, 4, HALF, PIECE), BF16),
         ],
         in_specs=anywhere(1) + vmem(3) + anywhere(6),
-        out_specs=vmem(2) + anywhere(2),
+        out_specs=vmem(4),
         scratch_shapes=[
             pltpu.VMEM((1, 4, ROWS, PACKED), BF16),
             pltpu.VMEM((1, wide, width), BF16),

time: 149 us -> 149 us (level)
  no operation moved by 1% of the time
where the time goes in v5:
time: 149 us
  waiting for transfers between devices  63.7 us (43%)
  starting transfers between devices  45.7 us (31%)
  Pallas kernels  37.6 us (25%)
    ppermute x19, waiting for transfers between devices, flip(): lax.ppermute(value, 'replica', [(place, place ^ bits) for place in range(...  42.6 us
    ppermute x19, starting transfers between devices, flip(): lax.ppermute(value, 'replica', [(place, place ^ bits) for place in range(...  25.5 us
    pallas_call x1, Pallas kernels, run_main(): pl.pallas_call(functools.partial(main_kernel, seq), out_shape=[shape((seq...  17.3 us
    ppermute x4, waiting for transfers between devices, shift(): lax.ppermute(value, 'shard', [(place, (place + steps) % 4) for place in r...  15.6 us
    ppermute x4, starting transfers between devices, shift(): lax.ppermute(value, 'shard', [(place, (place + steps) % 4) for place in r...  8.93 us
    pallas_call x1, Pallas kernels, run_last(): pl.pallas_call(functools.partial(last_kernel, seq), out_shape=[shape((seq...  8.46 us
    ppermute x24, waiting for transfers between devices, swap(): return lax.ppermute(value, 'section', [(0, 1), (1, 0)])  5.44 us
    pallas_call x11, Pallas kernels, small_call(): pl.pallas_call(kernel, out_shape=[shape(dims, BF16) for dims in outs], in...  5.15 us
  transfers between devices with their start and end apart: 49, of which 30 were waited for; matrix products, arithmetic and copies ran while one was open for 0% of the time, Pallas kernels for 10%

profile of v5, /device:TPU:0, one launch (start us, length us, event | category | flops | bytes accessed | tf_op | source)
XLA Modules:
  0.0 148.9 jit_solution(11575060115693827875)
XLA Ops:
  0.7 2.4 %pack.1 = (bf16[96,4736]{1,0:T(8,128)(2,1)}, bf16[96,1280]{1,0:T(8,128)(2,1)}) custom-call(bf16[1,96,1536]{2,1,0:T(8,128)(2,1)} %refs_0_.1, bf16[1,96,1152]{2,1,0:T(8,128)(2,1)} %refs_1_.1, bf16[1,96,384]{2,1,0:T(8,128)(2,1)} %refs_2_.1, bf16[1,384,384]{2,1,0:T(8,128)(2,1)} %refs_3_.2, f32[1,96]{1,0:T(1,128)} %refs_4_.1, f32[1,96]{1,0:T(1,128)} %refs_5_.1, ...), custom_call_target="tpu_custom_call" | custom-call | tf_op jit(solution)/shard_map/pack/pallas_call | solution.py:753
  3.1 5.1 %collective-permute-start.1 = (bf16[96,1280]{1,0:T(8,128)(2,1)}, bf16[96,1280]{1,0:T(8,128)(2,1)S(1)}, u32[]{:S(2)}, u32[]{:S(2)}) collective-permute-start(bf16[96,1280]{1,0:T(8,128)(2,1)} %get-tuple-element.89), channel_id=1, source_target_pairs={{0,12},{4,0},{8,4},{12,8},{1,13},{5,1},{9,5},{13,9},{2,14},{6,2},{... | collective-permute-start | bytes 737288 | tf_op jit(solution)/shard_map/ppermute | solution.py:708
  8.2 6.7 %collective-permute-done.1.third = bf16[96,1280]{1,0:T(8,128)(2,1)S(1)} collective-permute-done((bf16[96,1280]{1,0:T(8,128)(2,1)}, bf16[96,1280]{1,0:T(8,128)(2,1)S(1)}, u32[]{:S(2)}, u32[]{:S(2)}) %collective-permute-start.1) | collective-permute-done | bytes 245792 | tf_op jit(solution)/shard_map/ppermute | solution.py:708
  14.9 4.9 %collective-permute-done.first = bf16[96,1280]{1,0:T(8,128)(2,1)S(1)} collective-permute-done((bf16[96,1280]{1,0:T(8,128)(2,1)}, bf16[96,1280]{1,0:T(8,128)(2,1)S(1)}, u32[]{:S(2)}, u32[]{:S(2)}) %collective-permute-start) | collective-permute-done | bytes 245792 | tf_op jit(solution)/shard_map/ppermute | solution.py:708
  19.9 1.6 %collective-permute-start.5 = (bf16[2,96,1152]{2,1,0:T(8,128)(2,1)S(1)}, bf16[2,96,1152]{2,1,0:T(8,128)(2,1)S(1)}, u32[]{:S(2)}, u32[]{:S(2)}) collective-permute-start(bf16[2,96,1152]{2,1,0:T(8,128)(2,1)S(1)} %get-tuple-element.93.refs_2_), channel_id=1, source_target_pairs={{0,2},{1,3},{2,0},{3,1},{4,6},{5,7},{6,4},{7,5},{8,10},{9,11},{10,... | collective-permute-start | bytes 1327112 | tf_op jit(solution)/shard_map/ppermute | solution.py:704
  21.5 1.5 %collective-permute-start.4 = (bf16[2,96,1152]{2,1,0:T(8,128)(2,1)S(1)}, bf16[2,96,1152]{2,1,0:T(8,128)(2,1)S(1)}, u32[]{:S(2)}, u32[]{:S(2)}) collective-permute-start(bf16[2,96,1152]{2,1,0:T(8,128)(2,1)S(1)} %get-tuple-element.93.refs_2_), channel_id=1, source_target_pairs={{0,1},{1,0},{2,3},{3,2},{4,5},{5,4},{6,7},{7,6},{8,9},{9,8},{10,11... | collective-permute-start | bytes 1327112 | tf_op jit(solution)/shard_map/ppermute | solution.py:704
  23.0 1.6 %collective-permute-start.2 = (bf16[48,1280]{1,0:T(8,128)(2,1)S(1)}, bf16[48,1280]{1,0:T(8,128)(2,1)S(1)}, u32[]{:S(2)}, u32[]{:S(2)}) collective-permute-start(bf16[48,1280]{1,0:T(8,128)(2,1)S(1)} %get-tuple-element.90), channel_id=1, source_target_pairs={{0,4},{4,8},{8,12},{12,0},{1,5},{5,9},{9,13},{13,1},{2,6},{6,10},{... | collective-permute-start | bytes 368648 | tf_op jit(solution)/shard_map/ppermute | solution.py:708
  24.6 2.2 %collective-permute-start.3 = (bf16[48,1280]{1,0:T(8,128)(2,1)S(1)}, bf16[48,1280]{1,0:T(8,128)(2,1)S(1)}, u32[]{:S(2)}, u32[]{:S(2)}) collective-permute-start(bf16[48,1280]{1,0:T(8,128)(2,1)S(1)} %get-tuple-element.91), channel_id=1, source_target_pairs={{0,12},{4,0},{8,4},{12,8},{1,13},{5,1},{9,5},{13,9},{2,14},{6,2},{... | collective-permute-start | bytes 368648 | tf_op jit(solution)/shard_map/ppermute | solution.py:708
  26.8 3.1 %collective-permute-done.2.upper = bf16[48,1280]{1,0:T(8,128)(2,1)S(1)} collective-permute-done((bf16[48,1280]{1,0:T(8,128)(2,1)S(1)}, bf16[48,1280]{1,0:T(8,128)(2,1)S(1)}, u32[]{:S(2)}, u32[]{:S(2)}) %collective-permute-start.2) | collective-permute-done | bytes 122912 | tf_op jit(solution)/shard_map/ppermute | solution.py:708
  32.9 1.6 %collective-permute-start.8 = (bf16[96,1152]{1,0:T(8,128)(2,1)S(1)}, bf16[96,1152]{1,0:T(8,128)(2,1)S(1)}, u32[]{:S(2)}, u32[]{:S(2)}) collective-permute-start(bf16[96,1152]{1,0:T(8,128)(2,1)S(1)} %slice_bitcast_fusion.1), channel_id=1, source_target_pairs={{0,1},{1,0},{2,3},{3,2},{4,5},{5,4},{6,7},{7,6},{8,9},{9,8},{10,11... | collective-permute-start | bytes 663560 | tf_op jit(solution)/shard_map/ppermute | solution.py:704
  34.4 1.6 %collective-permute-start.10 = (bf16[96,1152]{1,0:T(8,128)(2,1)S(1)}, bf16[96,1152]{1,0:T(8,128)(2,1)S(1)}, u32[]{:S(2)}, u32[]{:S(2)}) collective-permute-start(bf16[96,1152]{1,0:T(8,128)(2,1)S(1)} %get-tuple-element.95.refs_3_), channel_id=1, source_target_pairs={{0,3},{1,2},{2,1},{3,0},{4,7},{5,6},{6,5},{7,4},{8,11},{9,10},{10,... | collective-permute-start | bytes 663560 | tf_op jit(solution)/shard_map/ppermute | solution.py:704
  36.0 3.4 %collective-permute-done.9.refs_9_ = bf16[96,1152]{1,0:T(8,128)(2,1)S(1)} collective-permute-done((bf16[96,1152]{1,0:T(8,128)(2,1)S(1)}, bf16[96,1152]{1,0:T(8,128)(2,1)S(1)}, u32[]{:S(2)}, u32[]{:S(2)}) %collective-permute-start.9) | collective-permute-done | bytes 221216 | tf_op jit(solution)/shard_map/ppermute | solution.py:704
  42.7 4.0 %collective-permute-done.10.refs_10_ = bf16[96,1152]{1,0:T(8,128)(2,1)S(1)} collective-permute-done((bf16[96,1152]{1,0:T(8,128)(2,1)S(1)}, bf16[96,1152]{1,0:T(8,128)(2,1)S(1)}, u32[]{:S(2)}, u32[]{:S(2)}) %collective-permute-start.10) | collective-permute-done | bytes 221216 | tf_op jit(solution)/shard_map/ppermute | solution.py:704
  46.7 2.3 %collective-permute-done.7.refs_7_ = bf16[96,1152]{1,0:T(8,128)(2,1)S(1)} collective-permute-done((bf16[96,1152]{1,0:T(8,128)(2,1)S(1)}, bf16[96,1152]{1,0:T(8,128)(2,1)S(1)}, u32[]{:S(2)}, u32[]{:S(2)}) %collective-permute-start.7) | collective-permute-done | bytes 221216 | tf_op jit(solution)/shard_map/ppermute | solution.py:704
  52.2 17.3 %forward_and_layer_one.1 = (bf16[197,384]{1,0:T(8,128)(2,1)S(1)}, bf16[197,384]{1,0:T(8,128)(2,1)S(1)}, bf16[197,384]{1,0:T(8,128)(2,1)S(1)}, bf16[4,4,48,1280]{...) custom-call(bf16[96,4736]{1,0:T(8,128)(2,1)S(1)} %copy-done, ...), custom_call_target="tpu_custom_call" | custom-call | tf_op jit(solution)/shard_map/forward_and_layer_one/pallas_call | solution.py:490
  70.1 2.1 %collective-permute-done.22.recv = bf16[2,4,48,1280]{3,2,1,0:T(8,128)(2,1)S(1)} collective-permute-done((bf16[2,4,48,1280]{3,2,1,0:T(8,128)(2,1)S(1)}, bf16[2,4,48,1280]{3,2,1,0:T(8,128)(2,1)S(1)}, u32[]{:S(2)}, u32[]{:S(2)}) %collective-permute-start.22) | collective-permute-done | bytes 983072 | tf_op jit(solution)/shard_map/ppermute | solution.py:700
  72.4 1.6 %collective-permute-start.24 = (bf16[4,48,1280]{2,1,0:T(8,128)(2,1)S(1)}, bf16[4,48,1280]{2,1,0:T(8,128)(2,1)S(1)}, u32[]{:S(2)}, u32[]{:S(2)}) collective-permute-start(bf16[4,48,1280]{2,1,0:T(8,128)(2,1)S(1)} %get-tuple-element.101), channel_id=1, source_target_pairs={{0,1},{1,0},{2,3},{3,2},{4,5},{5,4},{6,7},{7,6},{8,9},{9,8},{10,11... | collective-permute-start | bytes 1474568 | tf_op jit(solution)/shard_map/ppermute | solution.py:704
  74.0 2.0 %collective-permute-start.25 = (bf16[4,48,1280]{2,1,0:T(8,128)(2,1)S(1)}, bf16[4,48,1280]{2,1,0:T(8,128)(2,1)S(1)}, u32[]{:S(2)}, u32[]{:S(2)}) collective-permute-start(bf16[4,48,1280]{2,1,0:T(8,128)(2,1)S(1)} %get-tuple-element.102), channel_id=1, source_target_pairs={{0,2},{1,3},{2,0},{3,1},{4,6},{5,7},{6,4},{7,5},{8,10},{9,11},{10,... | collective-permute-start | bytes 1474568 | tf_op jit(solution)/shard_map/ppermute | solution.py:704
  75.9 8.5 %layer_zero_backward.1 = (f32[197,384]{1,0:T(8,128)S(1)}, f32[197,384]{1,0:T(8,128)S(1)}, bf16[4,4,48,1280]{3,2,1,0:T(8,128)(2,1)S(1)}, bf16[4,4,48,1280]{3,2,1,0:T(8,128)(2,1)}) custom-call(bf16[1,4,96,4736]{3,2,1,0:T(8,128)(2,1)S(1)} %get-tuple-element.103.refs_0_, f32[8,384]{1,0:T(8,128)S(1)} %get-tuple-element.104.refs_1_, ...), custom_call_target="tpu_custom_call" | custom-call | flops 8000000000 | bytes 8000000 | tf_op jit(solution)/shard_map/layer_zero_backward/pallas_call | solution.py:526
  88.5 3.5 %all-to-all-start.1 = ((bf16[4,2,48,1280]{3,2,1,0:T(8,128)(2,1)}), bf16[4,2,48,1280]{3,2,1,0:T(8,128)(2,1)S(1)}, u32[]{:S(2)}, u32[]{:S(2)}) async-start(bf16[4,2,48,1280]{3,2,1,0:T(8,128)(2,1)} %sum_of_plane.2), calls=%async_computation.1 | async-start | bytes 1966080 | tf_op jit(solution)/shard_map/all_to_all | solution.py:886
  92.1 2.0 %sum_of_cores.3 = (bf16[2,2,48,1280]{3,2,1,0:T(8,128)(2,1)S(1)}, bf16[2,2,48,1280]{3,2,1,0:T(8,128)(2,1)S(1)}, bf16[4,48,1280]{2,1,0:T(8,128)(2,1)S(1)}, bf16[2,...) custom-call(bf16[4,4,48,1280]{3,2,1,0:T(8,128)(2,1)S(1)} %get-tuple-element.121.keep, ...), custom_call_target="tpu_custom_call" | custom-call | tf_op jit(solution)/shard_map/sum_of_cores/pallas_call | solution.py:559
  99.7 8.1 %collective-permute-done.27.got.got_x = bf16[2,2,48,1280]{3,2,1,0:T(8,128)(2,1)S(1)} collective-permute-done((bf16[2,2,48,1280]{3,2,1,0:T(8,128)(2,1)S(1)}, bf16[2,2,48,1280]{3,2,1,0:T(8,128)(2,1)S(1)}, u32[]{:S(2)}, u32[]{:S(2)}) %collective-permute-start.27) | collective-permute-done | bytes 491552 | tf_op jit(solution)/shard_map/ppermute | solution.py:704
  109.7 1.8 %collective-permute-start.31 = (bf16[2,48,1280]{2,1,0:T(8,128)(2,1)S(1)}, bf16[2,48,1280]{2,1,0:T(8,128)(2,1)S(1)}, u32[]{:S(2)}, u32[]{:S(2)}) collective-permute-start(bf16[2,48,1280]{2,1,0:T(8,128)(2,1)S(1)} %relay.2), channel_id=1, source_target_pairs={{0,2},{1,3},{2,0},{3,1},{4,6},{5,7},{6,4},{7,5},{8,10},{9,11},{10,... | collective-permute-start | bytes 737288 | tf_op jit(solution)/shard_map/ppermute | solution.py:704
  111.5 4.0 %collective-permute-done.32.late_x = bf16[2,48,1280]{2,1,0:T(8,128)(2,1)S(1)} collective-permute-done((bf16[2,48,1280]{2,1,0:T(8,128)(2,1)S(1)}, bf16[2,48,1280]{2,1,0:T(8,128)(2,1)S(1)}, u32[]{:S(2)}, u32[]{:S(2)}) %collective-permute-start.32) | collective-permute-done | bytes 245792 | tf_op jit(solution)/shard_map/ppermute | solution.py:704
  117.8 4.4 %all-to-all-start = ((bf16[4,48,1280]{2,1,0:T(8,128)(2,1)}), bf16[4,48,1280]{2,1,0:T(8,128)(2,1)S(1)}, u32[]{:S(2)}, u32[]{:S(2)}) async-start(bf16[4,48,1280]{2,1,0:T(8,128)(2,1)} %sum_of_plane.3), calls=%async_computation | async-start | bytes 983040 | tf_op jit(solution)/shard_map/all_to_all | solution.py:896
  122.3 1.8 %collective-permute-start.35 = (bf16[2,48,1280]{2,1,0:T(8,128)(2,1)S(1)}, bf16[2,48,1280]{2,1,0:T(8,128)(2,1)S(1)}, u32[]{:S(2)}, u32[]{:S(2)}) collective-permute-start(bf16[2,48,1280]{2,1,0:T(8,128)(2,1)S(1)} %sum_of_column.2.refs_0_), channel_id=1, source_target_pairs={{0,3},{1,2},{2,1},{3,0},{4,7},{5,6},{6,5},{7,4},{8,11},{9,10},{10,... | collective-permute-start | bytes 737288 | tf_op jit(solution)/shard_map/ppermute | solution.py:704
  125.9 6.2 %collective-permute-done.35.refs_6_ = bf16[2,48,1280]{2,1,0:T(8,128)(2,1)S(1)} collective-permute-done((bf16[2,48,1280]{2,1,0:T(8,128)(2,1)S(1)}, bf16[2,48,1280]{2,1,0:T(8,128)(2,1)S(1)}, u32[]{:S(2)}, u32[]{:S(2)}) %collective-permute-start.35) | collective-permute-done | bytes 245792 | tf_op jit(solution)/shard_map/ppermute | solution.py:704
  132.1 2.6 %collective-permute-done.34.refs_4_ = bf16[2,48,1280]{2,1,0:T(8,128)(2,1)S(1)} collective-permute-done((bf16[2,48,1280]{2,1,0:T(8,128)(2,1)S(1)}, bf16[2,48,1280]{2,1,0:T(8,128)(2,1)S(1)}, u32[]{:S(2)}, u32[]{:S(2)}) %collective-permute-start.34) | collective-permute-done | bytes 245792 | tf_op jit(solution)/shard_map/ppermute | solution.py:704
  135.3 1.8 %collective-permute-start.41 = (bf16[48,1280]{1,0:T(8,128)(2,1)S(1)}, bf16[48,1280]{1,0:T(8,128)(2,1)S(1)}, u32[]{:S(2)}, u32[]{:S(2)}) collective-permute-start(bf16[48,1280]{1,0:T(8,128)(2,1)S(1)} %sum_of_column.3.refs_0_), channel_id=1, source_target_pairs={{0,3},{1,2},{2,1},{3,0},{4,7},{5,6},{6,5},{7,4},{8,11},{9,10},{10,... | collective-permute-start | bytes 368648 | tf_op jit(solution)/shard_map/ppermute | solution.py:704
  138.8 3.6 %collective-permute-done.41.refs_6_ = bf16[48,1280]{1,0:T(8,128)(2,1)S(1)} collective-permute-done((bf16[48,1280]{1,0:T(8,128)(2,1)S(1)}, bf16[48,1280]{1,0:T(8,128)(2,1)S(1)}, u32[]{:S(2)}, u32[]{:S(2)}) %collective-permute-start.41) | collective-permute-done | bytes 122912 | tf_op jit(solution)/shard_map/ppermute | solution.py:704
  142.4 2.0 %collective-permute-done.39.refs_4_ = bf16[48,1280]{1,0:T(8,128)(2,1)S(1)} collective-permute-done((bf16[48,1280]{1,0:T(8,128)(2,1)S(1)}, bf16[48,1280]{1,0:T(8,128)(2,1)S(1)}, u32[]{:S(2)}, u32[]{:S(2)}) %collective-permute-start.39) | collective-permute-done | bytes 122912 | tf_op jit(solution)/shard_map/ppermute | solution.py:704
  145.9 2.8 %unpack.1 = (f32[1,96,1152]{2,1,0:T(8,128)}, f32[1,96,384]{2,1,0:T(8,128)}, f32[1,96,1536]{2,1,0:T(8,128)}, f32[1,384,384]{2,1,0:T(8,128)}, f32[1,96]{1,0:T(1,12...) custom-call(bf16[48,1280]{1,0:T(8,128)(2,1)S(1)} %sum_of_column.3.re, ...), custom_call_target="tpu_custom_call" | custom-call | tf_op jit(solution)/shard_map/unpack/pallas_call | solution.py:678
  (102 shorter events, 29.8 us)
Async XLA Ops:
  3.1 11.8 %collective-permute-start.1 = (bf16[96,1280]{1,0:T(8,128)(2,1)}, bf16[96,1280]{1,0:T(8,128)(2,1)S(1)}, u32[]{:S(2)}, u32[]{:S(2)}) collective-permute-start(bf16[96,1280]{1,0:T(8,128)(2,1)} %get-tuple-element.89), channel_id=1, source_target_pairs={{0,12},{4,0},{8,4},{12,8},{1,13},{5,1},{9,5},{13,9},{2,14},{6,2},{... | collective-permute-start | bytes 737288 | tf_op jit(solution)/shard_map/ppermute | solution.py:708
  8.2 11.6 %collective-permute-start = (bf16[96,1280]{1,0:T(8,128)(2,1)}, bf16[96,1280]{1,0:T(8,128)(2,1)S(1)}, u32[]{:S(2)}, u32[]{:S(2)}) collective-permute-start(bf16[96,1280]{1,0:T(8,128)(2,1)} %get-tuple-element.89), channel_id=1, source_target_pairs={{0,4},{4,8},{8,12},{12,0},{1,5},{5,9},{9,13},{13,1},{2,6},{6,10},{... | collective-permute-start | bytes 737288 | tf_op jit(solution)/shard_map/ppermute | solution.py:708
  19.9 11.1 %collective-permute-start.5 = (bf16[2,96,1152]{2,1,0:T(8,128)(2,1)S(1)}, bf16[2,96,1152]{2,1,0:T(8,128)(2,1)S(1)}, u32[]{:S(2)}, u32[]{:S(2)}) collective-permute-start(bf16[2,96,1152]{2,1,0:T(8,128)(2,1)S(1)} %get-tuple-element.93.refs_2_), channel_id=1, source_target_pairs={{0,2},{1,3},{2,0},{3,1},{4,6},{5,7},{6,4},{7,5},{8,10},{9,11},{10,... | collective-permute-start | bytes 1327112 | tf_op jit(solution)/shard_map/ppermute | solution.py:704
  21.5 10.8 %collective-permute-start.4 = (bf16[2,96,1152]{2,1,0:T(8,128)(2,1)S(1)}, bf16[2,96,1152]{2,1,0:T(8,128)(2,1)S(1)}, u32[]{:S(2)}, u32[]{:S(2)}) collective-permute-start(bf16[2,96,1152]{2,1,0:T(8,128)(2,1)S(1)} %get-tuple-element.93.refs_2_), channel_id=1, source_target_pairs={{0,1},{1,0},{2,3},{3,2},{4,5},{5,4},{6,7},{7,6},{8,9},{9,8},{10,11... | collective-permute-start | bytes 1327112 | tf_op jit(solution)/shard_map/ppermute | solution.py:704
  23.0 6.9 %collective-permute-start.2 = (bf16[48,1280]{1,0:T(8,128)(2,1)S(1)}, bf16[48,1280]{1,0:T(8,128)(2,1)S(1)}, u32[]{:S(2)}, u32[]{:S(2)}) collective-permute-start(bf16[48,1280]{1,0:T(8,128)(2,1)S(1)} %get-tuple-element.90), channel_id=1, source_target_pairs={{0,4},{4,8},{8,12},{12,0},{1,5},{5,9},{9,13},{13,1},{2,6},{6,10},{... | collective-permute-start | bytes 368648 | tf_op jit(solution)/shard_map/ppermute | solution.py:708
  24.6 6.2 %collective-permute-start.3 = (bf16[48,1280]{1,0:T(8,128)(2,1)S(1)}, bf16[48,1280]{1,0:T(8,128)(2,1)S(1)}, u32[]{:S(2)}, u32[]{:S(2)}) collective-permute-start(bf16[48,1280]{1,0:T(8,128)(2,1)S(1)} %get-tuple-element.91), channel_id=1, source_target_pairs={{0,12},{4,0},{8,4},{12,8},{1,13},{5,1},{9,5},{13,9},{2,14},{6,2},{... | collective-permute-start | bytes 368648 | tf_op jit(solution)/shard_map/ppermute | solution.py:708
  26.8 23.0 %collective-permute-start.11 = (bf16[96,4736]{1,0:T(8,128)(2,1)}, bf16[96,4736]{1,0:T(8,128)(2,1)S(1)}, u32[]{:S(2)}, u32[]{:S(2)}) collective-permute-start(bf16[96,4736]{1,0:T(8,128)(2,1)} %get-tuple-element.88.refs_0_), channel_id=1, source_target_pairs={{0,16},{16,0},{1,17},{17,1},{2,18},{18,2},{3,19},{19,3},{4,20},{20... | collective-permute-start | bytes 2727944 | tf_op jit(solution)/shard_map/ppermute | solution.py:700
  32.3 7.2 %collective-permute-start.9 = (bf16[96,1152]{1,0:T(8,128)(2,1)S(1)}, bf16[96,1152]{1,0:T(8,128)(2,1)S(1)}, u32[]{:S(2)}, u32[]{:S(2)}) collective-permute-start(bf16[96,1152]{1,0:T(8,128)(2,1)S(1)} %slice_bitcast_fusion), channel_id=1, source_target_pairs={{0,2},{1,3},{2,0},{3,1},{4,6},{5,7},{6,4},{7,5},{8,10},{9,11},{10,... | collective-permute-start | bytes 663560 | tf_op jit(solution)/shard_map/ppermute | solution.py:704
  32.9 8.4 %collective-permute-start.8 = (bf16[96,1152]{1,0:T(8,128)(2,1)S(1)}, bf16[96,1152]{1,0:T(8,128)(2,1)S(1)}, u32[]{:S(2)}, u32[]{:S(2)}) collective-permute-start(bf16[96,1152]{1,0:T(8,128)(2,1)S(1)} %slice_bitcast_fusion.1), channel_id=1, source_target_pairs={{0,1},{1,0},{2,3},{3,2},{4,5},{5,4},{6,7},{7,6},{8,9},{9,8},{10,11... | collective-permute-start | bytes 663560 | tf_op jit(solution)/shard_map/ppermute | solution.py:704
  34.4 15.9 %collective-permute-start.17 = (bf16[2,96,1152]{2,1,0:T(8,128)(2,1)S(1)}, bf16[2,96,1152]{2,1,0:T(8,128)(2,1)S(1)}, u32[]{:S(2)}, u32[]{:S(2)}) collective-permute-start(bf16[2,96,1152]{2,1,0:T(8,128)(2,1)S(1)} %collective-permute-done.5.refs_6_), channel_id=1, source_target_pairs={{0,16},{16,0},{1,17},{17,1},{2,18},{18,2},{3,19},{19,3},{4,20},{20... | collective-permute-start | bytes 1327112 | tf_op jit(solution)/shard_map/ppermute | solution.py:700
  34.4 12.3 %collective-permute-start.10 = (bf16[96,1152]{1,0:T(8,128)(2,1)S(1)}, bf16[96,1152]{1,0:T(8,128)(2,1)S(1)}, u32[]{:S(2)}, u32[]{:S(2)}) collective-permute-start(bf16[96,1152]{1,0:T(8,128)(2,1)S(1)} %get-tuple-element.95.refs_3_), channel_id=1, source_target_pairs={{0,3},{1,2},{2,1},{3,0},{4,7},{5,6},{6,5},{7,4},{8,11},{9,10},{10,... | collective-permute-start | bytes 663560 | tf_op jit(solution)/shard_map/ppermute | solution.py:704
  39.4 9.6 %collective-permute-start.7 = (bf16[96,1152]{1,0:T(8,128)(2,1)S(1)}, bf16[96,1152]{1,0:T(8,128)(2,1)S(1)}, u32[]{:S(2)}, u32[]{:S(2)}) collective-permute-start(bf16[96,1152]{1,0:T(8,128)(2,1)S(1)} %get-tuple-element.95.refs_3_), channel_id=1, source_target_pairs={{0,2},{1,3},{2,0},{3,1},{4,6},{5,7},{6,4},{7,5},{8,10},{9,11},{10,... | collective-permute-start | bytes 663560 | tf_op jit(solution)/shard_map/ppermute | solution.py:704
  41.2 8.6 %collective-permute-start.6 = (bf16[96,1152]{1,0:T(8,128)(2,1)S(1)}, bf16[96,1152]{1,0:T(8,128)(2,1)S(1)}, u32[]{:S(2)}, u32[]{:S(2)}) collective-permute-start(bf16[96,1152]{1,0:T(8,128)(2,1)S(1)} %get-tuple-element.95.refs_3_), channel_id=1, source_target_pairs={{0,1},{1,0},{2,3},{3,2},{4,5},{5,4},{6,7},{7,6},{8,9},{9,8},{10,11... | collective-permute-start | bytes 663560 | tf_op jit(solution)/shard_map/ppermute | solution.py:704
  69.8 15.3 %collective-permute-start.23 = (bf16[2,4,48,1280]{3,2,1,0:T(8,128)(2,1)S(1)}, bf16[2,4,48,1280]{3,2,1,0:T(8,128)(2,1)S(1)}, u32[]{:S(2)}, u32[]{:S(2)}) collective-permute-start(bf16[2,4,48,1280]{3,2,1,0:T(8,128)(2,1)S(1)} %get-tuple-element.116), channel_id=1, source_target_pairs={{0,16},{16,0},{1,17},{17,1},{2,18},{18,2},{3,19},{19,3},{4,20},{20... | collective-permute-start | bytes 2949128 | tf_op jit(solution)/shard_map/ppermute | solution.py:700
  72.4 13.4 %collective-permute-start.24 = (bf16[4,48,1280]{2,1,0:T(8,128)(2,1)S(1)}, bf16[4,48,1280]{2,1,0:T(8,128)(2,1)S(1)}, u32[]{:S(2)}, u32[]{:S(2)}) collective-permute-start(bf16[4,48,1280]{2,1,0:T(8,128)(2,1)S(1)} %get-tuple-element.101), channel_id=1, source_target_pairs={{0,1},{1,0},{2,3},{3,2},{4,5},{5,4},{6,7},{7,6},{8,9},{9,8},{10,11... | collective-permute-start | bytes 1474568 | tf_op jit(solution)/shard_map/ppermute | solution.py:704
  74.0 13.2 %collective-permute-start.25 = (bf16[4,48,1280]{2,1,0:T(8,128)(2,1)S(1)}, bf16[4,48,1280]{2,1,0:T(8,128)(2,1)S(1)}, u32[]{:S(2)}, u32[]{:S(2)}) collective-permute-start(bf16[4,48,1280]{2,1,0:T(8,128)(2,1)S(1)} %get-tuple-element.102), channel_id=1, source_target_pairs={{0,2},{1,3},{2,0},{3,1},{4,6},{5,7},{6,4},{7,5},{8,10},{9,11},{10,... | collective-permute-start | bytes 1474568 | tf_op jit(solution)/shard_map/ppermute | solution.py:704
  88.5 29.2 %all-to-all-start.1 = ((bf16[4,2,48,1280]{3,2,1,0:T(8,128)(2,1)}), bf16[4,2,48,1280]{3,2,1,0:T(8,128)(2,1)S(1)}, u32[]{:S(2)}, u32[]{:S(2)}) async-start(bf16[4,2,48,1280]{3,2,1,0:T(8,128)(2,1)} %sum_of_plane.2), calls=%async_computation.1 | async-start | bytes 1966080 | tf_op jit(solution)/shard_map/all_to_all | solution.py:886
  94.1 13.7 %collective-permute-start.27 = (bf16[2,2,48,1280]{3,2,1,0:T(8,128)(2,1)S(1)}, bf16[2,2,48,1280]{3,2,1,0:T(8,128)(2,1)S(1)}, u32[]{:S(2)}, u32[]{:S(2)}) collective-permute-start(bf16[2,2,48,1280]{3,2,1,0:T(8,128)(2,1)S(1)} %get-tuple-element.123), channel_id=1, source_target_pairs={{0,1},{1,0},{2,3},{3,2},{4,5},{5,4},{6,7},{7,6},{8,9},{9,8},{10,11... | collective-permute-start | bytes 1474568 | tf_op jit(solution)/shard_map/ppermute | solution.py:704
  95.1 13.1 %collective-permute-start.28 = (bf16[2,2,48,1280]{3,2,1,0:T(8,128)(2,1)S(1)}, bf16[2,2,48,1280]{3,2,1,0:T(8,128)(2,1)S(1)}, u32[]{:S(2)}, u32[]{:S(2)}) collective-permute-start(bf16[2,2,48,1280]{3,2,1,0:T(8,128)(2,1)S(1)} %get-tuple-element.124), channel_id=1, source_target_pairs={{0,2},{1,3},{2,0},{3,1},{4,6},{5,7},{6,4},{7,5},{8,10},{9,11},{10,... | collective-permute-start | bytes 1474568 | tf_op jit(solution)/shard_map/ppermute | solution.py:704
  108.2 7.3 %collective-permute-start.32 = (bf16[2,48,1280]{2,1,0:T(8,128)(2,1)S(1)}, bf16[2,48,1280]{2,1,0:T(8,128)(2,1)S(1)}, u32[]{:S(2)}, u32[]{:S(2)}) collective-permute-start(bf16[2,48,1280]{2,1,0:T(8,128)(2,1)S(1)} %relay.3), channel_id=1, source_target_pairs={{0,1},{1,0},{2,3},{3,2},{4,5},{5,4},{6,7},{7,6},{8,9},{9,8},{10,11... | collective-permute-start | bytes 737288 | tf_op jit(solution)/shard_map/ppermute | solution.py:704
  109.7 7.1 %collective-permute-start.31 = (bf16[2,48,1280]{2,1,0:T(8,128)(2,1)S(1)}, bf16[2,48,1280]{2,1,0:T(8,128)(2,1)S(1)}, u32[]{:S(2)}, u32[]{:S(2)}) collective-permute-start(bf16[2,48,1280]{2,1,0:T(8,128)(2,1)S(1)} %relay.2), channel_id=1, source_target_pairs={{0,2},{1,3},{2,0},{3,1},{4,6},{5,7},{6,4},{7,5},{8,10},{9,11},{10,... | collective-permute-start | bytes 737288 | tf_op jit(solution)/shard_map/ppermute | solution.py:704
  117.8 17.5 %all-to-all-start = ((bf16[4,48,1280]{2,1,0:T(8,128)(2,1)}), bf16[4,48,1280]{2,1,0:T(8,128)(2,1)S(1)}, u32[]{:S(2)}, u32[]{:S(2)}) async-start(bf16[4,48,1280]{2,1,0:T(8,128)(2,1)} %sum_of_plane.3), calls=%async_computation | async-start | bytes 983040 | tf_op jit(solution)/shard_map/all_to_all | solution.py:896
  122.3 9.8 %collective-permute-start.35 = (bf16[2,48,1280]{2,1,0:T(8,128)(2,1)S(1)}, bf16[2,48,1280]{2,1,0:T(8,128)(2,1)S(1)}, u32[]{:S(2)}, u32[]{:S(2)}) collective-permute-start(bf16[2,48,1280]{2,1,0:T(8,128)(2,1)S(1)} %sum_of_column.2.refs_0_), channel_id=1, source_target_pairs={{0,3},{1,2},{2,1},{3,0},{4,7},{5,6},{6,5},{7,4},{8,11},{9,10},{10,... | collective-permute-start | bytes 737288 | tf_op jit(solution)/shard_map/ppermute | solution.py:704
  124.2 10.5 %collective-permute-start.34 = (bf16[2,48,1280]{2,1,0:T(8,128)(2,1)S(1)}, bf16[2,48,1280]{2,1,0:T(8,128)(2,1)S(1)}, u32[]{:S(2)}, u32[]{:S(2)}) collective-permute-start(bf16[2,48,1280]{2,1,0:T(8,128)(2,1)S(1)} %sum_of_column.2.refs_0_), channel_id=1, source_target_pairs={{0,2},{1,3},{2,0},{3,1},{4,6},{5,7},{6,4},{7,5},{8,10},{9,11},{10,... | collective-permute-start | bytes 737288 | tf_op jit(solution)/shard_map/ppermute | solution.py:704
  124.4 10.6 %collective-permute-start.33 = (bf16[2,48,1280]{2,1,0:T(8,128)(2,1)S(1)}, bf16[2,48,1280]{2,1,0:T(8,128)(2,1)S(1)}, u32[]{:S(2)}, u32[]{:S(2)}) collective-permute-start(bf16[2,48,1280]{2,1,0:T(8,128)(2,1)S(1)} %sum_of_column.2.refs_0_), channel_id=1, source_target_pairs={{0,1},{1,0},{2,3},{3,2},{4,5},{5,4},{6,7},{7,6},{8,9},{9,8},{10,11... | collective-permute-start | bytes 737288 | tf_op jit(solution)/shard_map/ppermute | solution.py:704
  125.9 11.2 %collective-permute-start.43 = (bf16[2,48,1280]{2,1,0:T(8,128)(2,1)S(1)}, bf16[2,48,1280]{2,1,0:T(8,128)(2,1)S(1)}, u32[]{:S(2)}, u32[]{:S(2)}) collective-permute-start(bf16[2,48,1280]{2,1,0:T(8,128)(2,1)S(1)} %sum_of_column.2.refs_0_), channel_id=1, source_target_pairs={{0,16},{16,0},{1,17},{17,1},{2,18},{18,2},{3,19},{19,3},{4,20},{20... | collective-permute-start | bytes 737288 | tf_op jit(solution)/shard_map/ppermute | solution.py:700
  132.1 5.3 %collective-permute-start.46 = (bf16[2,48,1280]{2,1,0:T(8,128)(2,1)S(1)}, bf16[2,48,1280]{2,1,0:T(8,128)(2,1)S(1)}, u32[]{:S(2)}, u32[]{:S(2)}) collective-permute-start(bf16[2,48,1280]{2,1,0:T(8,128)(2,1)S(1)} %collective-permute-done.35.refs_6_), channel_id=1, source_target_pairs={{0,16},{16,0},{1,17},{17,1},{2,18},{18,2},{3,19},{19,3},{4,20},{20... | collective-permute-start | bytes 737288 | tf_op jit(solution)/shard_map/ppermute | solution.py:700
  135.0 9.9 %collective-permute-start.44 = (bf16[2,48,1280]{2,1,0:T(8,128)(2,1)S(1)}, bf16[2,48,1280]{2,1,0:T(8,128)(2,1)S(1)}, u32[]{:S(2)}, u32[]{:S(2)}) collective-permute-start(bf16[2,48,1280]{2,1,0:T(8,128)(2,1)S(1)} %collective-permute-done.33.refs_2_), channel_id=1, source_target_pairs={{0,16},{16,0},{1,17},{17,1},{2,18},{18,2},{3,19},{19,3},{4,20},{20... | collective-permute-start | bytes 737288 | tf_op jit(solution)/shard_map/ppermute | solution.py:700
  135.3 7.2 %collective-permute-start.41 = (bf16[48,1280]{1,0:T(8,128)(2,1)S(1)}, bf16[48,1280]{1,0:T(8,128)(2,1)S(1)}, u32[]{:S(2)}, u32[]{:S(2)}) collective-permute-start(bf16[48,1280]{1,0:T(8,128)(2,1)S(1)} %sum_of_column.3.refs_0_), channel_id=1, source_target_pairs={{0,3},{1,2},{2,1},{3,0},{4,7},{5,6},{6,5},{7,4},{8,11},{9,10},{10,... | collective-permute-start | bytes 368648 | tf_op jit(solution)/shard_map/ppermute | solution.py:704
  137.1 7.4 %collective-permute-start.39 = (bf16[48,1280]{1,0:T(8,128)(2,1)S(1)}, bf16[48,1280]{1,0:T(8,128)(2,1)S(1)}, u32[]{:S(2)}, u32[]{:S(2)}) collective-permute-start(bf16[48,1280]{1,0:T(8,128)(2,1)S(1)} %sum_of_column.3.refs_0_), channel_id=1, source_target_pairs={{0,2},{1,3},{2,0},{3,1},{4,6},{5,7},{6,4},{7,5},{8,10},{9,11},{10,... | collective-permute-start | bytes 368648 | tf_op jit(solution)/shard_map/ppermute | solution.py:704
  137.4 7.1 %collective-permute-start.37 = (bf16[48,1280]{1,0:T(8,128)(2,1)S(1)}, bf16[48,1280]{1,0:T(8,128)(2,1)S(1)}, u32[]{:S(2)}, u32[]{:S(2)}) collective-permute-start(bf16[48,1280]{1,0:T(8,128)(2,1)S(1)} %sum_of_column.3.refs_0_), channel_id=1, source_target_pairs={{0,1},{1,0},{2,3},{3,2},{4,5},{5,4},{6,7},{7,6},{8,9},{9,8},{10,11... | collective-permute-start | bytes 368648 | tf_op jit(solution)/shard_map/ppermute | solution.py:704
  138.8 6.3 %collective-permute-start.36 = (bf16[48,1280]{1,0:T(8,128)(2,1)S(1)}, bf16[48,1280]{1,0:T(8,128)(2,1)S(1)}, u32[]{:S(2)}, u32[]{:S(2)}) collective-permute-start(bf16[48,1280]{1,0:T(8,128)(2,1)S(1)} %sum_of_column.3.refs_0_), channel_id=1, source_target_pairs={{0,16},{16,0},{1,17},{17,1},{2,18},{18,2},{3,19},{19,3},{4,20},{20... | collective-permute-start | bytes 368648 | tf_op jit(solution)/shard_map/ppermute | solution.py:700
  (25 other events, 269.8 us)
